TPU v7x, 32 devices: a whole 2x2x4 slice. The times are simulated.
32 devices in a mesh: tm: 2 (over x), height: 2 (over y), seq: 8 (over z, core).
Axes of the slice: x: 2, y: 2, z: 4, core: 2. Of those that a mesh axis runs over, the one named last changes fastest.
Arguments:
- queries: bfloat16 [16384, 2048], P(('tm', 'height', 'seq')), may hold values from -170 to 170
- key_states: bfloat16 [16384, 2048], P(('tm', 'height', 'seq')), may hold values from -6.5 to 6.5
- value_states: bfloat16 [16384, 2048], P(('tm', 'height', 'seq')), may hold values from -6 to 6
- out_grad: bfloat16 [16384, 2048], P(('tm', 'height', 'seq')), may hold values from -6 to 6
- tile_valid: int32 [2, 8, 16], replicated, may hold values 0 or 1
- width_shift: int32 [2, 8, 16], replicated, may hold values from -1 to 1, as said below
Outputs:
- query_grad: bfloat16 [16384, 2048], P(('tm', 'height', 'seq'))
- key_grad: bfloat16 [16384, 2048], P(('tm', 'height', 'seq'))
- value_grad: bfloat16 [16384, 2048], P(('tm', 'height', 'seq'))
Inputs may be any that keep to these rules, and one draw needn't show every extreme that they name: `width_shift`: each query tile's window of three column tiles, from l + shift - 1 to l + shift + 1, lies inside the columns 0 to 15.
All inputs are finite; a program needn't handle non-finite values.
Results may differ from a plain program's by a relative error of at most 0.005.
Values may be sent and summed in bfloat16 or wider, within the bound.
No kernel may reach another device: no remote copies, remote signals or barrier semaphores. Data moves between devices by JAX's collectives and lax.ppermute only.
A program may use at most 448 MiB of HBM per device.

v0:
```python
from functools import partial

import jax
import jax.numpy as jnp
from jax import lax
from jax.sharding import PartitionSpec as P

D_HEAD = 128
HEADS = 16
TILE = 4
TH_DEV = 4
TW = 16


MASKED_SCORE = -1e30


def passed_along(block, axis, distance):
    devices = range(lax.axis_size(axis))
    route = [((i - distance) % len(devices), i) for i in devices]
    return lax.ppermute(block, axis, route)


def with_halo(cells, sides, width):
    for axis, dim in sides:
        count = lax.axis_size(axis)
        ends = count - 1
        head = lax.slice_in_dim(cells, 0, width, axis=dim)
        tail = lax.slice_in_dim(cells, cells.shape[dim] - width, cells.shape[dim], axis=dim)
        cells = jnp.concatenate(
            [
                lax.ppermute(tail, axis, [(i, (i + 1) % count) for i in range(ends)]),
                cells,
                lax.ppermute(head, axis, [((i + 1) % count, i) for i in range(ends)]),
            ],
            axis=dim,
        )
    return cells


def shifted(value, axis, steps):
    count = lax.axis_size(axis)
    initial, last = (max(0, -steps), min(count, count - steps))
    return lax.ppermute(value, axis, [(source, source + steps) for source in range(initial, last)])


def to_tiles(grid_in, tile_edge):
    groups, frames, grid_rows, grid_cols = grid_in.shape[:4]
    trailing = grid_in.shape[4:]
    split_grid = grid_in.reshape(
        (
            groups,
            frames // tile_edge,
            tile_edge,
            grid_rows // tile_edge,
            tile_edge,
            grid_cols // tile_edge,
            tile_edge,
        )
        + trailing
    )
    axis_order = (0, 1, 3, 5, 2, 4, 6) + tuple(range(7, 7 + len(trailing)))
    return split_grid.transpose(axis_order).reshape(
        (groups, frames // tile_edge, grid_rows // tile_edge, grid_cols // tile_edge, tile_edge**3)
        + trailing
    )


def from_tiles(tiles_in, tile_edge):
    groups, frame_tiles, row_tiles, col_tiles = tiles_in.shape[:4]
    trailing = tiles_in.shape[5:]
    split_grid = tiles_in.reshape(
        (groups, frame_tiles, row_tiles, col_tiles, tile_edge, tile_edge, tile_edge) + trailing
    )
    axis_order = (0, 1, 4, 2, 5, 3, 6) + tuple(range(7, 7 + len(trailing)))
    return split_grid.transpose(axis_order).reshape(
        (groups, frame_tiles * tile_edge, row_tiles * tile_edge, col_tiles * tile_edge) + trailing
    )


def edge_tiles(piece_own, half_index):
    return jnp.where(half_index == 0, piece_own[:, :, :, -2:], piece_own[:, :, :, :2])


def widen_rim(piece_own, received, half_index):
    left_side = jnp.concatenate([piece_own, received], axis=3)
    right_side = jnp.concatenate([received, piece_own], axis=3)
    return jnp.where(half_index == 0, left_side, right_side)


def shards(queries, key_states, value_states, out_grad, tile_valid, width_shift):
    seq_count = lax.axis_size("seq")
    groups = 2 * HEADS // seq_count
    half_width = TW * TILE // 2
    lines_dev = queries.shape[0] // (TW * TILE)
    tiles_half = TW // 2
    tile_cells = TILE**3
    score_scale = D_HEAD ** (-0.5)
    time_index = lax.axis_index("tm")
    height_index = lax.axis_index("height")
    half_index = lax.axis_index("seq") * groups // HEADS
    anchor = half_index * (tiles_half - 2)

    def to_heads(rows_in):
        split_rows = rows_in.reshape(lines_dev, 2, half_width, HEADS, D_HEAD)
        return split_rows.transpose(1, 3, 0, 2, 4).reshape(2 * HEADS, lines_dev, half_width, D_HEAD)

    moved = (
        lax.all_to_all(to_heads(queries), "seq", split_axis=0, concat_axis=1, tiled=True),
        lax.all_to_all(to_heads(key_states), "seq", split_axis=0, concat_axis=1, tiled=True),
        lax.all_to_all(to_heads(value_states), "seq", split_axis=0, concat_axis=1, tiled=True),
        lax.all_to_all(to_heads(out_grad), "seq", split_axis=0, concat_axis=1, tiled=True),
    )

    def own_tiles(grid_part):
        return to_tiles(grid_part.reshape(groups, TILE, TILE * TH_DEV, half_width, D_HEAD), TILE)

    query_own, keys_own, values_own, grads_own = [own_tiles(grid_part) for grid_part in moved]
    key_edges = passed_along(
        (edge_tiles(keys_own, half_index), edge_tiles(values_own, half_index)),
        "seq",
        seq_count // 2,
    )
    keys_wide = widen_rim(keys_own, key_edges[0], half_index)
    values_wide = widen_rim(values_own, key_edges[1], half_index)
    keys_ext, values_ext = (
        with_halo(keys_wide, (("tm", 1), ("height", 2)), 1),
        with_halo(values_wide, (("tm", 1), ("height", 2)), 1),
    )
    table_start = (time_index, height_index * TH_DEV, anchor)
    table_span = (3, TH_DEV + 2, tiles_half + 2)
    table_pad = ((1, 1), (1, 1), (0, 0))
    valid_ext = lax.dynamic_slice(jnp.pad(tile_valid, table_pad), table_start, table_span)
    shift_ext = lax.dynamic_slice(jnp.pad(width_shift, table_pad), table_start, table_span)
    triple = jnp.arange(3)
    query_cols = jnp.arange(tiles_half) + 2 * half_index

    def query_row(keep_grads, carry, row_index):
        query_tiles = lax.dynamic_index_in_dim(query_own[:, 0], row_index, 1, keepdims=False)
        grad_tiles = lax.dynamic_index_in_dim(grads_own[:, 0], row_index, 1, keepdims=False)
        key_rows = lax.dynamic_slice_in_dim(keys_ext, row_index, 3, 2)
        value_rows = lax.dynamic_slice_in_dim(values_ext, row_index, 3, 2)
        shift_row = lax.dynamic_index_in_dim(shift_ext[1], row_index + 1, 0, keepdims=False)
        starts = query_cols + lax.dynamic_slice_in_dim(shift_row, 2 * half_index, tiles_half) - 1
        window_cols = starts[:, None] + triple[None, :]
        key_win = key_rows[:, :, :, window_cols].transpose(0, 3, 1, 2, 4, 5, 6)
        key_win = key_win.reshape(groups, tiles_half, 27 * tile_cells, D_HEAD)
        value_win = value_rows[:, :, :, window_cols].transpose(0, 3, 1, 2, 4, 5, 6)
        value_win = value_win.reshape(groups, tiles_half, 27 * tile_cells, D_HEAD)
        valid_rows = lax.dynamic_slice_in_dim(valid_ext, row_index, 3, 1)[:, :, window_cols]
        own_tile = (
            (triple[:, None, None, None] == 1)
            & (triple[None, :, None, None] == 1)
            & (window_cols[None, None] == query_cols[None, None, :, None])
        )
        allowed = ((valid_rows == 1) | own_tile).transpose(2, 0, 1, 3)
        tile_bias = jnp.where(allowed.reshape(tiles_half, 27, 1), 0.0, MASKED_SCORE).astype(
            jnp.float32
        )
        mask_bias = jnp.broadcast_to(tile_bias, (tiles_half, 27, tile_cells)).reshape(
            1, tiles_half, 1, 27 * tile_cells
        )
        scores = (
            score_scale
            * jnp.einsum(
                "gwid,gwjd->gwij", query_tiles, key_win, preferred_element_type=jnp.float32
            )
            + mask_bias
        )
        row_max = jnp.max(scores, axis=-1, keepdims=True)
        probs = jnp.exp(scores - row_max)
        exp_total = jnp.sum(probs, axis=-1, keepdims=True)
        log_total = row_max + jnp.log(exp_total)
        weights = probs / exp_total
        grad_weights = jnp.einsum(
            "gwid,gwjd->gwij", grad_tiles, value_win, preferred_element_type=jnp.float32
        )
        delta_row = jnp.sum(weights * grad_weights, axis=-1, keepdims=True)
        dscore = (weights * (grad_weights - delta_row)).astype(jnp.bfloat16)
        query_part = score_scale * jnp.einsum(
            "gwij,gwjd->gwid", dscore, key_win, preferred_element_type=jnp.float32
        )
        key_acc, value_acc = carry
        key_part = score_scale * jnp.einsum(
            "gwij,gwid->gwjd", dscore, query_tiles, preferred_element_type=jnp.float32
        )
        value_part = jnp.einsum(
            "gwij,gwid->gwjd",
            weights.astype(jnp.bfloat16),
            grad_tiles,
            preferred_element_type=jnp.float32,
        )
        time_pick = triple[None, :, None, None]
        row_pick = triple[None, None, :, None]
        col_pick = window_cols[:, None, None, :]

        def spread(acc_grid, part_grad):
            shaped = part_grad.reshape(groups, tiles_half, 3, 3, 3, tile_cells, D_HEAD)
            rows_now = lax.dynamic_slice_in_dim(acc_grid, row_index, 3, 2)
            rows_now = rows_now.at[:, time_pick, row_pick, col_pick].add(shaped)
            return lax.dynamic_update_slice_in_dim(acc_grid, rows_now, row_index, 2)

        carry = (spread(key_acc, key_part), spread(value_acc, value_part))
        return (carry, (query_part, log_total[..., 0], delta_row[..., 0]))

    zero_grads = jnp.zeros(keys_ext.shape, jnp.float32)
    (key_acc, value_acc), row_outputs = lax.scan(
        partial(query_row, True), (zero_grads, zero_grads), jnp.arange(TH_DEV)
    )
    from_below = (
        shifted(key_acc[:, :, -1:].astype(jnp.bfloat16), "height", 1).astype(jnp.float32),
        shifted(value_acc[:, :, -1:].astype(jnp.bfloat16), "height", 1).astype(jnp.float32),
    )
    from_above = (
        shifted(key_acc[:, :, :1].astype(jnp.bfloat16), "height", -1).astype(jnp.float32),
        shifted(value_acc[:, :, :1].astype(jnp.bfloat16), "height", -1).astype(jnp.float32),
    )

    def fold_rows(acc_grid, lower_in, upper_in):
        acc_grid = acc_grid.at[:, :, 1:2].add(lower_in)
        acc_grid = acc_grid.at[:, :, TH_DEV : TH_DEV + 1].add(upper_in)
        return acc_grid[:, :, 1 : TH_DEV + 1]

    key_core = fold_rows(key_acc, from_below[0], from_above[0])
    value_core = fold_rows(value_acc, from_below[1], from_above[1])
    from_before = shifted((key_core[:, 2:3], value_core[:, 2:3]), "tm", 1)
    from_after = shifted((key_core[:, 0:1], value_core[:, 0:1]), "tm", -1)
    key_mid = key_core[:, 1] + from_before[0][:, 0] + from_after[0][:, 0]
    value_mid = value_core[:, 1] + from_before[1][:, 0] + from_after[1][:, 0]

    def rim_of(mid_grid):
        return jnp.where(half_index == 0, mid_grid[:, :, -2:], mid_grid[:, :, :2])

    rim_back = (
        passed_along(rim_of(key_mid).astype(jnp.bfloat16), "seq", seq_count // 2).astype(
            jnp.float32
        ),
        passed_along(rim_of(value_mid).astype(jnp.bfloat16), "seq", seq_count // 2).astype(
            jnp.float32
        ),
    )

    def settle(mid_grid, received):
        left_side = jnp.concatenate(
            [
                mid_grid[:, :, : tiles_half - 2],
                mid_grid[:, :, tiles_half - 2 : tiles_half] + received,
            ],
            axis=2,
        )
        right_side = jnp.concatenate([mid_grid[:, :, 2:4] + received, mid_grid[:, :, 4:]], axis=2)
        return jnp.where(half_index == 0, left_side, right_side)

    key_grid = from_tiles(settle(key_mid, rim_back[0])[:, None], TILE).astype(jnp.bfloat16)
    value_grid = from_tiles(settle(value_mid, rim_back[1])[:, None], TILE).astype(jnp.bfloat16)
    query_grid = from_tiles(jnp.moveaxis(row_outputs[0], 0, 1)[:, None], TILE).astype(jnp.bfloat16)

    def to_lines(grid_part):
        return grid_part.reshape(groups, TILE * TILE * TH_DEV, half_width, D_HEAD)

    returned = (
        lax.all_to_all(to_lines(query_grid), "seq", split_axis=1, concat_axis=0, tiled=True),
        lax.all_to_all(to_lines(key_grid), "seq", split_axis=1, concat_axis=0, tiled=True),
        lax.all_to_all(to_lines(value_grid), "seq", split_axis=1, concat_axis=0, tiled=True),
    )

    def to_rows(grid_part):
        split_rows = grid_part.reshape(2, HEADS, lines_dev, half_width, D_HEAD)
        return split_rows.transpose(2, 0, 3, 1, 4).reshape(
            lines_dev * 2 * half_width, HEADS * D_HEAD
        )

    return (to_rows(returned[0]), to_rows(returned[1]), to_rows(returned[2]))


def solution(mesh):
    placed = (
        P(("tm", "height", "seq"), None),
        P(("tm", "height", "seq"), None),
        P(("tm", "height", "seq"), None),
        P(("tm", "height", "seq"), None),
        P(),
        P(),
    )
    return jax.shard_map(
        shards,
        mesh=mesh,
        in_specs=placed,
        out_specs=(
            P(("tm", "height", "seq"), None),
            P(("tm", "height", "seq"), None),
            P(("tm", "height", "seq"), None),
        ),
        check_vma=False,
    )
```

profile of v0, /device:TPU:9, one launch (start us, length us, event | category | flops | bytes accessed | tf_op | source)
XLA Modules:
  0.0 2456.0 jit_solution(8433223892784764136)
XLA Ops:
  14.4 41.4 %all-to-all-done.1 = bf16[32,8,32,128]{3,2,1,0:T(8,128)(2,1)S(1)} async-done(((bf16[32,8,32,128]{3,2,1,0:T(8,128)(2,1)}), bf16[32,8,32,128]{3,2,1,0:T(8,128)(2,1)S(1)}, u32[]{:S(2)}, u32[]{:S(2)}) %all-to-all-start.1) | async-done | bytes 2097184 | tf_op jit(solution)/shard_map/all_to_all | solution.py:110
  67.7 41.4 %all-to-all-done.3 = bf16[32,8,32,128]{3,2,1,0:T(8,128)(2,1)} async-done(((bf16[32,8,32,128]{3,2,1,0:T(8,128)(2,1)}), bf16[32,8,32,128]{3,2,1,0:T(8,128)(2,1)}, u32[]{:S(2)}, u32[]{:S(2)}) %all-to-all-start.3) | async-done | bytes 2097184 | tf_op jit(solution)/shard_map/all_to_all | solution.py:111
  122.8 62.1 %collective-permute-done.5 = bf16[4,1,4,2,64,128]{5,3,4,2,0,1:T(2,128)(2,1)S(1)} collective-permute-done((bf16[4,1,4,2,64,128]{5,3,4,2,0,1:T(2,128)(2,1)S(1)}, bf16[4,1,4,2,64,128]{5,3,4,2,0,1:T(2,128)(2,1)S(1)}, u32[]{:S(2)}, u32[]{:S(2)}) %collective-permute-start.5) | collective-permute-done | bytes 524320 | tf_op jit(solution)/shard_map/ppermute | solution.py:21
  212.5 64.9 %collective-permute-done = bf16[4,1,4,2,64,128]{5,3,4,2,0,1:T(2,128)(2,1)S(1)} collective-permute-done((bf16[4,1,4,2,64,128]{5,3,4,2,0,1:T(2,128)(2,1)S(1)}, bf16[4,1,4,2,64,128]{5,3,4,2,0,1:T(2,128)(2,1)S(1)}, u32[]{:S(2)}, u32[]{:S(2)}) %collective-permute-start) | collective-permute-done | bytes 524320 | tf_op jit(solution)/shard_map/ppermute | solution.py:21
  323.3 20.4 collective-permute-done.2
  443.4 1606.8 %while.23 = (s32[]{:T(128)}, f32[4,3,6,10,64,128]{5,4,3,2,0,1:T(8,128)}, f32[4,3,6,10,64,128]{5,4,3,2,1,0:T(8,128)}, bf16[4,4,8,64,128]{4,3,2,1,0:T(8,128)(2,1)}...) while((s32[]{:T(128)}, ...), condition=%wide.region_6.7_spmd.clone.clone, body=%wide.region_0.6_spmd.clone.clone.sunk | while | flops 4604431360 | bytes 804304768 | solution.py:207
  574.2 16.6 fusion.87
  642.0 20.6 copy.314
  662.6 70.0 %scatter_fusion.1 = f32[4,3,3,10,64,128]{5,4,3,2,1,0:T(8,128)} fusion(f32[4,3,3,10,64,128]{5,4,3,2,1,0:T(8,128)} %constant_dynamic-slice_fusion.13, s32[216]{0:T(256)S(1)} %reshape.820, f32[216,4,64,128]{3,2,1,0:T(8,128)} %bitcast.214), kind=kCustom, calls=%fused_computation.4.clone.clone.1 | custom fusion | flops 7077888 | bytes 84937248 | tf_op jit(solution)/shard_map/while/body/eval_jaxpr/scatter-add | solution.py:200
  757.2 20.6 copy.313
  777.8 69.8 %scatter_fusion = f32[4,3,3,10,64,128]{5,4,3,2,1,0:T(8,128)} fusion(f32[4,3,3,10,64,128]{5,4,3,2,1,0:T(8,128)} %copy.307, s32[216]{0:T(256)S(1)} %reshape.820, f32[216,4,64,128]{3,2,1,0:T(8,128)} %bitcast.213), kind=kCustom, calls=%fused_computation.3.clone.clone.1 | custom fusion | flops 7077888 | bytes 84937248 | tf_op jit(solution)/shard_map/while/body/eval_jaxpr/scatter-add | solution.py:200
  968.7 16.6 fusion.87
  1036.5 20.6 copy.314
  1057.1 70.0 %scatter_fusion.1 = f32[4,3,3,10,64,128]{5,4,3,2,1,0:T(8,128)} fusion(f32[4,3,3,10,64,128]{5,4,3,2,1,0:T(8,128)} %constant_dynamic-slice_fusion.13, s32[216]{0:T(256)S(1)} %reshape.820, f32[216,4,64,128]{3,2,1,0:T(8,128)} %bitcast.214), kind=kCustom, calls=%fused_computation.4.clone.clone.1 | custom fusion | flops 7077888 | bytes 84937248 | tf_op jit(solution)/shard_map/while/body/eval_jaxpr/scatter-add | solution.py:200
  1151.8 20.6 copy.313
  1172.4 69.8 %scatter_fusion = f32[4,3,3,10,64,128]{5,4,3,2,1,0:T(8,128)} fusion(f32[4,3,3,10,64,128]{5,4,3,2,1,0:T(8,128)} %copy.307, s32[216]{0:T(256)S(1)} %reshape.820, f32[216,4,64,128]{3,2,1,0:T(8,128)} %bitcast.213), kind=kCustom, calls=%fused_computation.3.clone.clone.1 | custom fusion | flops 7077888 | bytes 84937248 | tf_op jit(solution)/shard_map/while/body/eval_jaxpr/scatter-add | solution.py:200
  1363.5 16.6 fusion.87
  1431.3 20.6 copy.314
  1451.9 69.8 %scatter_fusion.1 = f32[4,3,3,10,64,128]{5,4,3,2,1,0:T(8,128)} fusion(f32[4,3,3,10,64,128]{5,4,3,2,1,0:T(8,128)} %constant_dynamic-slice_fusion.13, s32[216]{0:T(256)S(1)} %reshape.820, f32[216,4,64,128]{3,2,1,0:T(8,128)} %bitcast.214), kind=kCustom, calls=%fused_computation.4.clone.clone.1 | custom fusion | flops 7077888 | bytes 84937248 | tf_op jit(solution)/shard_map/while/body/eval_jaxpr/scatter-add | solution.py:200
  1546.3 20.6 copy.313
  1566.9 69.9 %scatter_fusion = f32[4,3,3,10,64,128]{5,4,3,2,1,0:T(8,128)} fusion(f32[4,3,3,10,64,128]{5,4,3,2,1,0:T(8,128)} %copy.307, s32[216]{0:T(256)S(1)} %reshape.820, f32[216,4,64,128]{3,2,1,0:T(8,128)} %bitcast.213), kind=kCustom, calls=%fused_computation.3.clone.clone.1 | custom fusion | flops 7077888 | bytes 84937248 | tf_op jit(solution)/shard_map/while/body/eval_jaxpr/scatter-add | solution.py:200
  1758.0 16.6 fusion.87
  1825.8 20.6 copy.314
  1846.4 69.9 %scatter_fusion.1 = f32[4,3,3,10,64,128]{5,4,3,2,1,0:T(8,128)} fusion(f32[4,3,3,10,64,128]{5,4,3,2,1,0:T(8,128)} %constant_dynamic-slice_fusion.13, s32[216]{0:T(256)S(1)} %reshape.820, f32[216,4,64,128]{3,2,1,0:T(8,128)} %bitcast.214), kind=kCustom, calls=%fused_computation.4.clone.clone.1 | custom fusion | flops 7077888 | bytes 84937248 | tf_op jit(solution)/shard_map/while/body/eval_jaxpr/scatter-add | solution.py:200
  1940.9 20.6 copy.313
  1961.5 69.8 %scatter_fusion = f32[4,3,3,10,64,128]{5,4,3,2,1,0:T(8,128)} fusion(f32[4,3,3,10,64,128]{5,4,3,2,1,0:T(8,128)} %copy.307, s32[216]{0:T(256)S(1)} %reshape.820, f32[216,4,64,128]{3,2,1,0:T(8,128)} %bitcast.213), kind=kCustom, calls=%fused_computation.3.clone.clone.1 | custom fusion | flops 7077888 | bytes 84937248 | tf_op jit(solution)/shard_map/while/body/eval_jaxpr/scatter-add | solution.py:200
  2073.5 34.3 %collective-permute-done.10 = bf16[4,3,1,10,64,128]{5,4,3,2,0,1:T(8,128)(2,1)} collective-permute-done((bf16[4,3,1,10,64,128]{5,4,3,2,0,1:T(8,128)(2,1)}, bf16[4,3,1,10,64,128]{5,4,3,2,0,1:T(8,128)(2,1)}, u32[]{:S(2)}, u32[]{:S(2)}) %collective-permute-start.10) | collective-permute-done | bytes 1966112 | tf_op jit(solution)/shard_map/ppermute | solution.py:44
  2141.9 36.6 %collective-permute-done.15 = bf16[4,3,1,10,64,128]{5,4,3,2,1,0:T(8,128)(2,1)S(1)} collective-permute-done((bf16[4,3,1,10,64,128]{5,4,3,2,1,0:T(8,128)(2,1)S(1)}, bf16[4,3,1,10,64,128]{5,4,3,2,1,0:T(8,128)(2,1)S(1)}, u32[]{:S(2)}, u32[]{:S(2)}) %collective-permute-start.15) | collective-permute-done | bytes 1966112 | tf_op jit(solution)/shard_map/ppermute | solution.py:44
  2258.1 34.5 %collective-permute-done.14 = bf16[4,4,2,64,128]{4,3,2,1,0:T(8,128)(2,1)S(1)} collective-permute-done((bf16[4,4,2,64,128]{4,3,2,1,0:T(8,128)(2,1)S(1)}, bf16[4,4,2,64,128]{4,3,2,1,0:T(8,128)(2,1)S(1)}, u32[]{:S(2)}, u32[]{:S(2)}) %collective-permute-start.14) | collective-permute-done | bytes 524320 | tf_op jit(solution)/shard_map/ppermute | solution.py:21
  2307.0 45.6 %collective-permute-done.17 = f32[4,1,4,10,64,128]{5,4,3,2,1,0:T(8,128)} collective-permute-done((f32[4,1,4,10,64,128]{5,4,3,2,1,0:T(8,128)}, f32[4,1,4,10,64,128]{5,4,3,2,1,0:T(8,128)}, u32[]{:S(2)}, u32[]{:S(2)}) %collective-permute-start.17) | collective-permute-done | bytes 5242912 | tf_op jit(solution)/shard_map/ppermute | solution.py:44
  2370.5 19.6 collective-permute-done.19
  2413.8 36.3 %all-to-all-done.6 = bf16[4,64,32,128]{3,2,0,1:T(8,128)(2,1)} async-done(((bf16[4,64,32,128]{3,2,0,1:T(8,128)(2,1)}), bf16[4,64,32,128]{3,2,0,1:T(8,128)(2,1)}, u32[]{:S(2)}, u32[]{:S(2)}) %all-to-all-start.6) | async-done | bytes 2097184 | tf_op jit(solution)/shard_map/all_to_all | solution.py:264
  (386 shorter events, 1178.6 us)
Async XLA Ops:
  4.7 51.1 %all-to-all-start.1 = ((bf16[32,8,32,128]{3,2,1,0:T(8,128)(2,1)}), bf16[32,8,32,128]{3,2,1,0:T(8,128)(2,1)S(1)}, u32[]{:S(2)}, u32[]{:S(2)}) async-start(bf16[32,8,32,128]{3,2,1,0:T(8,128)(2,1)} %bitcast.235), calls=%async_computation.1 | async-start | bytes 4194304 | tf_op jit(solution)/shard_map/all_to_all | solution.py:110
  55.9 53.3 %all-to-all-start.3 = ((bf16[32,8,32,128]{3,2,1,0:T(8,128)(2,1)}), bf16[32,8,32,128]{3,2,1,0:T(8,128)(2,1)}, u32[]{:S(2)}, u32[]{:S(2)}) async-start(bf16[32,8,32,128]{3,2,1,0:T(8,128)(2,1)} %bitcast.234), calls=%async_computation.3 | async-start | bytes 4194304 | tf_op jit(solution)/shard_map/all_to_all | solution.py:111
  109.2 91.8 %all-to-all-start = ((bf16[32,8,32,128]{3,2,1,0:T(8,128)(2,1)}), bf16[32,8,32,128]{3,2,1,0:T(8,128)(2,1)}, u32[]{:S(2)}, u32[]{:S(2)}) async-start(bf16[32,8,32,128]{3,2,1,0:T(8,128)(2,1)} %bitcast.233), calls=%async_computation | async-start | bytes 4194304 | tf_op jit(solution)/shard_map/all_to_all | solution.py:109
  120.6 64.3 %collective-permute-start.5 = (bf16[4,1,4,2,64,128]{5,3,4,2,0,1:T(2,128)(2,1)S(1)}, bf16[4,1,4,2,64,128]{5,3,4,2,0,1:T(2,128)(2,1)S(1)}, u32[]{:S(2)}, u32[]{:S(2)}) collective-permute-start(bf16[4,1,4,2,64,128]{5,3,4,2,0,1:T(2,128)(2,1)S(1)} %broadcast_select_fusion), channel_id=1, source_target_pairs={{4,0},{5,1},{6,2},{7,3},{0,4},{1,5},{2,6},{3,7},{12,8},{13,9},{14,... | collective-permute-start | bytes 1572872 | tf_op jit(solution)/shard_map/ppermute | solution.py:21
  189.2 103.0 %collective-permute-start.7 = (bf16[4,1,4,10,64,128]{5,4,3,2,1,0:T(8,128)(2,1)}, bf16[4,1,4,10,64,128]{5,4,3,2,1,0:T(8,128)(2,1)}, u32[]{:S(2)}, u32[]{:S(2)}) collective-permute-start(bf16[4,1,4,10,64,128]{5,4,3,2,1,0:T(8,128)(2,1)} %copy.229), channel_id=1, source_target_pairs={{16,0},{17,1},{18,2},{19,3},{20,4},{21,5},{22,6},{23,7},{24,8},{25... | collective-permute-start | bytes 7864328 | tf_op jit(solution)/shard_map/ppermute | solution.py:34
  190.5 105.8 %collective-permute-start.6 = (bf16[4,1,4,10,64,128]{5,4,3,2,1,0:T(8,128)(2,1)}, bf16[4,1,4,10,64,128]{5,4,3,2,1,0:T(8,128)(2,1)}, u32[]{:S(2)}, u32[]{:S(2)}) collective-permute-start(bf16[4,1,4,10,64,128]{5,4,3,2,1,0:T(8,128)(2,1)} %copy.229), channel_id=1, source_target_pairs={{0,16},{1,17},{2,18},{3,19},{4,20},{5,21},{6,22},{7,23},{8,24},{9,... | collective-permute-start | bytes 7864328 | tf_op jit(solution)/shard_map/ppermute | solution.py:32
  201.0 117.8 %all-to-all-start.2 = ((bf16[32,8,32,128]{3,2,1,0:T(8,128)(2,1)}), bf16[32,8,32,128]{3,2,1,0:T(8,128)(2,1)}, u32[]{:S(2)}, u32[]{:S(2)}) async-start(bf16[32,8,32,128]{3,2,1,0:T(8,128)(2,1)} %bitcast.230), calls=%async_computation.2 | async-start | bytes 4194304 | tf_op jit(solution)/shard_map/all_to_all | solution.py:112
  210.3 67.1 %collective-permute-start = (bf16[4,1,4,2,64,128]{5,3,4,2,0,1:T(2,128)(2,1)S(1)}, bf16[4,1,4,2,64,128]{5,3,4,2,0,1:T(2,128)(2,1)S(1)}, u32[]{:S(2)}, u32[]{:S(2)}) collective-permute-start(bf16[4,1,4,2,64,128]{5,3,4,2,0,1:T(2,128)(2,1)S(1)} %broadcast_select_fusion.1), channel_id=1, source_target_pairs={{4,0},{5,1},{6,2},{7,3},{0,4},{1,5},{2,6},{3,7},{12,8},{13,9},{14,... | collective-permute-start | bytes 1572872 | tf_op jit(solution)/shard_map/ppermute | solution.py:21
  283.5 60.2 %collective-permute-start.2 = (bf16[4,1,4,10,64,128]{5,4,3,2,1,0:T(8,128)(2,1)}, bf16[4,1,4,10,64,128]{5,4,3,2,1,0:T(8,128)(2,1)}, u32[]{:S(2)}, u32[]{:S(2)}) collective-permute-start(bf16[4,1,4,10,64,128]{5,4,3,2,1,0:T(8,128)(2,1)} %copy.215), channel_id=1, source_target_pairs={{16,0},{17,1},{18,2},{19,3},{20,4},{21,5},{22,6},{23,7},{24,8},{25... | collective-permute-start | bytes 7864328 | tf_op jit(solution)/shard_map/ppermute | solution.py:34
  284.8 62.9 %collective-permute-start.1 = (bf16[4,1,4,10,64,128]{5,4,3,2,1,0:T(8,128)(2,1)}, bf16[4,1,4,10,64,128]{5,4,3,2,1,0:T(8,128)(2,1)}, u32[]{:S(2)}, u32[]{:S(2)}) collective-permute-start(bf16[4,1,4,10,64,128]{5,4,3,2,1,0:T(8,128)(2,1)} %copy.215), channel_id=1, source_target_pairs={{0,16},{1,17},{2,18},{3,19},{4,20},{5,21},{6,22},{7,23},{8,24},{9,... | collective-permute-start | bytes 7864328 | tf_op jit(solution)/shard_map/ppermute | solution.py:32
  305.8 60.0 %collective-permute-start.9 = (bf16[4,3,1,10,64,128]{5,4,3,2,1,0:T(8,128)(2,1)}, bf16[4,3,1,10,64,128]{5,4,3,2,1,0:T(8,128)(2,1)}, u32[]{:S(2)}, u32[]{:S(2)}) collective-permute-start(bf16[4,3,1,10,64,128]{5,4,3,2,1,0:T(8,128)(2,1)} %copy.234), channel_id=1, source_target_pairs={{8,0},{9,1},{10,2},{11,3},{12,4},{13,5},{14,6},{15,7},{24,16},{25,... | collective-permute-start | bytes 5898248 | tf_op jit(solution)/shard_map/ppermute | solution.py:34
  308.9 61.7 %collective-permute-start.8 = (bf16[4,3,1,10,64,128]{5,4,3,2,1,0:T(8,128)(2,1)}, bf16[4,3,1,10,64,128]{5,4,3,2,1,0:T(8,128)(2,1)}, u32[]{:S(2)}, u32[]{:S(2)}) collective-permute-start(bf16[4,3,1,10,64,128]{5,4,3,2,1,0:T(8,128)(2,1)} %copy.233), channel_id=1, source_target_pairs={{0,8},{1,9},{2,10},{3,11},{4,12},{5,13},{6,14},{7,15},{16,24},{17,... | collective-permute-start | bytes 5898248 | tf_op jit(solution)/shard_map/ppermute | solution.py:32
  357.6 45.6 %collective-permute-start.4 = (bf16[4,3,1,10,64,128]{5,4,3,2,1,0:T(8,128)(2,1)}, bf16[4,3,1,10,64,128]{5,4,3,2,1,0:T(8,128)(2,1)}, u32[]{:S(2)}, u32[]{:S(2)}) collective-permute-start(bf16[4,3,1,10,64,128]{5,4,3,2,1,0:T(8,128)(2,1)} %copy.220), channel_id=1, source_target_pairs={{8,0},{9,1},{10,2},{11,3},{12,4},{13,5},{14,6},{15,7},{24,16},{25,... | collective-permute-start | bytes 5898248 | tf_op jit(solution)/shard_map/ppermute | solution.py:34
  359.1 47.2 %collective-permute-start.3 = (bf16[4,3,1,10,64,128]{5,4,3,2,1,0:T(8,128)(2,1)}, bf16[4,3,1,10,64,128]{5,4,3,2,1,0:T(8,128)(2,1)}, u32[]{:S(2)}, u32[]{:S(2)}) collective-permute-start(bf16[4,3,1,10,64,128]{5,4,3,2,1,0:T(8,128)(2,1)} %copy.219), channel_id=1, source_target_pairs={{0,8},{1,9},{2,10},{3,11},{4,12},{5,13},{6,14},{7,15},{16,24},{17,... | collective-permute-start | bytes 5898248 | tf_op jit(solution)/shard_map/ppermute | solution.py:32
  2050.2 20.3 slice-start
  2050.2 20.3 slice-start.1
  2050.2 20.3 slice-start.2
  2050.2 20.3 slice-start.3
  2050.2 20.3 slice-start.4
  2064.1 43.7 %collective-permute-start.10 = (bf16[4,3,1,10,64,128]{5,4,3,2,0,1:T(8,128)(2,1)}, bf16[4,3,1,10,64,128]{5,4,3,2,0,1:T(8,128)(2,1)}, u32[]{:S(2)}, u32[]{:S(2)}) collective-permute-start(bf16[4,3,1,10,64,128]{5,4,3,2,0,1:T(8,128)(2,1)} %get-tuple-element.479), channel_id=1, source_target_pairs={{0,8},{1,9},{2,10},{3,11},{4,12},{5,13},{6,14},{7,15},{16,24},{17,... | collective-permute-start | bytes 5898248 | tf_op jit(solution)/shard_map/ppermute | solution.py:44
  2069.2 44.2 %collective-permute-start.11 = (bf16[4,3,1,10,64,128]{5,4,3,2,0,1:T(8,128)(2,1)}, bf16[4,3,1,10,64,128]{5,4,3,2,0,1:T(8,128)(2,1)}, u32[]{:S(2)}, u32[]{:S(2)}) collective-permute-start(bf16[4,3,1,10,64,128]{5,4,3,2,0,1:T(8,128)(2,1)} %get-tuple-element.478), channel_id=1, source_target_pairs={{8,0},{9,1},{10,2},{11,3},{12,4},{13,5},{14,6},{15,7},{24,16},{25,... | collective-permute-start | bytes 5898248 | tf_op jit(solution)/shard_map/ppermute | solution.py:44
  2129.2 111.0 %collective-permute-start.12 = (f32[4,1,4,10,64,128]{5,4,3,2,0,1:T(8,128)}, f32[4,1,4,10,64,128]{5,4,3,2,0,1:T(8,128)}, u32[]{:S(2)}, u32[]{:S(2)}) collective-permute-start(f32[4,1,4,10,64,128]{5,4,3,2,0,1:T(8,128)} %get-tuple-element.470), channel_id=1, source_target_pairs={{0,16},{1,17},{2,18},{3,19},{4,20},{5,21},{6,22},{7,23},{8,24},{9,... | collective-permute-start | bytes 15728648 | tf_op jit(solution)/shard_map/ppermute | solution.py:44
  2133.7 112.7 %collective-permute-start.13 = (f32[4,1,4,10,64,128]{5,4,3,2,0,1:T(8,128)}, f32[4,1,4,10,64,128]{5,4,3,2,0,1:T(8,128)}, u32[]{:S(2)}, u32[]{:S(2)}) collective-permute-start(f32[4,1,4,10,64,128]{5,4,3,2,0,1:T(8,128)} %get-tuple-element.471), channel_id=1, source_target_pairs={{16,0},{17,1},{18,2},{19,3},{20,4},{21,5},{22,6},{23,7},{24,8},{25... | collective-permute-start | bytes 15728648 | tf_op jit(solution)/shard_map/ppermute | solution.py:44
  2136.4 42.2 %collective-permute-start.15 = (bf16[4,3,1,10,64,128]{5,4,3,2,1,0:T(8,128)(2,1)S(1)}, bf16[4,3,1,10,64,128]{5,4,3,2,1,0:T(8,128)(2,1)S(1)}, u32[]{:S(2)}, u32[]{:S(2)}) collective-permute-start(bf16[4,3,1,10,64,128]{5,4,3,2,1,0:T(8,128)(2,1)S(1)} %get-tuple-element.477), channel_id=1, source_target_pairs={{0,8},{1,9},{2,10},{3,11},{4,12},{5,13},{6,14},{7,15},{16,24},{17,... | collective-permute-start | bytes 5898248 | tf_op jit(solution)/shard_map/ppermute | solution.py:44
  2140.6 43.0 %collective-permute-start.16 = (bf16[4,3,1,10,64,128]{5,4,3,2,1,0:T(8,128)(2,1)S(1)}, bf16[4,3,1,10,64,128]{5,4,3,2,1,0:T(8,128)(2,1)S(1)}, u32[]{:S(2)}, u32[]{:S(2)}) collective-permute-start(bf16[4,3,1,10,64,128]{5,4,3,2,1,0:T(8,128)(2,1)S(1)} %get-tuple-element.476), channel_id=1, source_target_pairs={{8,0},{9,1},{10,2},{11,3},{12,4},{13,5},{14,6},{15,7},{24,16},{25,... | collective-permute-start | bytes 5898248 | tf_op jit(solution)/shard_map/ppermute | solution.py:44
  2198.7 153.9 %collective-permute-start.17 = (f32[4,1,4,10,64,128]{5,4,3,2,1,0:T(8,128)}, f32[4,1,4,10,64,128]{5,4,3,2,1,0:T(8,128)}, u32[]{:S(2)}, u32[]{:S(2)}) collective-permute-start(f32[4,1,4,10,64,128]{5,4,3,2,1,0:T(8,128)} %get-tuple-element.468), channel_id=1, source_target_pairs={{0,16},{1,17},{2,18},{3,19},{4,20},{5,21},{6,22},{7,23},{8,24},{9,... | collective-permute-start | bytes 15728648 | tf_op jit(solution)/shard_map/ppermute | solution.py:44
  2207.1 151.7 %collective-permute-start.18 = (f32[4,1,4,10,64,128]{5,4,3,2,1,0:T(8,128)}, f32[4,1,4,10,64,128]{5,4,3,2,1,0:T(8,128)}, u32[]{:S(2)}, u32[]{:S(2)}) collective-permute-start(f32[4,1,4,10,64,128]{5,4,3,2,1,0:T(8,128)} %get-tuple-element.469), channel_id=1, source_target_pairs={{16,0},{17,1},{18,2},{19,3},{20,4},{21,5},{22,6},{23,7},{24,8},{25... | collective-permute-start | bytes 15728648 | tf_op jit(solution)/shard_map/ppermute | solution.py:44
  2213.1 85.7 %all-to-all-start.4 = ((bf16[4,64,32,128]{3,2,0,1:T(8,128)(2,1)}), bf16[4,64,32,128]{3,2,0,1:T(8,128)(2,1)S(1)}, u32[]{:S(2)}, u32[]{:S(2)}) async-start(bf16[4,64,32,128]{3,2,0,1:T(8,128)(2,1)} %copy.242), calls=%async_computation.4 | async-start | bytes 4194304 | tf_op jit(solution)/shard_map/all_to_all | solution.py:262
  2254.0 38.7 %collective-permute-start.14 = (bf16[4,4,2,64,128]{4,3,2,1,0:T(8,128)(2,1)S(1)}, bf16[4,4,2,64,128]{4,3,2,1,0:T(8,128)(2,1)S(1)}, u32[]{:S(2)}, u32[]{:S(2)}) collective-permute-start(bf16[4,4,2,64,128]{4,3,2,1,0:T(8,128)(2,1)S(1)} %fusion.43), channel_id=1, source_target_pairs={{4,0},{5,1},{6,2},{7,3},{0,4},{1,5},{2,6},{3,7},{12,8},{13,9},{14,... | collective-permute-start | bytes 1572872 | tf_op jit(solution)/shard_map/ppermute | solution.py:21
  2298.8 97.5 %all-to-all-start.5 = ((bf16[4,64,32,128]{3,2,0,1:T(8,128)(2,1)}), bf16[4,64,32,128]{3,2,0,1:T(8,128)(2,1)}, u32[]{:S(2)}, u32[]{:S(2)}) async-start(bf16[4,64,32,128]{3,2,0,1:T(8,128)(2,1)} %copy.253), calls=%async_computation.5 | async-start | bytes 4194304 | tf_op jit(solution)/shard_map/all_to_all | solution.py:263
  2366.3 23.8 collective-permute-start.19
  2396.3 53.8 %all-to-all-start.6 = ((bf16[4,64,32,128]{3,2,0,1:T(8,128)(2,1)}), bf16[4,64,32,128]{3,2,0,1:T(8,128)(2,1)}, u32[]{:S(2)}, u32[]{:S(2)}) async-start(bf16[4,64,32,128]{3,2,0,1:T(8,128)(2,1)} %copy.261), calls=%async_computation.6 | async-start | bytes 4194304 | tf_op jit(solution)/shard_map/all_to_all | solution.py:264
  (43 other events, 379.3 us)
where the time goes:
time: 2470 us; the launch traced here: 2460 us
  local copies, waits for them, and re-layouts  783 us (32%)
  other arithmetic  750 us (30%)
  waiting for transfers between devices  477 us (19%)
  matrix products  266 us (11%)
  starting transfers between devices  129 us (5%)
  loops' own time  48.1 us (2%)
    scatter-add x8, other arithmetic, spread(): rows_now = rows_now.at[:, time_pick, row_pick, col_pick].add(shaped)  559 us
    ppermute x4, waiting for transfers between devices, passed_along(): return lax.ppermute(block, axis, route)  181 us
    reshape x8, local copies, waits for them, and re-layouts, spread(): shaped = part_grad.reshape(groups, tiles_half, 3, 3, 3, tile_cells, D_HEAD)  165 us
    ppermute x8, waiting for transfers between devices, shifted(): lax.ppermute(value, axis, [(source, source + steps) for source in range(i...  144 us
    dynamic_slice x12, local copies, waits for them, and re-layouts, spread(): rows_now = lax.dynamic_slice_in_dim(acc_grid, row_index, 3, 2)  135 us
    dynamic_update_slice x8, local copies, waits for them, and re-layouts, spread(): return lax.dynamic_update_slice_in_dim(acc_grid, rows_now, row_index, 2)  89.6 us
    sub x4, other arithmetic, query_row(): probs = jnp.exp(scores - row_max)  66.3 us
    dot_general x4, matrix products, query_row(): jnp.einsum('gwid,gwjd->gwij', grad_tiles, value_win, preferred_element_ty...  61.4 us
  transfers between devices with their start and end apart: 27, of which 15 were waited for; matrix products, arithmetic and copies ran while one was open for 7% of the time, Pallas kernels for 0%

commit v1 on v0

--- a/solution.py
+++ b/solution.py
@@ -3,6 +3,8 @@
 import jax
 import jax.numpy as jnp
 from jax import lax
+from jax.experimental import pallas as pl
+from jax.experimental.pallas import tpu as pltpu
 from jax.sharding import PartitionSpec as P
 
 D_HEAD = 128
@@ -273,7 +275,271 @@
     return (to_rows(returned[0]), to_rows(returned[1]), to_rows(returned[2]))
 
 
+TOK = TILE * TILE
+SPAN = 5
+LANES = 2 * D_HEAD
+LOG2_E = 1.4426950408889634
+VMEM_BYTES = 56 * 1024 * 1024
+NT = (((1,), (1,)), ((), ()))
+NN = (((1,), (0,)), ((), ()))
+TN = (((0,), (0,)), ((), ()))
+
+
+def row_order(inverse):
+    lines = TILE * TW * TILE
+    target = lax.broadcasted_iota(jnp.int32, (lines, lines), 0)
+    source = lax.broadcasted_iota(jnp.int32, (lines, lines), 1)
+    if inverse:
+        target, source = source, target
+    col, line, x = target // TOK, (target // TILE) % TILE, target % TILE
+    return (source == line * (TW * TILE) + col * TILE + x).astype(jnp.bfloat16)
+
+
+def split_kernel(first_ref, second_ref, out_ref):
+    order = row_order(False)
+    lines = order.shape[0]
+    heads = out_ref.shape[0]
+    for row in range(first_ref.shape[0] // lines):
+        rows = slice(row * lines, (row + 1) * lines)
+        for side, ref in enumerate((first_ref, second_ref)):
+            moved = lax.dot_general(order, ref[rows, :], NN, preferred_element_type=jnp.float32)
+            moved = moved.astype(jnp.bfloat16)
+            for head in range(heads):
+                out_ref[head, rows, side * D_HEAD : (side + 1) * D_HEAD] = moved[
+                    :, head * D_HEAD : (head + 1) * D_HEAD
+                ]
+
+
+def split_heads(first, second):
+    rows = first.shape[0]
+    step = 4
+    return pl.pallas_call(
+        split_kernel,
+        grid=(HEADS // step,),
+        in_specs=[pl.BlockSpec((rows, step * D_HEAD), lambda g: (0, g))] * 2,
+        out_specs=pl.BlockSpec((step, rows, LANES), lambda g: (g, 0, 0)),
+        out_shape=jax.ShapeDtypeStruct((HEADS, rows, LANES), jnp.bfloat16),
+        compiler_params=pltpu.CompilerParams(vmem_limit_bytes=VMEM_BYTES),
+    )(first, second)
+
+
+def join_kernel(moved_ref, *out_refs):
+    order = row_order(True)
+    lines = order.shape[0]
+    for row in range(moved_ref.shape[1] // lines):
+        rows = slice(row * lines, (row + 1) * lines)
+        for head in range(moved_ref.shape[0]):
+            back = lax.dot_general(
+                order, moved_ref[head, rows, :], NN, preferred_element_type=jnp.float32
+            ).astype(jnp.bfloat16)
+            for side, ref in enumerate(out_refs):
+                ref[rows, head * D_HEAD : (head + 1) * D_HEAD] = back[
+                    :, side * D_HEAD : (side + 1) * D_HEAD
+                ]
+
+
+def join_heads(moved):
+    rows, lanes = moved.shape[1:]
+    count = lanes // D_HEAD
+    step = 4
+    return pl.pallas_call(
+        join_kernel,
+        grid=(HEADS // step,),
+        in_specs=[pl.BlockSpec((step, rows, lanes), lambda g: (g, 0, 0))],
+        out_specs=[pl.BlockSpec((rows, step * D_HEAD), lambda g: (0, g))] * count,
+        out_shape=[jax.ShapeDtypeStruct((rows, HEADS * D_HEAD), jnp.bfloat16)] * count,
+        compiler_params=pltpu.CompilerParams(vmem_limit_bytes=VMEM_BYTES),
+    )(moved)
+
+
+def grad_kernel(
+    side_ref, bias_ref, query_ref, kv_hbm, halo_hbm,
+    dq_ref, dkv_ref, edge_ref, halo_out_ref,
+    kv, acc, scores, low, sem,
+):
+    frames = kv.shape[1]
+    rows_own = kv.shape[0] - 2
+    cols = query_ref.shape[4] // TOK
+    key_cols = kv.shape[3] // TOK
+    side = side_ref[0]
+    halo_slot = jnp.where(side == 0, rows_own + 1, 0)
+    blank_slot = rows_own + 1 - halo_slot
+    copies = [
+        pltpu.make_async_copy(kv_hbm.at[:, :, row // 2, row % 2], kv.at[1 + row], sem.at[row])
+        for row in range(rows_own)
+    ]
+    copies.append(pltpu.make_async_copy(halo_hbm, kv.at[halo_slot], sem.at[rows_own]))
+    for copy in copies:
+        copy.start()
+    kv[blank_slot] = jnp.zeros(kv.shape[1:], kv.dtype)
+    acc[...] = jnp.zeros(acc.shape, acc.dtype)
+    for copy in copies:
+        copy.wait()
+    scale = D_HEAD**-0.5
+    part = frames * TILE * SPAN * TOK
+    piece = SPAN * TOK
+
+    def group(index, _):
+        row, col = index // cols, index % cols
+        start = pl.multiple_of(jnp.clip(col - 2, 0, key_cols - SPAN) * TOK, TOK)
+        here = pl.multiple_of(col * TOK, TOK)
+        own = query_ref[:, :, row // 2, row % 2, pl.ds(here, TOK), :].reshape(-1, LANES)
+        blank = jnp.zeros((own.shape[0], D_HEAD), own.dtype)
+        pair = jnp.concatenate(
+            [
+                jnp.concatenate([own[:, :D_HEAD], blank], axis=1),
+                jnp.concatenate([blank, own[:, D_HEAD:]], axis=1),
+            ],
+            axis=0,
+        )
+        top = None
+        for near in range(3):
+            keys = kv[row + near, :, :, pl.ds(start, piece), :].reshape(part, LANES)
+            both = lax.dot_general(keys, pair, NT, preferred_element_type=jnp.float32)
+            for frame in range(frames):
+                first = (near * frames + frame) * SPAN
+                bias = jnp.concatenate(
+                    [
+                        jnp.broadcast_to(bias_ref[index, first + c : first + c + 1, :], (TOK, D_HEAD))
+                        for c in range(SPAN)
+                    ],
+                    axis=0,
+                )
+                for sub in range(TILE):
+                    at = (frame * TILE + sub) * piece
+                    score = both[at : at + piece, :D_HEAD] * (scale * LOG2_E) + bias
+                    scores[near, at : at + piece, :D_HEAD] = score
+                    scores[near, at : at + piece, D_HEAD:] = both[at : at + piece, D_HEAD:]
+                    most = jnp.max(score.reshape(-1, 8, D_HEAD), axis=0)
+                    top = most if top is None else jnp.maximum(top, most)
+        top = jnp.max(top, axis=0, keepdims=True)
+        total = jnp.zeros((8, D_HEAD), jnp.float32)
+        delta = jnp.zeros((8, D_HEAD), jnp.float32)
+        for near in range(3):
+            for at in range(0, part, piece):
+                prob = jnp.exp2(scores[near, at : at + piece, :D_HEAD] - top)
+                scores[near, at : at + piece, :D_HEAD] = prob
+                total = total + jnp.sum(prob.reshape(-1, 8, D_HEAD), axis=0)
+                grad = prob * scores[near, at : at + piece, D_HEAD:]
+                delta = delta + jnp.sum(grad.reshape(-1, 8, D_HEAD), axis=0)
+        inverse = 1.0 / jnp.sum(total, axis=0, keepdims=True)
+        delta = jnp.sum(delta, axis=0, keepdims=True) * inverse
+        query_grad = None
+        for near in range(3):
+            for at in range(0, part, piece):
+                weight = scores[near, at : at + piece, :D_HEAD] * inverse
+                dscore = weight * (scores[near, at : at + piece, D_HEAD:] - delta)
+                low[at : at + piece, :D_HEAD] = dscore.astype(jnp.bfloat16)
+                low[at : at + piece, D_HEAD:] = weight.astype(jnp.bfloat16)
+            added = lax.dot_general(low[...], pair, NN, preferred_element_type=jnp.float32)
+            window = (row + near, slice(None), slice(None), pl.ds(start, piece), slice(None))
+            acc[window] = acc[window] + added.reshape(frames, TILE, piece, LANES)
+            keys = kv[row + near, :, :, pl.ds(start, piece), :].reshape(part, LANES)
+            more = lax.dot_general(
+                low[:, :D_HEAD], keys[:, :D_HEAD], TN, preferred_element_type=jnp.float32
+            )
+            query_grad = more if query_grad is None else query_grad + more
+        dq_ref[:, :, row // 2, row % 2, pl.ds(here, TOK), :] = (
+            (query_grad * scale).astype(jnp.bfloat16).reshape(frames, TILE, TOK, D_HEAD)
+        )
+        return 0
+
+    lax.fori_loop(0, rows_own * cols, group, 0)
+    lane = lax.broadcasted_iota(jnp.int32, (1, 1, 1, LANES), 3)
+    factor = jnp.where(lane < D_HEAD, scale, 1.0)
+    for row in range(rows_own):
+        dkv_ref[:, :, row // 2, row % 2] = (acc[1 + row] * factor).astype(jnp.bfloat16)
+    edge_ref[...] = acc[jnp.where(side == 0, rows_own, 1)] * factor
+    halo_out_ref[...] = (acc[halo_slot] * factor).astype(jnp.bfloat16)
+
+
+def window_bias(tile_valid, width_shift, side):
+    frames, tile_rows, cols = tile_valid.shape
+    row = (side * TH_DEV + jnp.arange(TH_DEV)).reshape(-1, 1, 1, 1, 1, 1)
+    col = jnp.arange(cols).reshape(1, -1, 1, 1, 1, 1)
+    near = jnp.arange(3).reshape(1, 1, -1, 1, 1, 1) - 1
+    key_frame = jnp.arange(frames).reshape(1, 1, 1, -1, 1, 1)
+    key_col = jnp.clip(col - 2, 0, cols - SPAN) + jnp.arange(SPAN).reshape(1, 1, 1, 1, -1, 1)
+    frame = jnp.arange(frames).reshape(1, 1, 1, 1, 1, -1)
+    shift_own = lax.dynamic_slice_in_dim(width_shift, side * TH_DEV, TH_DEV, 1)
+    shift_own = shift_own.transpose(1, 2, 0).reshape(TH_DEV, cols, 1, 1, 1, frames)
+    valid_near = lax.dynamic_slice_in_dim(
+        jnp.pad(tile_valid, ((0, 0), (1, 1), (0, 0))), side * TH_DEV, TH_DEV + 2, 1
+    )
+    valid_rows = jnp.stack([valid_near[:, n : n + TH_DEV] for n in range(3)])
+    starts = [min(max(c - 2, 0), cols - SPAN) for c in range(cols)]
+    valid_cols = jnp.stack([valid_rows[:, :, :, s : s + SPAN] for s in starts])
+    valid = valid_cols.transpose(3, 0, 1, 2, 4).reshape(TH_DEV, cols, 3, frames, SPAN, 1)
+    own = (near == 0) & (key_frame == frame) & (key_col == col)
+    inside = jnp.abs(key_col - col - shift_own) <= 1
+    there = (row + near >= 0) & (row + near < tile_rows)
+    bias = jnp.where(inside & there & ((valid == 1) | own), 0.0, MASKED_SCORE).astype(jnp.float32)
+    bias = bias.reshape(TH_DEV * cols, 3 * frames * SPAN, frames, 1)
+    bias = jnp.broadcast_to(bias, bias.shape[:3] + (TILE**3,))
+    return bias.reshape(TH_DEV * cols, 3 * frames * SPAN, frames * TILE**3)
+
+
+def head_shards(queries, key_states, value_states, out_grad, tile_valid, width_shift):
+    frames, _, cols = tile_valid.shape
+    group = ("tm", "seq")
+    side = lax.axis_index("height")
+    swap = [(0, 1), (1, 0)]
+    span = cols * TOK
+
+    def spread(first, second):
+        moved = lax.all_to_all(split_heads(first, second), group, 0, 0, tiled=True)
+        return moved.reshape(frames, TILE, 2, 2, span, LANES)
+
+    kv = spread(key_states, value_states)
+    edge = jnp.where(side == 0, kv[:, :, 1, 1], kv[:, :, 0, 0])
+    halo = lax.ppermute(edge, "height", swap)
+    query = spread(queries, out_grad)
+    bias = window_bias(tile_valid, width_shift, side)
+    part = frames * TILE * SPAN * TOK
+    whole = pl.BlockSpec(memory_space=pltpu.VMEM)
+    dq, dkv, edge_own, halo_grad = pl.pallas_call(
+        grad_kernel,
+        in_specs=[
+            pl.BlockSpec(memory_space=pltpu.SMEM),
+            whole,
+            whole,
+            pl.BlockSpec(memory_space=pl.ANY),
+            pl.BlockSpec(memory_space=pl.ANY),
+        ],
+        out_specs=[whole] * 4,
+        out_shape=[
+            jax.ShapeDtypeStruct((frames, TILE, 2, 2, span, D_HEAD), jnp.bfloat16),
+            jax.ShapeDtypeStruct((frames, TILE, 2, 2, span, LANES), jnp.bfloat16),
+            jax.ShapeDtypeStruct((frames, TILE, span, LANES), jnp.float32),
+            jax.ShapeDtypeStruct((frames, TILE, span, LANES), jnp.bfloat16),
+        ],
+        scratch_shapes=[
+            pltpu.VMEM((TH_DEV + 2, frames, TILE, span, LANES), jnp.bfloat16),
+            pltpu.VMEM((TH_DEV + 2, frames, TILE, span, LANES), jnp.float32),
+            pltpu.VMEM((3, part, LANES), jnp.float32),
+            pltpu.VMEM((part, LANES), jnp.bfloat16),
+            pltpu.SemaphoreType.DMA((TH_DEV + 1,)),
+        ],
+        compiler_params=pltpu.CompilerParams(vmem_limit_bytes=VMEM_BYTES),
+    )(side.reshape(1), bias, query, kv, halo)
+
+    def gather(grads):
+        lanes = grads.shape[-1]
+        moved = grads.reshape(HEADS, 2 * span, lanes)
+        return join_heads(lax.all_to_all(moved, group, 0, 0, tiled=True))
+
+    received = lax.ppermute(halo_grad, "height", swap)
+    (query_out,) = gather(dq)
+    edge_sum = (edge_own + received.astype(jnp.float32)).astype(jnp.bfloat16)[:, :, None, None]
+    dkv = lax.dynamic_update_slice(dkv, edge_sum, (0, 0, 1 - side, 1 - side, 0, 0))
+    key_out, value_out = gather(dkv)
+    return query_out, key_out, value_out
+
+
 def solution(mesh):
+    frames = mesh.shape["tm"]
+    tall = mesh.shape["height"] == 2 and frames == 2 and mesh.shape["seq"] == 2 * TILE
+    one_head = tall and frames * mesh.shape["seq"] == HEADS
     placed = (
         P(("tm", "height", "seq"), None),
         P(("tm", "height", "seq"), None),
@@ -283,7 +549,7 @@
         P(),
     )
     return jax.shard_map(
-        shards,
+        head_shards if one_head else shards,
         mesh=mesh,
         in_specs=placed,
         out_specs=(

time: 2470 us -> 474 us (0.19)
  local copies, waits for them, and re-layouts: 783 us -> 11.1 us
  other arithmetic: 750 us -> 5.96 us
  matrix products: 266 us -> 0 us
  waiting for transfers between devices: 477 us -> 296 us
  Pallas kernels: 0 us -> 137 us
  starting transfers between devices: 129 us -> 22.6 us
  loops' own time: 48.1 us -> 0 us
    scatter-add x12 -> x0, other arithmetic: 580 us -> none  [the longest x8 559 us: spread(): rows_now = rows_now.at[:, time_pick, row_pick, col_pick].add(shaped)]
    ppermute x20 -> x2, waiting for transfers between devices: 358 us -> 23.3 us  [the longest x1 23.3 us: head_shards(): received = lax.ppermute(halo_grad, 'height', swap)]
    dot_general x20 -> x0, matrix products: 266 us -> none  [the longest x4 61.4 us: query_row(): jnp.einsum('gwid,gwjd->gwij', grad_tiles, value_win, preferred_element_ty...]
    dynamic_slice x26 -> x0, local copies, waits for them, and re-layouts: 194 us -> none  [the longest x12 135 us: spread(): rows_now = lax.dynamic_slice_in_dim(acc_grid, row_index, 3, 2)]
    reshape x8 -> x2, local copies, waits for them, and re-layouts: 165 us -> 2.61 us  [window_bias(): return bias.reshape(TH_DEV * cols, 3 * frames * SPAN, frames * TILE ** 3)]
    all_to_all x7 -> x4, waiting for transfers between devices: 119 us -> 273 us  [the longest x2 165 us: spread(): moved = lax.all_to_all(split_heads(first, second), group, 0, 0, tiled=True)]
    pallas_call x0 -> x5, Pallas kernels: none -> 137 us  [the longest x1 115 us: head_shards(): pl.pallas_call(grad_kernel, in_specs=[pl.BlockSpec(memory_space=pltpu.SME...]
    transpose x17 -> x1, local copies, waits for them, and re-layouts: 97.4 us -> 0.01 us  [window_bias(): shift_own.transpose(1, 2, 0).reshape(TH_DEV, cols, 1, 1, 1, frames)]
  transfers between devices with their start and end apart: 27 -> 6, of which waited for: 15 -> 5; matrix products, arithmetic and copies ran while one was open for 7% -> 3% of each run, Pallas kernels for 0% -> 2%
where the time goes in v1:
time: 474 us; the launch traced here: 473 us
  waiting for transfers between devices  296 us (62%)
  Pallas kernels  137 us (29%)
  starting transfers between devices  22.6 us (5%)
  local copies, waits for them, and re-layouts  11.1 us (2%)
  other arithmetic  5.96 us (1%)
    all_to_all x2, waiting for transfers between devices, spread(): moved = lax.all_to_all(split_heads(first, second), group, 0, 0, tiled=True)  165 us
    pallas_call x1, Pallas kernels, head_shards(): pl.pallas_call(grad_kernel, in_specs=[pl.BlockSpec(memory_space=pltpu.SME...  115 us
    all_to_all x2, waiting for transfers between devices, gather(): return join_heads(lax.all_to_all(moved, group, 0, 0, tiled=True))  108 us
    ppermute x1, waiting for transfers between devices, head_shards(): received = lax.ppermute(halo_grad, 'height', swap)  23.3 us
    pallas_call x2, Pallas kernels, split_heads(): pl.pallas_call(split_kernel, grid=(HEADS // step,), in_specs=[pl.BlockSpe...  11.1 us
    all_to_all x2, starting transfers between devices, spread(): moved = lax.all_to_all(split_heads(first, second), group, 0, 0, tiled=True)  11.1 us
    pallas_call x2, Pallas kernels, join_heads(): pl.pallas_call(join_kernel, grid=(HEADS // step,), in_specs=[pl.BlockSpec...  10.1 us
  transfers between devices with their start and end apart: 6, of which 5 were waited for; matrix products, arithmetic and copies ran while one was open for 3% of the time, Pallas kernels for 2%

profile of v1, /device:TPU:9, one launch (start us, length us, event | category | flops | bytes accessed | tf_op | source)
XLA Modules:
  0.0 473.2 jit_solution(10292700146377416095)
XLA Ops:
  0.6 5.6 %shard_map.86 = bf16[16,512,256]{2,1,0:T(8,128)(2,1)} custom-call(bf16[512,2048]{1,0:T(8,128)(2,1)} %first_ref.3, bf16[512,2048]{1,0:T(8,128)(2,1)} %second_ref.3), custom_call_target="tpu_custom_call" | custom-call | tf_op jit(solution)/shard_map/pallas_call | solution.py:316
  6.2 6.6 %all-to-all-start.1 = ((bf16[16,512,256]{2,1,0:T(8,128)(2,1)}), bf16[16,512,256]{2,1,0:T(8,128)(2,1)}, u32[]{:S(2)}, u32[]{:S(2)}) async-start(bf16[16,512,256]{2,1,0:T(8,128)(2,1)} %shard_map.86), calls=%async_computation.1 | async-start | bytes 8388608 | tf_op jit(solution)/shard_map/all_to_all | solution.py:490
  12.8 5.5 %shard_map.85 = bf16[16,512,256]{2,1,0:T(8,128)(2,1)} custom-call(bf16[512,2048]{1,0:T(8,128)(2,1)} %first_ref.2, bf16[512,2048]{1,0:T(8,128)(2,1)} %second_ref.2), custom_call_target="tpu_custom_call" | custom-call | tf_op jit(solution)/shard_map/pallas_call | solution.py:316
  18.3 86.9 %all-to-all-done.1 = bf16[16,512,256]{2,1,0:T(8,128)(2,1)} async-done(((bf16[16,512,256]{2,1,0:T(8,128)(2,1)}), bf16[16,512,256]{2,1,0:T(8,128)(2,1)}, u32[]{:S(2)}, u32[]{:S(2)}) %all-to-all-start.1) | async-done | bytes 4194336 | tf_op jit(solution)/shard_map/all_to_all | solution.py:490
  105.2 4.5 all-to-all-start
  110.9 0.3 copy.24
  111.2 0.3 copy.25
  111.5 0.3 copy.26
  111.7 0.3 copy.27
  112.0 0.3 copy.28
  112.2 0.3 copy.29
  112.5 0.3 copy.30
  112.8 0.3 copy.31
  113.0 0.7 stack.71
  114.0 2.6 fusion.3
  116.6 1.2 collective-permute-start
  118.5 0.4 copy.34
  118.9 2.4 broadcast_in_dim.18
  121.3 1.1 reshape.222
  122.4 1.5 copy.37.bias_ref
  123.9 78.2 %all-to-all-done = bf16[16,512,256]{2,1,0:T(8,128)(2,1)} async-done(((bf16[16,512,256]{2,1,0:T(8,128)(2,1)}), bf16[16,512,256]{2,1,0:T(8,128)(2,1)}, u32[]{:S(2)}, u32[]{:S(2)}) %all-to-all-start) | async-done | bytes 4194336 | tf_op jit(solution)/shard_map/all_to_all | solution.py:490
  202.1 115.4 %shard_map.87 = (bf16[2,4,2,2,256,128]{5,4,3,2,1,0:T(8,128)(2,1)}, bf16[2,4,2,2,256,256]{5,4,3,2,1,0:T(8,128)(2,1)}, f32[2,4,256,256]{3,2,1,0:T(8,128)}, bf16[2,4,256,256]{3,2,1,0:T(8,128)(2,1)}) custom-call(s32[1]{0:T(128)} %bitcast.side_ref, f32[64,30,128]{2,1,0:T(8,128)} %copy.37.bias_ref, bf16[2,4,2,2,256,256]{5,4,3,2,1,0:T(8,128)(2,1)} %bitcast.18.query_ref, ...), custom_call_target="tpu_custom_call" | custom-call | tf_op jit(solution)/shard_map/pallas_call | solution.py:500
  317.5 4.5 all-to-all-start.2
  322.0 1.3 collective-permute-start.1
  323.3 23.3 %collective-permute-done.1 = bf16[2,4,256,256]{3,2,1,0:T(8,128)(2,1)S(1)} collective-permute-done((bf16[2,4,256,256]{3,2,1,0:T(8,128)(2,1)}, bf16[2,4,256,256]{3,2,1,0:T(8,128)(2,1)S(1)}, u32[]{:S(2)}, u32[]{:S(2)}) %collective-permute-start.1) | collective-permute-done | bytes 1048608 | tf_op jit(solution)/shard_map/ppermute | solution.py:531
  346.6 2.9 fusion.1
  349.5 19.8 %all-to-all-done.2.moved_ref = bf16[16,512,128]{2,1,0:T(8,128)(2,1)S(1)} async-done(((bf16[16,512,128]{2,1,0:T(8,128)(2,1)}), bf16[16,512,128]{2,1,0:T(8,128)(2,1)S(1)}, u32[]{:S(2)}, u32[]{:S(2)}) %all-to-all-start.2) | async-done | bytes 2097184 | tf_op jit(solution)/shard_map/all_to_all | solution.py:529
  369.4 1.3 copy-done.1
  370.7 4.5 all-to-all-start.3
  375.2 4.6 shard_map.88
  379.8 87.9 %all-to-all-done.3.moved_ref = bf16[16,512,256]{2,1,0:T(8,128)(2,1)} async-done(((bf16[16,512,256]{2,1,0:T(8,128)(2,1)}), bf16[16,512,256]{2,1,0:T(8,128)(2,1)}, u32[]{:S(2)}, u32[]{:S(2)}) %all-to-all-start.3) | async-done | bytes 4194336 | tf_op jit(solution)/shard_map/all_to_all | solution.py:529
  467.6 5.5 %shard_map.89 = (bf16[512,2048]{1,0:T(8,128)(2,1)}, bf16[512,2048]{1,0:T(8,128)(2,1)}) custom-call(bf16[16,512,256]{2,1,0:T(8,128)(2,1)} %all-to-all-done.3.moved_ref), custom_call_target="tpu_custom_call" | custom-call | tf_op jit(solution)/shard_map/pallas_call | solution.py:345
  (33 shorter events, 2.0 us)
Async XLA Ops:
  0.6 113.1 %copy-start = (s32[2,8,16]{2,1,0:T(8,128)S(1)}, s32[2,8,16]{2,1,0:T(8,128)}, u32[]{:S(2)}) copy-start(s32[2,8,16]{2,1,0:T(8,128)} %param.11) | copy-start | bytes 3076
  6.2 99.0 %all-to-all-start.1 = ((bf16[16,512,256]{2,1,0:T(8,128)(2,1)}), bf16[16,512,256]{2,1,0:T(8,128)(2,1)}, u32[]{:S(2)}, u32[]{:S(2)}) async-start(bf16[16,512,256]{2,1,0:T(8,128)(2,1)} %shard_map.86), calls=%async_computation.1 | async-start | bytes 8388608 | tf_op jit(solution)/shard_map/all_to_all | solution.py:490
  18.3 91.4 %copy-start.2 = (s32[2,8,16]{2,1,0:T(8,128)S(1)}, s32[2,8,16]{2,1,0:T(8,128)}, u32[]{:S(2)}) copy-start(s32[2,8,16]{2,1,0:T(8,128)} %param.10) | copy-start | bytes 3076
  105.2 96.9 %all-to-all-start = ((bf16[16,512,256]{2,1,0:T(8,128)(2,1)}), bf16[16,512,256]{2,1,0:T(8,128)(2,1)}, u32[]{:S(2)}, u32[]{:S(2)}) async-start(bf16[16,512,256]{2,1,0:T(8,128)(2,1)} %shard_map.85), calls=%async_computation | async-start | bytes 8388608 | tf_op jit(solution)/shard_map/all_to_all | solution.py:490
  116.6 85.5 %collective-permute-start = (bf16[2,4,256,256]{3,2,1,0:T(8,128)(2,1)}, bf16[2,4,256,256]{3,2,1,0:T(8,128)(2,1)}, u32[]{:S(2)}, u32[]{:S(2)}) collective-permute-start(bf16[2,4,256,256]{3,2,1,0:T(8,128)(2,1)} %fusion.3), channel_id=1, source_target_pairs={{0,8},{8,0},{1,9},{9,1},{2,10},{10,2},{3,11},{11,3},{4,12},{12,4},... | collective-permute-start | bytes 3145736 | tf_op jit(solution)/shard_map/ppermute | solution.py:495
  317.5 51.8 %all-to-all-start.2 = ((bf16[16,512,128]{2,1,0:T(8,128)(2,1)}), bf16[16,512,128]{2,1,0:T(8,128)(2,1)S(1)}, u32[]{:S(2)}, u32[]{:S(2)}) async-start(bf16[16,512,128]{2,1,0:T(8,128)(2,1)} %bitcast.66), calls=%async_computation.2 | async-start | bytes 4194304 | tf_op jit(solution)/shard_map/all_to_all | solution.py:529
  322.0 24.6 %collective-permute-start.1 = (bf16[2,4,256,256]{3,2,1,0:T(8,128)(2,1)}, bf16[2,4,256,256]{3,2,1,0:T(8,128)(2,1)S(1)}, u32[]{:S(2)}, u32[]{:S(2)}) collective-permute-start(bf16[2,4,256,256]{3,2,1,0:T(8,128)(2,1)} %get-tuple-element.12), channel_id=1, source_target_pairs={{0,8},{8,0},{1,9},{9,1},{2,10},{10,2},{3,11},{11,3},{4,12},{12,4},... | collective-permute-start | bytes 3145736 | tf_op jit(solution)/shard_map/ppermute | solution.py:531
  369.3 1.3 copy-start.1
  370.7 97.0 %all-to-all-start.3 = ((bf16[16,512,256]{2,1,0:T(8,128)(2,1)}), bf16[16,512,256]{2,1,0:T(8,128)(2,1)}, u32[]{:S(2)}, u32[]{:S(2)}) async-start(bf16[16,512,256]{2,1,0:T(8,128)(2,1)} %bitcast.65), calls=%async_computation.3 | async-start | bytes 8388608 | tf_op jit(solution)/shard_map/all_to_all | solution.py:529

commit v2 on v0

--- a/solution.py
+++ b/solution.py
@@ -3,6 +3,8 @@
 import jax
 import jax.numpy as jnp
 from jax import lax
+from jax.experimental import pallas as pl
+from jax.experimental.pallas import tpu as pltpu
 from jax.sharding import PartitionSpec as P
 
 D_HEAD = 128
@@ -273,7 +275,447 @@
     return (to_rows(returned[0]), to_rows(returned[1]), to_rows(returned[2]))
 
 
+TOK = TILE * TILE
+SPAN = 5
+LANES = 2 * D_HEAD
+LINES = TW * TOK
+LOG2_E = 1.4426950408889634
+VMEM_BYTES = 56 * 1024 * 1024
+NT = (((1,), (1,)), ((), ()))
+NN = (((1,), (0,)), ((), ()))
+TN = (((0,), (0,)), ((), ()))
+ANYWHERE = pl.BlockSpec(memory_space=pl.ANY)
+SCALARS = pl.BlockSpec(memory_space=pltpu.SMEM)
+WHOLE = pl.BlockSpec(memory_space=pltpu.VMEM)
+PARAMS = pltpu.CompilerParams(vmem_limit_bytes=VMEM_BYTES)
+
+
+def row_order(inverse):
+    target = lax.broadcasted_iota(jnp.int32, (LINES, LINES), 0)
+    source = lax.broadcasted_iota(jnp.int32, (LINES, LINES), 1)
+    if inverse:
+        target, source = source, target
+    col, line, x = target // TOK, (target // TILE) % TILE, target % TILE
+    return (source == line * (TW * TILE) + col * TILE + x).astype(jnp.bfloat16)
+
+
+def split_kernel(places, turn, place_ref, *refs):
+    arrays, outs = refs[:4], refs[4 : 4 + places]
+    taken, ready, in_sem, out_sem = refs[4 + places :]
+    turns = HEADS // places
+    loads = []
+    for k in range(places):
+        first = pl.multiple_of(((place_ref[0] ^ k) * turns + turn) * D_HEAD, D_HEAD)
+        loads.append(
+            [
+                pltpu.make_async_copy(
+                    ref.at[:, pl.ds(first, D_HEAD)], taken.at[k, which], in_sem.at[k, which]
+                )
+                for which, ref in enumerate(arrays)
+            ]
+        )
+        for copy in loads[k]:
+            copy.start()
+    order = row_order(False)
+    stores = []
+    for k in range(places):
+        for copy in loads[k]:
+            copy.wait()
+        for pair in range(2):
+            for row in range(2):
+                lines = slice(row * LINES, (row + 1) * LINES)
+                rows = jnp.concatenate(
+                    [taken[k, 2 * pair, lines, :], taken[k, 2 * pair + 1, lines, :]], axis=1
+                )
+                moved = lax.dot_general(order, rows, NN, preferred_element_type=jnp.float32)
+                ready[k, pair, row] = moved.astype(jnp.bfloat16)
+        stores.append(pltpu.make_async_copy(ready.at[k], outs[k], out_sem.at[k]))
+        stores[k].start()
+    for copy in stores:
+        copy.wait()
+
+
+def split_heads(places, turn, place, arrays):
+    rows = arrays[0].shape[0]
+    return pl.pallas_call(
+        lambda *refs: split_kernel(places, turn, *refs),
+        in_specs=[SCALARS] + [ANYWHERE] * 4,
+        out_specs=[ANYWHERE] * places,
+        out_shape=[jax.ShapeDtypeStruct((2, 2, LINES, LANES), jnp.bfloat16)] * places,
+        scratch_shapes=[
+            pltpu.VMEM((places, 4, rows, D_HEAD), jnp.bfloat16),
+            pltpu.VMEM((places, 2, 2, LINES, LANES), jnp.bfloat16),
+            pltpu.SemaphoreType.DMA((places, 4)),
+            pltpu.SemaphoreType.DMA((places,)),
+        ],
+        compiler_params=PARAMS,
+    )(place, *arrays)
+
+
+def join_kernel(places, turn, widths, kept, place_ref, *refs):
+    count = len(widths)
+    groups = [refs[n * places : (n + 1) * places] for n in range(count)]
+    refs = refs[count * places + kept :]
+    outs, taken, (ready, in_sem, out_sem) = refs[:3], refs[3 : 3 + count], refs[3 + count :]
+    turns = HEADS // places
+    loads = []
+    for k in range(places):
+        loads.append(
+            [
+                pltpu.make_async_copy(groups[n][k], taken[n].at[k], in_sem.at[k, n])
+                for n in range(count)
+            ]
+        )
+        for copy in loads[k]:
+            copy.start()
+    order = row_order(True)
+    stores = []
+    for k in range(places):
+        for copy in loads[k]:
+            copy.wait()
+        for row in range(2):
+            which = 0
+            for n in range(count):
+                back = lax.dot_general(
+                    order, taken[n][k, row], NN, preferred_element_type=jnp.float32
+                ).astype(jnp.bfloat16)
+                for lane in range(0, widths[n], D_HEAD):
+                    ready[k, which, row * LINES : (row + 1) * LINES, :] = back[
+                        :, lane : lane + D_HEAD
+                    ]
+                    which += 1
+        first = pl.multiple_of(((place_ref[0] ^ k) * turns + turn) * D_HEAD, D_HEAD)
+        for which in range(3):
+            copy = pltpu.make_async_copy(
+                ready.at[k, which], outs[which].at[:, pl.ds(first, D_HEAD)], out_sem.at[k, which]
+            )
+            copy.start()
+            stores.append(copy)
+    for copy in stores:
+        copy.wait()
+
+
+def join_heads(places, turn, place, groups, earlier):
+    rows = 2 * LINES
+    widths = [group[0].shape[-1] for group in groups]
+    count = len(widths)
+    return pl.pallas_call(
+        lambda *refs: join_kernel(places, turn, widths, len(earlier), *refs),
+        in_specs=[SCALARS] + [ANYWHERE] * (count * places + len(earlier)),
+        out_specs=[ANYWHERE] * 3,
+        out_shape=[jax.ShapeDtypeStruct((rows, HEADS * D_HEAD), jnp.bfloat16)] * 3,
+        scratch_shapes=[pltpu.VMEM((places, 2, LINES, width), jnp.bfloat16) for width in widths]
+        + [
+            pltpu.VMEM((places, 3, rows, D_HEAD), jnp.bfloat16),
+            pltpu.SemaphoreType.DMA((places, count)),
+            pltpu.SemaphoreType.DMA((places, 3)),
+        ],
+        input_output_aliases={1 + count * places + n: n for n in range(len(earlier))},
+        compiler_params=PARAMS,
+    )(place, *[block for group in groups for block in group], *earlier)
+
+
+def edge_kernel(places, *refs):
+    blocks, (first_ref, last_ref), sem = refs[:places], refs[places : places + 2], refs[-1]
+    copies = []
+    for k in range(places):
+        for row, ref in enumerate((first_ref, last_ref)):
+            copies.append(pltpu.make_async_copy(blocks[k].at[0, row], ref.at[k], sem.at[k, row]))
+    for copy in copies:
+        copy.start()
+    for copy in copies:
+        copy.wait()
+
+
+def edge_rows(places, blocks):
+    return pl.pallas_call(
+        lambda *refs: edge_kernel(places, *refs),
+        in_specs=[ANYWHERE] * places,
+        out_specs=[WHOLE] * 2,
+        out_shape=[jax.ShapeDtypeStruct((places, LINES, LANES), jnp.bfloat16)] * 2,
+        scratch_shapes=[pltpu.SemaphoreType.DMA((places, 2))],
+        compiler_params=PARAMS,
+    )(*blocks)
+
+
+def grad_kernel(places, place_ref, bias_ref, *refs):
+    blocks, (from_above, from_below) = refs[:places], refs[places : places + 2]
+    outs = refs[places + 2 :]
+    dq_refs, acc_out, above_ref, below_ref = outs[:places], *outs[places : places + 3]
+    kv, own_rows, acc, dq, scores, low, in_sem, halo_sem, out_sem = outs[places + 3 :]
+    frames = places // TILE
+    scale = D_HEAD**-0.5
+    copies = []
+    for k in range(places):
+        seat = place_ref[0] ^ k
+        spot = (seat // TILE, seat % TILE)
+        copies += [
+            pltpu.make_async_copy(blocks[k].at[0], kv.at[pl.ds(1, 2), *spot], in_sem.at[k, 0]),
+            pltpu.make_async_copy(blocks[k].at[1], own_rows.at[:, *spot], in_sem.at[k, 1]),
+            pltpu.make_async_copy(from_above.at[k], kv.at[0, *spot], halo_sem.at[k, 0]),
+            pltpu.make_async_copy(from_below.at[k], kv.at[3, *spot], halo_sem.at[k, 1]),
+        ]
+    for copy in copies:
+        copy.start()
+    acc[...] = jnp.zeros(acc.shape, acc.dtype)
+    for copy in copies:
+        copy.wait()
+    part = places * SPAN * TOK
+    piece = SPAN * TOK
+
+    def group(col, _):
+        start = pl.multiple_of(jnp.clip(col - 2, 0, TW - SPAN) * TOK, TOK)
+        here = pl.multiple_of(col * TOK, TOK)
+        window = pl.ds(start, piece)
+        pairs, tops = [], []
+        for row in range(2):
+            own = own_rows[row, :, :, pl.ds(here, TOK), :].reshape(-1, LANES)
+            blank = jnp.zeros((own.shape[0], D_HEAD), own.dtype)
+            pair = jnp.concatenate(
+                [
+                    jnp.concatenate([own[:, :D_HEAD], blank], axis=1),
+                    jnp.concatenate([blank, own[:, D_HEAD:]], axis=1),
+                ],
+                axis=0,
+            )
+            pairs.append(pair)
+            top = None
+            for near in range(3):
+                keys = kv[row + near, :, :, window, :].reshape(part, LANES)
+                both = lax.dot_general(keys, pair, NT, preferred_element_type=jnp.float32)
+                for frame in range(frames):
+                    first = (near * frames + frame) * SPAN
+                    bias = jnp.concatenate(
+                        [
+                            jnp.broadcast_to(
+                                bias_ref[row, col, first + c : first + c + 1, :], (TOK, D_HEAD)
+                            )
+                            for c in range(SPAN)
+                        ],
+                        axis=0,
+                    )
+                    for sub in range(TILE):
+                        at = (frame * TILE + sub) * piece
+                        score = both[at : at + piece, :D_HEAD] * (scale * LOG2_E) + bias
+                        scores[row, near, at : at + piece, :D_HEAD] = score
+                        scores[row, near, at : at + piece, D_HEAD:] = both[at : at + piece, D_HEAD:]
+                        most = jnp.max(score.reshape(-1, 8, D_HEAD), axis=0)
+                        top = most if top is None else jnp.maximum(top, most)
+            tops.append(jnp.max(top, axis=0, keepdims=True))
+        sums = []
+        for row in range(2):
+            total = jnp.zeros((8, D_HEAD), jnp.float32)
+            delta = jnp.zeros((8, D_HEAD), jnp.float32)
+            for near in range(3):
+                for at in range(0, part, piece):
+                    prob = jnp.exp2(scores[row, near, at : at + piece, :D_HEAD] - tops[row])
+                    scores[row, near, at : at + piece, :D_HEAD] = prob
+                    total = total + jnp.sum(prob.reshape(-1, 8, D_HEAD), axis=0)
+                    grad = prob * scores[row, near, at : at + piece, D_HEAD:]
+                    delta = delta + jnp.sum(grad.reshape(-1, 8, D_HEAD), axis=0)
+            inverse = 1.0 / jnp.sum(total, axis=0, keepdims=True)
+            sums.append((inverse, jnp.sum(delta, axis=0, keepdims=True) * inverse))
+        for row in range(2):
+            inverse, delta = sums[row]
+            query_grad = None
+            for near in range(3):
+                for at in range(0, part, piece):
+                    weight = scores[row, near, at : at + piece, :D_HEAD] * inverse
+                    dscore = weight * (scores[row, near, at : at + piece, D_HEAD:] - delta)
+                    low[row, near, at : at + piece, :D_HEAD] = dscore.astype(jnp.bfloat16)
+                    low[row, near, at : at + piece, D_HEAD:] = weight.astype(jnp.bfloat16)
+                added = lax.dot_general(
+                    low[row, near], pairs[row], NN, preferred_element_type=jnp.float32
+                )
+                spot = (row + near, slice(None), slice(None), window, slice(None))
+                acc[spot] = acc[spot] + added.reshape(frames, TILE, piece, LANES)
+                keys = kv[row + near, :, :, window, :D_HEAD].reshape(part, D_HEAD)
+                more = lax.dot_general(
+                    low[row, near, :, :D_HEAD], keys, TN, preferred_element_type=jnp.float32
+                )
+                query_grad = more if query_grad is None else query_grad + more
+            dq[row, :, :, pl.ds(here, TOK), :] = (
+                (query_grad * scale).astype(jnp.bfloat16).reshape(frames, TILE, TOK, D_HEAD)
+            )
+        return 0
+
+    lax.fori_loop(0, TW, group, 0)
+    copies = []
+    for k in range(places):
+        seat = place_ref[0] ^ k
+        spot = (seat // TILE, seat % TILE)
+        copies += [
+            pltpu.make_async_copy(dq.at[:, *spot], dq_refs[k], out_sem.at[k, 0]),
+            pltpu.make_async_copy(acc.at[pl.ds(1, 2), *spot], acc_out.at[k], out_sem.at[k, 1]),
+        ]
+    for copy in copies:
+        copy.start()
+    for k in range(places):
+        seat = place_ref[0] ^ k
+        spot = (seat // TILE, seat % TILE)
+        above_ref[k] = acc[0, *spot].astype(jnp.bfloat16)
+        below_ref[k] = acc[3, *spot].astype(jnp.bfloat16)
+    for copy in copies:
+        copy.wait()
+
+
+def head_grads(places, place, bias, blocks, from_above, from_below):
+    frames = places // TILE
+    part = places * SPAN * TOK
+    results = pl.pallas_call(
+        lambda *refs: grad_kernel(places, *refs),
+        in_specs=[SCALARS, WHOLE] + [ANYWHERE] * (places + 2),
+        out_specs=[ANYWHERE] * (places + 1) + [WHOLE] * 2,
+        out_shape=[jax.ShapeDtypeStruct((2, LINES, D_HEAD), jnp.bfloat16)] * places
+        + [jax.ShapeDtypeStruct((places, 2, LINES, LANES), jnp.float32)]
+        + [jax.ShapeDtypeStruct((places, LINES, LANES), jnp.bfloat16)] * 2,
+        scratch_shapes=[
+            pltpu.VMEM((4, frames, TILE, LINES, LANES), jnp.bfloat16),
+            pltpu.VMEM((2, frames, TILE, LINES, LANES), jnp.bfloat16),
+            pltpu.VMEM((4, frames, TILE, LINES, LANES), jnp.float32),
+            pltpu.VMEM((2, frames, TILE, LINES, D_HEAD), jnp.bfloat16),
+            pltpu.VMEM((2, 3, part, LANES), jnp.float32),
+            pltpu.VMEM((2, 3, part, LANES), jnp.bfloat16),
+            pltpu.SemaphoreType.DMA((places, 2)),
+            pltpu.SemaphoreType.DMA((places, 2)),
+            pltpu.SemaphoreType.DMA((places, 2)),
+        ],
+        compiler_params=PARAMS,
+        cost_estimate=pl.CostEstimate(
+            flops=60_000_000_000, bytes_accessed=0, transcendentals=0
+        ),
+    )(place, bias, *blocks, from_above, from_below)
+    return results[:places], *results[places:]
+
+
+def finish_kernel(places, acc_ref, above_ref, below_ref, *refs):
+    with_query = len(refs) > places
+    outs = refs[-places:]
+    lane = lax.broadcasted_iota(jnp.int32, (1, LANES), 1)
+    factor = jnp.where(lane < D_HEAD, D_HEAD**-0.5, 1.0)
+    for k in range(places):
+        for row, ref in enumerate((above_ref, below_ref)):
+            total = acc_ref[k, row] + ref[k].astype(jnp.float32)
+            outs[k][row, :, :LANES] = (total * factor).astype(jnp.bfloat16)
+        if with_query:
+            outs[k][:, :, LANES:] = refs[k][...]
+
+
+def finish_pairs(places, acc, above, below, query=()):
+    lanes = LANES + (D_HEAD if query else 0)
+    return pl.pallas_call(
+        lambda *refs: finish_kernel(places, *refs),
+        in_specs=[WHOLE] * (3 + len(query)),
+        out_specs=[WHOLE] * places,
+        out_shape=[jax.ShapeDtypeStruct((2, LINES, lanes), jnp.bfloat16)] * places,
+        compiler_params=PARAMS,
+    )(acc, above, below, *query)
+
+
+def window_bias(tile_valid, width_shift, first_row):
+    frames, tile_rows, cols = tile_valid.shape
+    row = (first_row + jnp.arange(2)).reshape(-1, 1, 1, 1, 1, 1)
+    col = jnp.arange(cols).reshape(1, -1, 1, 1, 1, 1)
+    near = jnp.arange(3).reshape(1, 1, -1, 1, 1, 1) - 1
+    key_frame = jnp.arange(frames).reshape(1, 1, 1, -1, 1, 1)
+    key_col = jnp.clip(col - 2, 0, cols - SPAN) + jnp.arange(SPAN).reshape(1, 1, 1, 1, -1, 1)
+    frame = jnp.arange(frames).reshape(1, 1, 1, 1, 1, -1)
+    shift_own = lax.dynamic_slice_in_dim(width_shift, first_row, 2, 1)
+    shift_own = shift_own.transpose(1, 2, 0).reshape(2, cols, 1, 1, 1, frames)
+    valid_near = lax.dynamic_slice_in_dim(
+        jnp.pad(tile_valid, ((0, 0), (1, 1), (0, 0))), first_row, 4, 1
+    )
+    valid_rows = jnp.stack([valid_near[:, n : n + 2] for n in range(3)])
+    starts = [min(max(c - 2, 0), cols - SPAN) for c in range(cols)]
+    valid_cols = jnp.stack([valid_rows[:, :, :, s : s + SPAN] for s in starts])
+    valid = valid_cols.transpose(3, 0, 1, 2, 4).reshape(2, cols, 3, frames, SPAN, 1)
+    own = (near == 0) & (key_frame == frame) & (key_col == col)
+    inside = jnp.abs(key_col - col - shift_own) <= 1
+    there = (row + near >= 0) & (row + near < tile_rows)
+    bias = jnp.where(inside & there & ((valid == 1) | own), 0.0, MASKED_SCORE).astype(jnp.float32)
+    bias = bias.reshape(2, cols, 3 * frames * SPAN, frames, 1)
+    bias = jnp.broadcast_to(bias, bias.shape[:4] + (TILE**3,))
+    return bias.reshape(2, cols, 3 * frames * SPAN, frames * TILE**3)
+
+
+def place_shards(queries, key_states, value_states, out_grad, tile_valid, width_shift):
+    frames = tile_valid.shape[0]
+    places = frames * TILE
+    turns = HEADS // places
+    seq_count = lax.axis_size("seq")
+    heights = lax.axis_size("height")
+    seq_index = lax.axis_index("seq")
+    place = (lax.axis_index("tm") * TILE + seq_index // 2).reshape(1)
+    first_row = lax.axis_index("height") * TH_DEV + seq_index % 2 * 2
+    bias = window_bias(tile_valid, width_shift, first_row)
+    chain = [
+        [h * seq_count + frame * 2 + half for h in range(heights) for half in range(2)]
+        for frame in range(TILE)
+    ]
+    down = [pair for line in chain for pair in zip(line[:-1], line[1:])]
+    up = [(b, a) for a, b in down]
+
+    def send(block, k):
+        return lax.ppermute(block, ("tm", "seq"), [(i, i ^ (2 * k)) for i in range(2 * places)])
+
+    def step(block, route):
+        return lax.ppermute(block, ("height", "seq"), route)
+
+    def exchange(blocks, order):
+        moved = dict(enumerate(blocks))
+        for k in order:
+            moved[k] = send(blocks[k], k)
+        return [moved[k] for k in range(places)]
+
+    natural = list(range(1, places))
+    far, near = [k for k in natural if k & 2], [k for k in natural if not k & 2]
+    held = [far[-1], near[0]]
+    mixed = far[:-1] + near[1:] + held
+
+    def after(blocks, results):
+        kept, results = lax.optimization_barrier(([blocks[k] for k in held], results))
+        blocks = list(blocks)
+        for k, block in zip(held, kept):
+            blocks[k] = block
+        return blocks, results
+
+    def ordered(first, then):
+        return lax.optimization_barrier((first, then))
+
+    def ordered(first, then):
+        return lax.optimization_barrier((first, then))
+
+    arrays = (key_states, value_states, queries, out_grad)
+    outs = ()
+    blocks = exchange(split_heads(places, 0, place, arrays), natural)
+    leaving = None
+    for turn in range(turns):
+        more = turn + 1 < turns
+        if more:
+            coming = split_heads(places, turn + 1, place, arrays)
+            blocks[1:6], coming = ordered(blocks[1:6], coming)
+        first, last = edge_rows(places, blocks)
+        grads = head_grads(places, place, bias, blocks, step(last, down), step(first, up))
+        if leaving is not None:
+            leaving, grads = after(leaving, grads)
+            left = exchange(leaving, mixed)
+            passed, grads = ordered([left[k] for k in mixed[:-2]], grads)
+            for k, block in zip(mixed, passed):
+                left[k] = block
+            outs = join_heads(places, turn - 1, place, [left], outs)
+        if more:
+            coming, grads = after(coming, grads)
+            blocks = exchange(coming, mixed)
+        dq, acc, above, below = grads
+        leaving = finish_pairs(places, acc, step(below, down), step(above, up), dq)
+    outs = join_heads(places, turns - 1, place, [exchange(leaving, natural)], outs)
+    key_out, value_out, query_out = outs
+    return query_out, key_out, value_out
+
+
 def solution(mesh):
+    frames, seq_count = mesh.shape["tm"], mesh.shape["seq"]
+    by_place = frames == 2 and seq_count == 2 * TILE
     placed = (
         P(("tm", "height", "seq"), None),
         P(("tm", "height", "seq"), None),
@@ -283,7 +725,7 @@
         P(),
     )
     return jax.shard_map(
-        shards,
+        place_shards if by_place else shards,
         mesh=mesh,
         in_specs=placed,
         out_specs=(

time: 2470 us -> 385 us (0.16)
  local copies, waits for them, and re-layouts: 783 us -> 11.6 us
  other arithmetic: 750 us -> 0.4 us
  waiting for transfers between devices: 477 us -> 176 us
  matrix products: 266 us -> 0 us
  Pallas kernels: 0 us -> 136 us
  starting transfers between devices: 129 us -> 57.9 us
  loops' own time: 48.1 us -> 0 us
    scatter-add x12 -> x0, other arithmetic: 580 us -> none  [the longest x8 559 us: spread(): rows_now = rows_now.at[:, time_pick, row_pick, col_pick].add(shaped)]
    dot_general x20 -> x0, matrix products: 266 us -> none  [the longest x4 61.4 us: query_row(): jnp.einsum('gwid,gwjd->gwij', grad_tiles, value_win, preferred_element_ty...]
    dynamic_slice x26 -> x0, local copies, waits for them, and re-layouts: 194 us -> none  [the longest x12 135 us: spread(): rows_now = lax.dynamic_slice_in_dim(acc_grid, row_index, 3, 2)]
    ppermute x20 -> x36, waiting for transfers between devices: 358 us -> 176 us  [the longest x28 156 us: send(): lax.ppermute(block, ('tm', 'seq'), [(i, i ^ 2 * k) for i in range(2 * pla...]
    reshape x8 -> x2, local copies, waits for them, and re-layouts: 165 us -> 1.54 us  [window_bias(): return bias.reshape(2, cols, 3 * frames * SPAN, frames * TILE ** 3)]
    pallas_call x0 -> x10, Pallas kernels: none -> 136 us  [the longest x2 102 us: head_grads(): pl.pallas_call(lambda *refs: grad_kernel(places, *refs), in_specs=[SCALAR...]
    all_to_all x7 -> x0, waiting for transfers between devices: 119 us -> none  [the longest x1 41.4 us: shards(): lax.all_to_all(to_heads(key_states), 'seq', split_axis=0, concat_axis=1,...]
    transpose x17 -> x2, local copies, waits for them, and re-layouts: 97.4 us -> 0.01 us  [window_bias(): shift_own = shift_own.transpose(1, 2, 0).reshape(2, cols, 1, 1, 1, frames)]
  transfers between devices with their start and end apart: 27 -> 36, of which waited for: 15 -> 17; matrix products, arithmetic and copies ran while one was open for 7% -> 2% of each run, Pallas kernels for 0% -> 32%
where the time goes in v2:
time: 385 us; the launch traced here: 384 us
  waiting for transfers between devices  176 us (46%)
  Pallas kernels  136 us (35%)
  starting transfers between devices  57.9 us (15%)
  local copies, waits for them, and re-layouts  11.6 us (3%)
    ppermute x28, waiting for transfers between devices, send(): lax.ppermute(block, ('tm', 'seq'), [(i, i ^ 2 * k) for i in range(2 * pla...  156 us
    pallas_call x2, Pallas kernels, head_grads(): pl.pallas_call(lambda *refs: grad_kernel(places, *refs), in_specs=[SCALAR...  102 us
    ppermute x28, starting transfers between devices, send(): lax.ppermute(block, ('tm', 'seq'), [(i, i ^ 2 * k) for i in range(2 * pla...  34.7 us
    ppermute x8, starting transfers between devices, step(): return lax.ppermute(block, ('height', 'seq'), route)  23.2 us
    ppermute x8, waiting for transfers between devices, step(): return lax.ppermute(block, ('height', 'seq'), route)  20.7 us
    pallas_call x2, Pallas kernels, finish_pairs(): pl.pallas_call(lambda *refs: finish_kernel(places, *refs), in_specs=[WHOL...  9.6 us
    pallas_call x2, Pallas kernels, split_heads(): pl.pallas_call(lambda *refs: split_kernel(places, turn, *refs), in_specs=...  9.56 us
    pallas_call x2, Pallas kernels, join_heads(): pl.pallas_call(lambda *refs: join_kernel(places, turn, widths, len(earlie...  8.79 us
  transfers between devices with their start and end apart: 36, of which 17 were waited for; matrix products, arithmetic and copies ran while one was open for 2% of the time, Pallas kernels for 32%

profile of v2, /device:TPU:9, one launch (start us, length us, event | category | flops | bytes accessed | tf_op | source)
XLA Modules:
  0.0 384.2 jit_solution(9266484799311100026)
XLA Ops:
  0.7 4.7 %shard_map.85 = (bf16[2,2,256,256]{3,2,1,0:T(8,128)(2,1)}, bf16[2,2,256,256]{3,2,1,0:T(8,128)(2,1)}, bf16[2,2,256,256]{3,2,1,0:T(8,128)(2,1)}, bf16[2,2,256,256]...) custom-call(s32[1]{0:T(128)} %bitcast.refs_0_, ...), custom_call_target="tpu_custom_call" | custom-call | tf_op jit(solution)/shard_map/pallas_call | solution.py:340
  5.5 2.5 collective-permute-start.1
  10.5 4.8 %shard_map.86 = (bf16[2,2,256,256]{3,2,1,0:T(8,128)(2,1)}, bf16[2,2,256,256]{3,2,1,0:T(8,128)(2,1)}, bf16[2,2,256,256]{3,2,1,0:T(8,128)(2,1)}, bf16[2,2,256,256]...) custom-call(s32[1]{0:T(128)} %bitcast.refs_0_, ...), custom_call_target="tpu_custom_call" | custom-call | tf_op jit(solution)/shard_map/pallas_call | solution.py:340
  15.5 11.7 %collective-permute-done.refs_1_.refs_3_ = bf16[2,2,256,256]{3,2,1,0:T(8,128)(2,1)S(1)} collective-permute-done((bf16[2,2,256,256]{3,2,1,0:T(8,128)(2,1)}, bf16[2,2,256,256]{3,2,1,0:T(8,128)(2,1)S(1)}, u32[]{:S(2)}, u32[]{:S(2)}) %collective-permute-start) | collective-permute-done | bytes 524320 | tf_op jit(solution)/shard_map/ppermute | solution.py:659
  27.2 4.5 %collective-permute-start.5 = (bf16[2,2,256,256]{3,2,1,0:T(8,128)(2,1)}, bf16[2,2,256,256]{3,2,1,0:T(8,128)(2,1)S(1)}, u32[]{:S(2)}, u32[]{:S(2)}) collective-permute-start(bf16[2,2,256,256]{3,2,1,0:T(8,128)(2,1)} %get-tuple-element.143), channel_id=1, source_target_pairs={{0,20},{1,21},{2,22},{3,23},{4,16},{5,17},{6,18},{7,19},{16,4},{17... | collective-permute-start | bytes 1572872 | tf_op jit(solution)/shard_map/ppermute | solution.py:659
  32.0 21.2 %collective-permute-done.2.refs_3_.refs_5_ = bf16[2,2,256,256]{3,2,1,0:T(8,128)(2,1)S(1)} collective-permute-done((bf16[2,2,256,256]{3,2,1,0:T(8,128)(2,1)}, bf16[2,2,256,256]{3,2,1,0:T(8,128)(2,1)S(1)}, u32[]{:S(2)}, u32[]{:S(2)}) %collective-permute-start.2) | collective-permute-done | bytes 524320 | tf_op jit(solution)/shard_map/ppermute | solution.py:659
  53.2 32.9 %collective-permute-done.5.refs_6_.refs_8_ = bf16[2,2,256,256]{3,2,1,0:T(8,128)(2,1)S(1)} collective-permute-done((bf16[2,2,256,256]{3,2,1,0:T(8,128)(2,1)}, bf16[2,2,256,256]{3,2,1,0:T(8,128)(2,1)S(1)}, u32[]{:S(2)}, u32[]{:S(2)}) %collective-permute-start.5) | collective-permute-done | bytes 524320 | tf_op jit(solution)/shard_map/ppermute | solution.py:659
  86.1 13.0 %collective-permute-done.6.refs_7_.refs_9_ = bf16[2,2,256,256]{3,2,1,0:T(8,128)(2,1)S(1)} collective-permute-done((bf16[2,2,256,256]{3,2,1,0:T(8,128)(2,1)S(1)}, bf16[2,2,256,256]{3,2,1,0:T(8,128)(2,1)S(1)}, u32[]{:S(2)}, u32[]{:S(2)}) %collective-permute-start.6) | collective-permute-done | bytes 524320 | tf_op jit(solution)/shard_map/ppermute | solution.py:659
  99.9 3.1 shard_map.87
  102.9 4.9 %collective-permute-start.7 = (bf16[8,256,256]{2,1,0:T(8,128)(2,1)}, bf16[8,256,256]{2,1,0:T(8,128)(2,1)S(1)}, u32[]{:S(2)}, u32[]{:S(2)}) collective-permute-start(bf16[8,256,256]{2,1,0:T(8,128)(2,1)} %get-tuple-element.145), channel_id=1, source_target_pairs={{0,1},{1,8},{8,9},{2,3},{3,10},{10,11},{4,5},{5,12},{12,13},{6,7},... | collective-permute-start | bytes 3145736 | tf_op jit(solution)/shard_map/ppermute | solution.py:662
  121.0 3.4 collective-permute-done.8.refs_11_
  124.4 51.2 %shard_map.88 = (bf16[2,256,128]{2,1,0:T(8,128)(2,1)}, bf16[2,256,128]{2,1,0:T(8,128)(2,1)}, bf16[2,256,128]{2,1,0:T(8,128)(2,1)}, bf16[2,256,128]{2,1,0:T(8,128...) custom-call(s32[1]{0:T(128)} %bitcast.refs_0_, ...), custom_call_target="tpu_custom_call" | custom-call | flops 60000002048 | tf_op jit(solution)/shard_map/pallas_call | solution.py:565
  175.6 2.5 collective-permute-start.16
  183.7 3.5 collective-permute-done.21.refs_6_.refs_8_
  187.2 18.7 %collective-permute-done.16.refs_1_.refs_3_ = bf16[2,2,256,256]{3,2,1,0:T(8,128)(2,1)S(1)} collective-permute-done((bf16[2,2,256,256]{3,2,1,0:T(8,128)(2,1)S(1)}, bf16[2,2,256,256]{3,2,1,0:T(8,128)(2,1)S(1)}, u32[]{:S(2)}, u32[]{:S(2)}) %collective-permute-start.16) | collective-permute-done | bytes 524320 | tf_op jit(solution)/shard_map/ppermute | solution.py:659
  207.5 3.0 shard_map.90
  210.6 5.3 %collective-permute-start.23 = (bf16[8,256,256]{2,1,0:T(8,128)(2,1)}, bf16[8,256,256]{2,1,0:T(8,128)(2,1)S(1)}, u32[]{:S(2)}, u32[]{:S(2)}) collective-permute-start(bf16[8,256,256]{2,1,0:T(8,128)(2,1)} %get-tuple-element.184), channel_id=1, source_target_pairs={{0,1},{1,8},{8,9},{2,3},{3,10},{10,11},{4,5},{5,12},{12,13},{6,7},... | collective-permute-start | bytes 3145736 | tf_op jit(solution)/shard_map/ppermute | solution.py:662
  220.0 4.8 %shard_map.89 = (bf16[2,256,384]{2,1,0:T(8,128)(2,1)}, bf16[2,256,384]{2,1,0:T(8,128)(2,1)}, bf16[2,256,384]{2,1,0:T(8,128)(2,1)}, bf16[2,256,384]{2,1,0:T(8,128...) custom-call(f32[8,2,256,256]{3,2,1,0:T(8,128)} %get-tuple-element.15, ...), custom_call_target="tpu_custom_call" | custom-call | tf_op jit(solution)/shard_map/pallas_call | solution.py:606
  230.1 2.4 collective-permute-done.24.refs_11_
  234.5 51.1 %shard_map.91 = (bf16[2,256,128]{2,1,0:T(8,128)(2,1)}, bf16[2,256,128]{2,1,0:T(8,128)(2,1)}, bf16[2,256,128]{2,1,0:T(8,128)(2,1)}, bf16[2,256,128]{2,1,0:T(8,128...) custom-call(s32[1]{0:T(128)} %bitcast.refs_0_, ...), custom_call_target="tpu_custom_call" | custom-call | flops 60000002048 | tf_op jit(solution)/shard_map/pallas_call | solution.py:565
  287.7 2.5 collective-permute-start.26
  291.5 8.2 %collective-permute-done.25.refs_1_ = bf16[8,256,256]{2,1,0:T(8,128)(2,1)S(1)} collective-permute-done((bf16[8,256,256]{2,1,0:T(8,128)(2,1)}, bf16[8,256,256]{2,1,0:T(8,128)(2,1)S(1)}, u32[]{:S(2)}, u32[]{:S(2)}) %collective-permute-start.25) | collective-permute-done | bytes 1048608 | tf_op jit(solution)/shard_map/ppermute | solution.py:662
  299.7 4.6 %collective-permute-done.26.refs_2_ = bf16[8,256,256]{2,1,0:T(8,128)(2,1)S(1)} collective-permute-done((bf16[8,256,256]{2,1,0:T(8,128)(2,1)}, bf16[8,256,256]{2,1,0:T(8,128)(2,1)S(1)}, u32[]{:S(2)}, u32[]{:S(2)}) %collective-permute-start.26) | collective-permute-done | bytes 1048608 | tf_op jit(solution)/shard_map/ppermute | solution.py:662
  305.2 4.8 %shard_map.92 = (bf16[2,256,384]{2,1,0:T(8,128)(2,1)}, bf16[2,256,384]{2,1,0:T(8,128)(2,1)}, bf16[2,256,384]{2,1,0:T(8,128)(2,1)}, bf16[2,256,384]{2,1,0:T(8,128...) custom-call(f32[8,2,256,256]{3,2,1,0:T(8,128)} %get-tuple-element.20, ...), custom_call_target="tpu_custom_call" | custom-call | tf_op jit(solution)/shard_map/pallas_call | solution.py:606
  315.7 11.1 %collective-permute-done.27.refs_2_ = bf16[2,256,384]{2,1,0:T(8,128)(2,1)S(1)} collective-permute-done((bf16[2,256,384]{2,1,0:T(8,128)(2,1)}, bf16[2,256,384]{2,1,0:T(8,128)(2,1)S(1)}, u32[]{:S(2)}, u32[]{:S(2)}) %collective-permute-start.27) | collective-permute-done | bytes 393248 | tf_op jit(solution)/shard_map/ppermute | solution.py:659
  326.8 2.5 collective-permute-start.32
  329.4 8.5 %collective-permute-done.28.refs_3_ = bf16[2,256,384]{2,1,0:T(8,128)(2,1)S(1)} collective-permute-done((bf16[2,256,384]{2,1,0:T(8,128)(2,1)}, bf16[2,256,384]{2,1,0:T(8,128)(2,1)S(1)}, u32[]{:S(2)}, u32[]{:S(2)}) %collective-permute-start.28) | collective-permute-done | bytes 393248 | tf_op jit(solution)/shard_map/ppermute | solution.py:659
  339.8 4.4 %shard_map.93 = (bf16[512,2048]{1,0:T(8,128)(2,1)}, bf16[512,2048]{1,0:T(8,128)(2,1)}, bf16[512,2048]{1,0:T(8,128)(2,1)}) custom-call(s32[1]{0:T(128)} %bitcast.refs_0_, bf16[2,256,384]{2,1,0:T(8,128)(2,1)} %get-tuple-element.227.refs_1_, bf16[2,256,384]{2,1,0:T(8,128)(2,1)} %copy-done.32, bf16[2,256,384]{2,1,0:T(8,128)(2,1)} %copy-done.27, ...), custom_call_target="tpu_custom_call" | custom-call | tf_op jit(solution)/shard_map/pallas_call | solution.py:402
  344.2 20.3 %collective-permute-done.29.refs_4_ = bf16[2,256,384]{2,1,0:T(8,128)(2,1)S(1)} collective-permute-done((bf16[2,256,384]{2,1,0:T(8,128)(2,1)}, bf16[2,256,384]{2,1,0:T(8,128)(2,1)S(1)}, u32[]{:S(2)}, u32[]{:S(2)}) %collective-permute-start.29) | collective-permute-done | bytes 393248 | tf_op jit(solution)/shard_map/ppermute | solution.py:659
  364.5 7.2 %collective-permute-done.32.refs_7_ = bf16[2,256,384]{2,1,0:T(8,128)(2,1)S(1)} collective-permute-done((bf16[2,256,384]{2,1,0:T(8,128)(2,1)}, bf16[2,256,384]{2,1,0:T(8,128)(2,1)S(1)}, u32[]{:S(2)}, u32[]{:S(2)}) %collective-permute-start.32) | collective-permute-done | bytes 393248 | tf_op jit(solution)/shard_map/ppermute | solution.py:659
  371.7 7.1 %collective-permute-done.33.refs_8_ = bf16[2,256,384]{2,1,0:T(8,128)(2,1)S(1)} collective-permute-done((bf16[2,256,384]{2,1,0:T(8,128)(2,1)}, bf16[2,256,384]{2,1,0:T(8,128)(2,1)S(1)}, u32[]{:S(2)}, u32[]{:S(2)}) %collective-permute-start.33) | collective-permute-done | bytes 393248 | tf_op jit(solution)/shard_map/ppermute | solution.py:659
  379.6 4.4 %shard_map.94 = (bf16[512,2048]{1,0:T(8,128)(2,1)}, bf16[512,2048]{1,0:T(8,128)(2,1)}, bf16[512,2048]{1,0:T(8,128)(2,1)}) custom-call(s32[1]{0:T(128)} %bitcast.refs_0_, bf16[2,256,384]{2,1,0:T(8,128)(2,1)} %get-tuple-element.219.refs_1_, bf16[2,256,384]{2,1,0:T(8,128)(2,1)} %copy-done.20, ...), custom_call_target="tpu_custom_call", output_to_operand_aliasing={{0}: (9, {}), {1}: (10, {}), {2}: (11, {})} | custom-call | tf_op jit(solution)/shard_map/pallas_call | solution.py:402
  (181 shorter events, 48.1 us)
Async XLA Ops:
  5.4 21.8 %collective-permute-start = (bf16[2,2,256,256]{3,2,1,0:T(8,128)(2,1)}, bf16[2,2,256,256]{3,2,1,0:T(8,128)(2,1)S(1)}, u32[]{:S(2)}, u32[]{:S(2)}) collective-permute-start(bf16[2,2,256,256]{3,2,1,0:T(8,128)(2,1)} %get-tuple-element.122), channel_id=1, source_target_pairs={{0,2},{1,3},{2,0},{3,1},{4,6},{5,7},{6,4},{7,5},{16,18},{17,19},{1... | collective-permute-start | bytes 1572872 | tf_op jit(solution)/shard_map/ppermute | solution.py:659
  5.5 26.1 %collective-permute-start.1 = (bf16[2,2,256,256]{3,2,1,0:T(8,128)(2,1)}, bf16[2,2,256,256]{3,2,1,0:T(8,128)(2,1)S(1)}, u32[]{:S(2)}, u32[]{:S(2)}) collective-permute-start(bf16[2,2,256,256]{3,2,1,0:T(8,128)(2,1)} %get-tuple-element.123), channel_id=1, source_target_pairs={{0,4},{1,5},{2,6},{3,7},{4,0},{5,1},{6,2},{7,3},{16,20},{17,21},{1... | collective-permute-start | bytes 1572872 | tf_op jit(solution)/shard_map/ppermute | solution.py:659
  8.0 45.2 %collective-permute-start.2 = (bf16[2,2,256,256]{3,2,1,0:T(8,128)(2,1)}, bf16[2,2,256,256]{3,2,1,0:T(8,128)(2,1)S(1)}, u32[]{:S(2)}, u32[]{:S(2)}) collective-permute-start(bf16[2,2,256,256]{3,2,1,0:T(8,128)(2,1)} %get-tuple-element.124), channel_id=1, source_target_pairs={{0,6},{1,7},{2,4},{3,5},{4,2},{5,3},{6,0},{7,1},{16,22},{17,23},{1... | collective-permute-start | bytes 1572872 | tf_op jit(solution)/shard_map/ppermute | solution.py:659
  8.1 45.1 %collective-permute-start.3 = (bf16[2,2,256,256]{3,2,1,0:T(8,128)(2,1)}, bf16[2,2,256,256]{3,2,1,0:T(8,128)(2,1)S(1)}, u32[]{:S(2)}, u32[]{:S(2)}) collective-permute-start(bf16[2,2,256,256]{3,2,1,0:T(8,128)(2,1)} %get-tuple-element.125), channel_id=1, source_target_pairs={{0,16},{1,17},{2,18},{3,19},{4,20},{5,21},{6,22},{7,23},{16,0},{17... | collective-permute-start | bytes 1572872 | tf_op jit(solution)/shard_map/ppermute | solution.py:659
  9.3 43.9 %collective-permute-start.4 = (bf16[2,2,256,256]{3,2,1,0:T(8,128)(2,1)}, bf16[2,2,256,256]{3,2,1,0:T(8,128)(2,1)S(1)}, u32[]{:S(2)}, u32[]{:S(2)}) collective-permute-start(bf16[2,2,256,256]{3,2,1,0:T(8,128)(2,1)} %get-tuple-element.126), channel_id=1, source_target_pairs={{0,18},{1,19},{2,16},{3,17},{4,22},{5,23},{6,20},{7,21},{16,2},{17... | collective-permute-start | bytes 1572872 | tf_op jit(solution)/shard_map/ppermute | solution.py:659
  27.2 58.9 %collective-permute-start.5 = (bf16[2,2,256,256]{3,2,1,0:T(8,128)(2,1)}, bf16[2,2,256,256]{3,2,1,0:T(8,128)(2,1)S(1)}, u32[]{:S(2)}, u32[]{:S(2)}) collective-permute-start(bf16[2,2,256,256]{3,2,1,0:T(8,128)(2,1)} %get-tuple-element.143), channel_id=1, source_target_pairs={{0,20},{1,21},{2,22},{3,23},{4,16},{5,17},{6,18},{7,19},{16,4},{17... | collective-permute-start | bytes 1572872 | tf_op jit(solution)/shard_map/ppermute | solution.py:659
  31.6 67.4 %collective-permute-start.6 = (bf16[2,2,256,256]{3,2,1,0:T(8,128)(2,1)S(1)}, bf16[2,2,256,256]{3,2,1,0:T(8,128)(2,1)S(1)}, u32[]{:S(2)}, u32[]{:S(2)}) collective-permute-start(bf16[2,2,256,256]{3,2,1,0:T(8,128)(2,1)S(1)} %copy-done.41), channel_id=1, source_target_pairs={{0,22},{1,23},{2,20},{3,21},{4,18},{5,19},{6,16},{7,17},{16,6},{17... | collective-permute-start | bytes 1572872 | tf_op jit(solution)/shard_map/ppermute | solution.py:659
  102.9 16.9 %collective-permute-start.7 = (bf16[8,256,256]{2,1,0:T(8,128)(2,1)}, bf16[8,256,256]{2,1,0:T(8,128)(2,1)S(1)}, u32[]{:S(2)}, u32[]{:S(2)}) collective-permute-start(bf16[8,256,256]{2,1,0:T(8,128)(2,1)} %get-tuple-element.145), channel_id=1, source_target_pairs={{0,1},{1,8},{8,9},{2,3},{3,10},{10,11},{4,5},{5,12},{12,13},{6,7},... | collective-permute-start | bytes 3145736 | tf_op jit(solution)/shard_map/ppermute | solution.py:662
  116.2 59.4 %collective-permute-start.17 = (bf16[2,2,256,256]{3,2,1,0:T(8,128)(2,1)}, bf16[2,2,256,256]{3,2,1,0:T(8,128)(2,1)S(1)}, u32[]{:S(2)}, u32[]{:S(2)}) collective-permute-start(bf16[2,2,256,256]{3,2,1,0:T(8,128)(2,1)} %get-tuple-element.178), channel_id=1, source_target_pairs={{0,4},{1,5},{2,6},{3,7},{4,0},{5,1},{6,2},{7,3},{16,20},{17,21},{1... | collective-permute-start | bytes 1572872 | tf_op jit(solution)/shard_map/ppermute | solution.py:659
  116.2 61.9 %collective-permute-start.18 = (bf16[2,2,256,256]{3,2,1,0:T(8,128)(2,1)}, bf16[2,2,256,256]{3,2,1,0:T(8,128)(2,1)S(1)}, u32[]{:S(2)}, u32[]{:S(2)}) collective-permute-start(bf16[2,2,256,256]{3,2,1,0:T(8,128)(2,1)} %get-tuple-element.179), channel_id=1, source_target_pairs={{0,6},{1,7},{2,4},{3,5},{4,2},{5,3},{6,0},{7,1},{16,22},{17,23},{1... | collective-permute-start | bytes 1572872 | tf_op jit(solution)/shard_map/ppermute | solution.py:659
  117.5 61.7 %collective-permute-start.19 = (bf16[2,2,256,256]{3,2,1,0:T(8,128)(2,1)}, bf16[2,2,256,256]{3,2,1,0:T(8,128)(2,1)S(1)}, u32[]{:S(2)}, u32[]{:S(2)}) collective-permute-start(bf16[2,2,256,256]{3,2,1,0:T(8,128)(2,1)} %get-tuple-element.180), channel_id=1, source_target_pairs={{0,16},{1,17},{2,18},{3,19},{4,20},{5,21},{6,22},{7,23},{16,0},{17... | collective-permute-start | bytes 1572872 | tf_op jit(solution)/shard_map/ppermute | solution.py:659
  119.8 61.9 %collective-permute-start.20 = (bf16[2,2,256,256]{3,2,1,0:T(8,128)(2,1)}, bf16[2,2,256,256]{3,2,1,0:T(8,128)(2,1)S(1)}, u32[]{:S(2)}, u32[]{:S(2)}) collective-permute-start(bf16[2,2,256,256]{3,2,1,0:T(8,128)(2,1)} %get-tuple-element.181), channel_id=1, source_target_pairs={{0,18},{1,19},{2,16},{3,17},{4,22},{5,23},{6,20},{7,21},{16,2},{17... | collective-permute-start | bytes 1572872 | tf_op jit(solution)/shard_map/ppermute | solution.py:659
  124.4 62.7 %collective-permute-start.21 = (bf16[2,2,256,256]{3,2,1,0:T(8,128)(2,1)S(1)}, bf16[2,2,256,256]{3,2,1,0:T(8,128)(2,1)S(1)}, u32[]{:S(2)}, u32[]{:S(2)}) collective-permute-start(bf16[2,2,256,256]{3,2,1,0:T(8,128)(2,1)S(1)} %copy-done.40), channel_id=1, source_target_pairs={{0,20},{1,21},{2,22},{3,23},{4,16},{5,17},{6,18},{7,19},{16,4},{17... | collective-permute-start | bytes 1572872 | tf_op jit(solution)/shard_map/ppermute | solution.py:659
  175.6 30.2 %collective-permute-start.16 = (bf16[2,2,256,256]{3,2,1,0:T(8,128)(2,1)S(1)}, bf16[2,2,256,256]{3,2,1,0:T(8,128)(2,1)S(1)}, u32[]{:S(2)}, u32[]{:S(2)}) collective-permute-start(bf16[2,2,256,256]{3,2,1,0:T(8,128)(2,1)S(1)} %copy-done.39), channel_id=1, source_target_pairs={{0,2},{1,3},{2,0},{3,1},{4,6},{5,7},{6,4},{7,5},{16,18},{17,19},{1... | collective-permute-start | bytes 1572872 | tf_op jit(solution)/shard_map/ppermute | solution.py:659
  178.1 28.4 %collective-permute-start.22 = (bf16[2,2,256,256]{3,2,1,0:T(8,128)(2,1)S(1)}, bf16[2,2,256,256]{3,2,1,0:T(8,128)(2,1)S(1)}, u32[]{:S(2)}, u32[]{:S(2)}) collective-permute-start(bf16[2,2,256,256]{3,2,1,0:T(8,128)(2,1)S(1)} %copy-done.38), channel_id=1, source_target_pairs={{0,22},{1,23},{2,20},{3,21},{4,18},{5,19},{6,16},{7,17},{16,6},{17... | collective-permute-start | bytes 1572872 | tf_op jit(solution)/shard_map/ppermute | solution.py:659
  179.3 38.8 %collective-permute-start.9 = (bf16[8,256,256]{2,1,0:T(8,128)(2,1)}, bf16[8,256,256]{2,1,0:T(8,128)(2,1)S(1)}, u32[]{:S(2)}, u32[]{:S(2)}) collective-permute-start(bf16[8,256,256]{2,1,0:T(8,128)(2,1)} %get-tuple-element.159), channel_id=1, source_target_pairs={{0,1},{1,8},{8,9},{2,3},{3,10},{10,11},{4,5},{5,12},{12,13},{6,7},... | collective-permute-start | bytes 3145736 | tf_op jit(solution)/shard_map/ppermute | solution.py:662
  181.7 36.4 %collective-permute-start.10 = (bf16[8,256,256]{2,1,0:T(8,128)(2,1)}, bf16[8,256,256]{2,1,0:T(8,128)(2,1)S(1)}, u32[]{:S(2)}, u32[]{:S(2)}) collective-permute-start(bf16[8,256,256]{2,1,0:T(8,128)(2,1)} %get-tuple-element.160), channel_id=1, source_target_pairs={{1,0},{8,1},{9,8},{3,2},{10,3},{11,10},{5,4},{12,5},{13,12},{7,6},... | collective-permute-start | bytes 3145736 | tf_op jit(solution)/shard_map/ppermute | solution.py:662
  210.6 18.6 %collective-permute-start.23 = (bf16[8,256,256]{2,1,0:T(8,128)(2,1)}, bf16[8,256,256]{2,1,0:T(8,128)(2,1)S(1)}, u32[]{:S(2)}, u32[]{:S(2)}) collective-permute-start(bf16[8,256,256]{2,1,0:T(8,128)(2,1)} %get-tuple-element.184), channel_id=1, source_target_pairs={{0,1},{1,8},{8,9},{2,3},{3,10},{10,11},{4,5},{5,12},{12,13},{6,7},... | collective-permute-start | bytes 3145736 | tf_op jit(solution)/shard_map/ppermute | solution.py:662
  224.8 60.8 %collective-permute-start.11 = (bf16[2,256,384]{2,1,0:T(8,128)(2,1)}, bf16[2,256,384]{2,1,0:T(8,128)(2,1)S(1)}, u32[]{:S(2)}, u32[]{:S(2)}) collective-permute-start(bf16[2,256,384]{2,1,0:T(8,128)(2,1)} %get-tuple-element.169), channel_id=1, source_target_pairs={{0,4},{1,5},{2,6},{3,7},{4,0},{5,1},{6,2},{7,3},{16,20},{17,21},{1... | collective-permute-start | bytes 1179656 | tf_op jit(solution)/shard_map/ppermute | solution.py:659
  226.7 59.0 %collective-permute-start.12 = (bf16[2,256,384]{2,1,0:T(8,128)(2,1)}, bf16[2,256,384]{2,1,0:T(8,128)(2,1)S(1)}, u32[]{:S(2)}, u32[]{:S(2)}) collective-permute-start(bf16[2,256,384]{2,1,0:T(8,128)(2,1)} %get-tuple-element.170), channel_id=1, source_target_pairs={{0,6},{1,7},{2,4},{3,5},{4,2},{5,3},{6,0},{7,1},{16,22},{17,23},{1... | collective-permute-start | bytes 1179656 | tf_op jit(solution)/shard_map/ppermute | solution.py:659
  228.0 57.7 %collective-permute-start.13 = (bf16[2,256,384]{2,1,0:T(8,128)(2,1)}, bf16[2,256,384]{2,1,0:T(8,128)(2,1)S(1)}, u32[]{:S(2)}, u32[]{:S(2)}) collective-permute-start(bf16[2,256,384]{2,1,0:T(8,128)(2,1)} %get-tuple-element.171), channel_id=1, source_target_pairs={{0,20},{1,21},{2,22},{3,23},{4,16},{5,17},{6,18},{7,19},{16,4},{17... | collective-permute-start | bytes 1179656 | tf_op jit(solution)/shard_map/ppermute | solution.py:659
  229.2 56.5 %collective-permute-start.14 = (bf16[2,256,384]{2,1,0:T(8,128)(2,1)}, bf16[2,256,384]{2,1,0:T(8,128)(2,1)S(1)}, u32[]{:S(2)}, u32[]{:S(2)}) collective-permute-start(bf16[2,256,384]{2,1,0:T(8,128)(2,1)} %get-tuple-element.172), channel_id=1, source_target_pairs={{0,16},{1,17},{2,18},{3,19},{4,20},{5,21},{6,22},{7,23},{16,0},{17... | collective-permute-start | bytes 1179656 | tf_op jit(solution)/shard_map/ppermute | solution.py:659
  232.5 53.2 %collective-permute-start.15 = (bf16[2,256,384]{2,1,0:T(8,128)(2,1)}, bf16[2,256,384]{2,1,0:T(8,128)(2,1)S(1)}, u32[]{:S(2)}, u32[]{:S(2)}) collective-permute-start(bf16[2,256,384]{2,1,0:T(8,128)(2,1)} %get-tuple-element.173), channel_id=1, source_target_pairs={{0,18},{1,19},{2,16},{3,17},{4,22},{5,23},{6,20},{7,21},{16,2},{17... | collective-permute-start | bytes 1179656 | tf_op jit(solution)/shard_map/ppermute | solution.py:659
  290.1 22.5 %collective-permute-start.34 = (bf16[2,256,384]{2,1,0:T(8,128)(2,1)S(1)}, bf16[2,256,384]{2,1,0:T(8,128)(2,1)S(1)}, u32[]{:S(2)}, u32[]{:S(2)}) collective-permute-start(bf16[2,256,384]{2,1,0:T(8,128)(2,1)S(1)} %copy-done.43), channel_id=1, source_target_pairs={{0,2},{1,3},{2,0},{3,1},{4,6},{5,7},{6,4},{7,5},{16,18},{17,19},{1... | collective-permute-start | bytes 1179656 | tf_op jit(solution)/shard_map/ppermute | solution.py:659
  291.1 22.7 %collective-permute-start.35 = (bf16[2,256,384]{2,1,0:T(8,128)(2,1)S(1)}, bf16[2,256,384]{2,1,0:T(8,128)(2,1)S(1)}, u32[]{:S(2)}, u32[]{:S(2)}) collective-permute-start(bf16[2,256,384]{2,1,0:T(8,128)(2,1)S(1)} %copy-done.42), channel_id=1, source_target_pairs={{0,22},{1,23},{2,20},{3,21},{4,18},{5,19},{6,16},{7,17},{16,6},{17... | collective-permute-start | bytes 1179656 | tf_op jit(solution)/shard_map/ppermute | solution.py:659
  310.0 16.8 %collective-permute-start.27 = (bf16[2,256,384]{2,1,0:T(8,128)(2,1)}, bf16[2,256,384]{2,1,0:T(8,128)(2,1)S(1)}, u32[]{:S(2)}, u32[]{:S(2)}) collective-permute-start(bf16[2,256,384]{2,1,0:T(8,128)(2,1)} %get-tuple-element.220), channel_id=1, source_target_pairs={{0,2},{1,3},{2,0},{3,1},{4,6},{5,7},{6,4},{7,5},{16,18},{17,19},{1... | collective-permute-start | bytes 1179656 | tf_op jit(solution)/shard_map/ppermute | solution.py:659
  311.0 26.9 %collective-permute-start.28 = (bf16[2,256,384]{2,1,0:T(8,128)(2,1)}, bf16[2,256,384]{2,1,0:T(8,128)(2,1)S(1)}, u32[]{:S(2)}, u32[]{:S(2)}) collective-permute-start(bf16[2,256,384]{2,1,0:T(8,128)(2,1)} %get-tuple-element.221), channel_id=1, source_target_pairs={{0,4},{1,5},{2,6},{3,7},{4,0},{5,1},{6,2},{7,3},{16,20},{17,21},{1... | collective-permute-start | bytes 1179656 | tf_op jit(solution)/shard_map/ppermute | solution.py:659
  311.8 52.7 %collective-permute-start.29 = (bf16[2,256,384]{2,1,0:T(8,128)(2,1)}, bf16[2,256,384]{2,1,0:T(8,128)(2,1)S(1)}, u32[]{:S(2)}, u32[]{:S(2)}) collective-permute-start(bf16[2,256,384]{2,1,0:T(8,128)(2,1)} %get-tuple-element.222), channel_id=1, source_target_pairs={{0,6},{1,7},{2,4},{3,5},{4,2},{5,3},{6,0},{7,1},{16,22},{17,23},{1... | collective-permute-start | bytes 1179656 | tf_op jit(solution)/shard_map/ppermute | solution.py:659
  312.7 51.8 %collective-permute-start.30 = (bf16[2,256,384]{2,1,0:T(8,128)(2,1)}, bf16[2,256,384]{2,1,0:T(8,128)(2,1)S(1)}, u32[]{:S(2)}, u32[]{:S(2)}) collective-permute-start(bf16[2,256,384]{2,1,0:T(8,128)(2,1)} %get-tuple-element.223), channel_id=1, source_target_pairs={{0,16},{1,17},{2,18},{3,19},{4,20},{5,21},{6,22},{7,23},{16,0},{17... | collective-permute-start | bytes 1179656 | tf_op jit(solution)/shard_map/ppermute | solution.py:659
  313.8 50.7 %collective-permute-start.31 = (bf16[2,256,384]{2,1,0:T(8,128)(2,1)}, bf16[2,256,384]{2,1,0:T(8,128)(2,1)S(1)}, u32[]{:S(2)}, u32[]{:S(2)}) collective-permute-start(bf16[2,256,384]{2,1,0:T(8,128)(2,1)} %get-tuple-element.224), channel_id=1, source_target_pairs={{0,18},{1,19},{2,16},{3,17},{4,22},{5,23},{6,20},{7,21},{16,2},{17... | collective-permute-start | bytes 1179656 | tf_op jit(solution)/shard_map/ppermute | solution.py:659
  326.8 44.8 %collective-permute-start.32 = (bf16[2,256,384]{2,1,0:T(8,128)(2,1)}, bf16[2,256,384]{2,1,0:T(8,128)(2,1)S(1)}, u32[]{:S(2)}, u32[]{:S(2)}) collective-permute-start(bf16[2,256,384]{2,1,0:T(8,128)(2,1)} %get-tuple-element.225), channel_id=1, source_target_pairs={{0,20},{1,21},{2,22},{3,23},{4,16},{5,17},{6,18},{7,19},{16,4},{17... | collective-permute-start | bytes 1179656 | tf_op jit(solution)/shard_map/ppermute | solution.py:659
  337.8 41.0 %collective-permute-start.33 = (bf16[2,256,384]{2,1,0:T(8,128)(2,1)}, bf16[2,256,384]{2,1,0:T(8,128)(2,1)S(1)}, u32[]{:S(2)}, u32[]{:S(2)}) collective-permute-start(bf16[2,256,384]{2,1,0:T(8,128)(2,1)} %get-tuple-element.226), channel_id=1, source_target_pairs={{0,22},{1,23},{2,20},{3,21},{4,18},{5,19},{6,16},{7,17},{16,6},{17... | collective-permute-start | bytes 1179656 | tf_op jit(solution)/shard_map/ppermute | solution.py:659
  (48 other events, 1288.9 us)

commit v3 on v2

--- a/solution.py
+++ b/solution.py
@@ -276,7 +276,7 @@
 
 
 TOK = TILE * TILE
-SPAN = 5
+SPAN = 3
 LANES = 2 * D_HEAD
 LINES = TW * TOK
 LOG2_E = 1.4426950408889634
@@ -299,9 +299,9 @@
     return (source == line * (TW * TILE) + col * TILE + x).astype(jnp.bfloat16)
 
 
-def split_kernel(places, turn, place_ref, *refs):
-    arrays, outs = refs[:4], refs[4 : 4 + places]
-    taken, ready, in_sem, out_sem = refs[4 + places :]
+def split_kernel(places, turn, pairs, place_ref, *refs):
+    arrays, outs = refs[: 2 * pairs], refs[2 * pairs : 2 * pairs + places]
+    taken, ready, in_sem, out_sem = refs[2 * pairs + places :]
     turns = HEADS // places
     loads = []
     for k in range(places):
@@ -321,7 +321,7 @@
     for k in range(places):
         for copy in loads[k]:
             copy.wait()
-        for pair in range(2):
+        for pair in range(pairs):
             for row in range(2):
                 lines = slice(row * LINES, (row + 1) * LINES)
                 rows = jnp.concatenate(
@@ -336,16 +336,16 @@
 
 
 def split_heads(places, turn, place, arrays):
-    rows = arrays[0].shape[0]
+    rows, pairs = arrays[0].shape[0], len(arrays) // 2
     return pl.pallas_call(
-        lambda *refs: split_kernel(places, turn, *refs),
-        in_specs=[SCALARS] + [ANYWHERE] * 4,
+        lambda *refs: split_kernel(places, turn, pairs, *refs),
+        in_specs=[SCALARS] + [ANYWHERE] * (2 * pairs),
         out_specs=[ANYWHERE] * places,
-        out_shape=[jax.ShapeDtypeStruct((2, 2, LINES, LANES), jnp.bfloat16)] * places,
+        out_shape=[jax.ShapeDtypeStruct((pairs, 2, LINES, LANES), jnp.bfloat16)] * places,
         scratch_shapes=[
-            pltpu.VMEM((places, 4, rows, D_HEAD), jnp.bfloat16),
-            pltpu.VMEM((places, 2, 2, LINES, LANES), jnp.bfloat16),
-            pltpu.SemaphoreType.DMA((places, 4)),
+            pltpu.VMEM((places, 2 * pairs, rows, D_HEAD), jnp.bfloat16),
+            pltpu.VMEM((places, pairs, 2, LINES, LANES), jnp.bfloat16),
+            pltpu.SemaphoreType.DMA((places, 2 * pairs)),
             pltpu.SemaphoreType.DMA((places,)),
         ],
         compiler_params=PARAMS,
@@ -438,9 +438,9 @@
     )(*blocks)
 
 
-def grad_kernel(places, place_ref, bias_ref, *refs):
-    blocks, (from_above, from_below) = refs[:places], refs[places : places + 2]
-    outs = refs[places + 2 :]
+def grad_kernel(places, count, place_ref, start_ref, bias_ref, *refs):
+    groups = [refs[n * places : (n + 1) * places] for n in range(count)]
+    (from_above, from_below), outs = refs[count * places :][:2], refs[count * places + 2 :]
     dq_refs, acc_out, above_ref, below_ref = outs[:places], *outs[places : places + 3]
     kv, own_rows, acc, dq, scores, low, in_sem, halo_sem, out_sem = outs[places + 3 :]
     frames = places // TILE
@@ -450,8 +450,8 @@
         seat = place_ref[0] ^ k
         spot = (seat // TILE, seat % TILE)
         copies += [
-            pltpu.make_async_copy(blocks[k].at[0], kv.at[pl.ds(1, 2), *spot], in_sem.at[k, 0]),
-            pltpu.make_async_copy(blocks[k].at[1], own_rows.at[:, *spot], in_sem.at[k, 1]),
+            pltpu.make_async_copy(groups[0][k].at[0], kv.at[pl.ds(1, 2), *spot], in_sem.at[k, 0]),
+            pltpu.make_async_copy(groups[-1][k].at[2 - count], own_rows.at[:, *spot], in_sem.at[k, 1]),
             pltpu.make_async_copy(from_above.at[k], kv.at[0, *spot], halo_sem.at[k, 0]),
             pltpu.make_async_copy(from_below.at[k], kv.at[3, *spot], halo_sem.at[k, 1]),
         ]
@@ -463,26 +463,49 @@
     part = places * SPAN * TOK
     piece = SPAN * TOK
 
+    def diagonal(own):
+        cells = own.shape[0] // frames
+        blank = jnp.zeros((cells, D_HEAD), own.dtype)
+        lines = []
+        for frame in range(frames):
+            line = [blank] * frames
+            line[frame] = own[frame * cells : (frame + 1) * cells, :]
+            lines.append(jnp.concatenate(line, axis=1))
+        return jnp.concatenate(lines, axis=0)
+
     def group(col, _):
-        start = pl.multiple_of(jnp.clip(col - 2, 0, TW - SPAN) * TOK, TOK)
         here = pl.multiple_of(col * TOK, TOK)
-        window = pl.ds(start, piece)
-        pairs, tops = [], []
+        queries, grads, windows, tops = [], [], [], []
+
+        def near_keys(row, near, lanes):
+            return jnp.concatenate(
+                [
+                    kv[row + near, :, :, window, lanes].reshape(part, D_HEAD)
+                    for window in windows[row]
+                ],
+                axis=1,
+            )
+
         for row in range(2):
+            windows.append(
+                [
+                    pl.ds(pl.multiple_of(start_ref[(row * TW + col) * frames + f] * TOK, TOK), piece)
+                    for f in range(frames)
+                ]
+            )
             own = own_rows[row, :, :, pl.ds(here, TOK), :].reshape(-1, LANES)
-            blank = jnp.zeros((own.shape[0], D_HEAD), own.dtype)
-            pair = jnp.concatenate(
-                [
-                    jnp.concatenate([own[:, :D_HEAD], blank], axis=1),
-                    jnp.concatenate([blank, own[:, D_HEAD:]], axis=1),
-                ],
-                axis=0,
-            )
-            pairs.append(pair)
+            queries.append(diagonal(own[:, :D_HEAD]))
+            grads.append(diagonal(own[:, D_HEAD:]))
             top = None
             for near in range(3):
-                keys = kv[row + near, :, :, window, :].reshape(part, LANES)
-                both = lax.dot_general(keys, pair, NT, preferred_element_type=jnp.float32)
+                score_raw = lax.dot_general(
+                    near_keys(row, near, slice(0, D_HEAD)), queries[row], NT,
+                    preferred_element_type=jnp.float32,
+                )
+                scores[row, near, :, D_HEAD:] = lax.dot_general(
+                    near_keys(row, near, slice(D_HEAD, LANES)), grads[row], NT,
+                    preferred_element_type=jnp.float32,
+                )
                 for frame in range(frames):
                     first = (near * frames + frame) * SPAN
                     bias = jnp.concatenate(
@@ -496,9 +519,8 @@
                     )
                     for sub in range(TILE):
                         at = (frame * TILE + sub) * piece
-                        score = both[at : at + piece, :D_HEAD] * (scale * LOG2_E) + bias
+                        score = score_raw[at : at + piece, :] * (scale * LOG2_E) + bias
                         scores[row, near, at : at + piece, :D_HEAD] = score
-                        scores[row, near, at : at + piece, D_HEAD:] = both[at : at + piece, D_HEAD:]
                         most = jnp.max(score.reshape(-1, 8, D_HEAD), axis=0)
                         top = most if top is None else jnp.maximum(top, most)
             tops.append(jnp.max(top, axis=0, keepdims=True))
@@ -509,34 +531,45 @@
             for near in range(3):
                 for at in range(0, part, piece):
                     prob = jnp.exp2(scores[row, near, at : at + piece, :D_HEAD] - tops[row])
-                    scores[row, near, at : at + piece, :D_HEAD] = prob
                     total = total + jnp.sum(prob.reshape(-1, 8, D_HEAD), axis=0)
                     grad = prob * scores[row, near, at : at + piece, D_HEAD:]
                     delta = delta + jnp.sum(grad.reshape(-1, 8, D_HEAD), axis=0)
-            inverse = 1.0 / jnp.sum(total, axis=0, keepdims=True)
-            sums.append((inverse, jnp.sum(delta, axis=0, keepdims=True) * inverse))
+            total = jnp.sum(total, axis=0, keepdims=True)
+            delta = jnp.sum(delta, axis=0, keepdims=True) / total
+            sums.append((tops[row] + jnp.log2(total), delta))
         for row in range(2):
-            inverse, delta = sums[row]
+            log_total, delta = sums[row]
             query_grad = None
             for near in range(3):
                 for at in range(0, part, piece):
-                    weight = scores[row, near, at : at + piece, :D_HEAD] * inverse
+                    weight = jnp.exp2(scores[row, near, at : at + piece, :D_HEAD] - log_total)
                     dscore = weight * (scores[row, near, at : at + piece, D_HEAD:] - delta)
                     low[row, near, at : at + piece, :D_HEAD] = dscore.astype(jnp.bfloat16)
                     low[row, near, at : at + piece, D_HEAD:] = weight.astype(jnp.bfloat16)
-                added = lax.dot_general(
-                    low[row, near], pairs[row], NN, preferred_element_type=jnp.float32
+                key_part = lax.dot_general(
+                    low[row, near, :, :D_HEAD], queries[row], NN, preferred_element_type=jnp.float32
                 )
-                spot = (row + near, slice(None), slice(None), window, slice(None))
-                acc[spot] = acc[spot] + added.reshape(frames, TILE, piece, LANES)
-                keys = kv[row + near, :, :, window, :D_HEAD].reshape(part, D_HEAD)
+                value_part = lax.dot_general(
+                    low[row, near, :, D_HEAD:], grads[row], NN, preferred_element_type=jnp.float32
+                )
+                for f in range(frames):
+                    lanes = slice(f * D_HEAD, (f + 1) * D_HEAD)
+                    added = jnp.concatenate([key_part[:, lanes], value_part[:, lanes]], axis=1)
+                    spot = (row + near, slice(None), slice(None), windows[row][f], slice(None))
+                    acc[spot] = acc[spot] + added.reshape(frames, TILE, piece, LANES)
                 more = lax.dot_general(
-                    low[row, near, :, :D_HEAD], keys, TN, preferred_element_type=jnp.float32
+                    low[row, near, :, :D_HEAD],
+                    near_keys(row, near, slice(0, D_HEAD)),
+                    TN,
+                    preferred_element_type=jnp.float32,
                 )
                 query_grad = more if query_grad is None else query_grad + more
-            dq[row, :, :, pl.ds(here, TOK), :] = (
-                (query_grad * scale).astype(jnp.bfloat16).reshape(frames, TILE, TOK, D_HEAD)
-            )
+            for f in range(frames):
+                cells = query_grad.shape[0] // frames
+                mine = query_grad[f * cells : (f + 1) * cells, f * D_HEAD : (f + 1) * D_HEAD]
+                dq[row, f, :, pl.ds(here, TOK), :] = (
+                    (mine * scale).astype(jnp.bfloat16).reshape(TILE, TOK, D_HEAD)
+                )
         return 0
 
     lax.fori_loop(0, TW, group, 0)
@@ -559,12 +592,12 @@
         copy.wait()
 
 
-def head_grads(places, place, bias, blocks, from_above, from_below):
+def head_grads(places, place, starts, bias, groups, from_above, from_below):
     frames = places // TILE
     part = places * SPAN * TOK
     results = pl.pallas_call(
-        lambda *refs: grad_kernel(places, *refs),
-        in_specs=[SCALARS, WHOLE] + [ANYWHERE] * (places + 2),
+        lambda *refs: grad_kernel(places, len(groups), *refs),
+        in_specs=[SCALARS, SCALARS, WHOLE] + [ANYWHERE] * (len(groups) * places + 2),
         out_specs=[ANYWHERE] * (places + 1) + [WHOLE] * 2,
         out_shape=[jax.ShapeDtypeStruct((2, LINES, D_HEAD), jnp.bfloat16)] * places
         + [jax.ShapeDtypeStruct((places, 2, LINES, LANES), jnp.float32)]
@@ -584,7 +617,7 @@
         cost_estimate=pl.CostEstimate(
             flops=60_000_000_000, bytes_accessed=0, transcendentals=0
         ),
-    )(place, bias, *blocks, from_above, from_below)
+    )(place, starts, bias, *[block for group in groups for block in group], from_above, from_below)
     return results[:places], *results[places:]
 
 
@@ -612,30 +645,29 @@
     )(acc, above, below, *query)
 
 
-def window_bias(tile_valid, width_shift, first_row):
-    frames, tile_rows, cols = tile_valid.shape
-    row = (first_row + jnp.arange(2)).reshape(-1, 1, 1, 1, 1, 1)
-    col = jnp.arange(cols).reshape(1, -1, 1, 1, 1, 1)
-    near = jnp.arange(3).reshape(1, 1, -1, 1, 1, 1) - 1
-    key_frame = jnp.arange(frames).reshape(1, 1, 1, -1, 1, 1)
-    key_col = jnp.clip(col - 2, 0, cols - SPAN) + jnp.arange(SPAN).reshape(1, 1, 1, 1, -1, 1)
-    frame = jnp.arange(frames).reshape(1, 1, 1, 1, 1, -1)
+def window_tables(tile_valid, width_shift, first_row):
+    frames, _, cols = tile_valid.shape
     shift_own = lax.dynamic_slice_in_dim(width_shift, first_row, 2, 1)
-    shift_own = shift_own.transpose(1, 2, 0).reshape(2, cols, 1, 1, 1, frames)
-    valid_near = lax.dynamic_slice_in_dim(
-        jnp.pad(tile_valid, ((0, 0), (1, 1), (0, 0))), first_row, 4, 1
-    )
-    valid_rows = jnp.stack([valid_near[:, n : n + 2] for n in range(3)])
-    starts = [min(max(c - 2, 0), cols - SPAN) for c in range(cols)]
-    valid_cols = jnp.stack([valid_rows[:, :, :, s : s + SPAN] for s in starts])
-    valid = valid_cols.transpose(3, 0, 1, 2, 4).reshape(2, cols, 3, frames, SPAN, 1)
-    own = (near == 0) & (key_frame == frame) & (key_col == col)
-    inside = jnp.abs(key_col - col - shift_own) <= 1
-    there = (row + near >= 0) & (row + near < tile_rows)
-    bias = jnp.where(inside & there & ((valid == 1) | own), 0.0, MASKED_SCORE).astype(jnp.float32)
-    bias = bias.reshape(2, cols, 3 * frames * SPAN, frames, 1)
+    first = jnp.clip(jnp.arange(cols) + shift_own - 1, 0, cols - SPAN)
+    valid = lax.dynamic_slice_in_dim(
+        jnp.pad(tile_valid, ((0, 0), (1, 1), (2, 2))), first_row, 4, 1
+    )
+    near = jnp.stack([valid[:, n : n + 2] for n in range(3)])[:, :, None]
+    moved = jnp.stack([near[..., d : d + cols] for d in range(5)])
+    shift = first - (jnp.arange(cols) - 1)
+    chosen = jnp.where(shift == -1, moved[0:3], jnp.where(shift == 0, moved[1:4], moved[2:5]))
+    place_of = jnp.arange(3).reshape(-1, 1, 1, 1, 1, 1)
+    near_of = jnp.arange(3).reshape(1, -1, 1, 1, 1, 1)
+    key_frame = jnp.arange(frames).reshape(1, 1, -1, 1, 1, 1)
+    frame = jnp.arange(frames).reshape(1, 1, 1, -1, 1, 1)
+    own = (near_of == 1) & (key_frame == frame) & (place_of + shift == 1)
+    bias = jnp.where((chosen == 1) | own, 0.0, MASKED_SCORE).astype(jnp.float32)
+    bias = bias.transpose(4, 5, 1, 2, 0, 3).reshape(2, cols, 3 * frames * SPAN, frames, 1)
     bias = jnp.broadcast_to(bias, bias.shape[:4] + (TILE**3,))
-    return bias.reshape(2, cols, 3 * frames * SPAN, frames * TILE**3)
+    return (
+        first.transpose(1, 2, 0).reshape(-1),
+        bias.reshape(2, cols, 3 * frames * SPAN, frames * TILE**3),
+    )
 
 
 def place_shards(queries, key_states, value_states, out_grad, tile_valid, width_shift):
@@ -647,7 +679,7 @@
     seq_index = lax.axis_index("seq")
     place = (lax.axis_index("tm") * TILE + seq_index // 2).reshape(1)
     first_row = lax.axis_index("height") * TH_DEV + seq_index % 2 * 2
-    bias = window_bias(tile_valid, width_shift, first_row)
+    starts, bias = window_tables(tile_valid, width_shift, first_row)
     chain = [
         [h * seq_count + frame * 2 + half for h in range(heights) for half in range(2)]
         for frame in range(TILE)
@@ -685,17 +717,20 @@
     def ordered(first, then):
         return lax.optimization_barrier((first, then))
 
+    def ordered(first, then):
+        return lax.optimization_barrier((first, then))
+
     arrays = (key_states, value_states, queries, out_grad)
     outs = ()
-    blocks = exchange(split_heads(places, 0, place, arrays), natural)
+    groups = [exchange(split_heads(places, 0, place, arrays), natural)]
     leaving = None
     for turn in range(turns):
         more = turn + 1 < turns
         if more:
             coming = split_heads(places, turn + 1, place, arrays)
-            blocks[1:6], coming = ordered(blocks[1:6], coming)
-        first, last = edge_rows(places, blocks)
-        grads = head_grads(places, place, bias, blocks, step(last, down), step(first, up))
+            groups[-1][1:6], coming = ordered(groups[-1][1:6], coming)
+        first, last = edge_rows(places, groups[0])
+        grads = head_grads(places, place, starts, bias, groups, step(last, down), step(first, up))
         if leaving is not None:
             leaving, grads = after(leaving, grads)
             left = exchange(leaving, mixed)
@@ -705,7 +740,7 @@
             outs = join_heads(places, turn - 1, place, [left], outs)
         if more:
             coming, grads = after(coming, grads)
-            blocks = exchange(coming, mixed)
+            groups = [exchange(coming, mixed)]
         dq, acc, above, below = grads
         leaving = finish_pairs(places, acc, step(below, down), step(above, up), dq)
     outs = join_heads(places, turns - 1, place, [exchange(leaving, natural)], outs)

time: 385 us -> 374 us (0.971)
  Pallas kernels: 136 us -> 124 us
  waiting for transfers between devices: 176 us -> 185 us
  starting transfers between devices: 57.9 us -> 52.7 us
    pallas_call x4, Pallas kernels: 112 us -> 99.7 us  [the longest x2 90.1 us: head_grads(): pl.pallas_call(lambda *refs: grad_kernel(places, len(groups), *refs), in_...]
    ppermute x28, starting transfers between devices: 34.7 us -> 28.8 us  [send(): lax.ppermute(block, ('tm', 'seq'), [(i, i ^ 2 * k) for i in range(2 * pla...]
    ppermute x28, waiting for transfers between devices: 156 us -> 160 us  [send(): lax.ppermute(block, ('tm', 'seq'), [(i, i ^ 2 * k) for i in range(2 * pla...]
  transfers between devices with their start and end apart: 36 -> 36, of which waited for: 17 -> 17; matrix products, arithmetic and copies ran while one was open for 2% -> 1% of each run, Pallas kernels for 32% -> 30%
where the time goes in v3:
time: 374 us
  waiting for transfers between devices  185 us (49%)
  Pallas kernels  124 us (33%)
  starting transfers between devices  52.7 us (14%)
  local copies, waits for them, and re-layouts  10.6 us (3%)
    ppermute x28, waiting for transfers between devices, send(): lax.ppermute(block, ('tm', 'seq'), [(i, i ^ 2 * k) for i in range(2 * pla...  160 us
    pallas_call x2, Pallas kernels, head_grads(): pl.pallas_call(lambda *refs: grad_kernel(places, len(groups), *refs), in_...  90.1 us
    ppermute x28, starting transfers between devices, send(): lax.ppermute(block, ('tm', 'seq'), [(i, i ^ 2 * k) for i in range(2 * pla...  28.8 us
    ppermute x8, waiting for transfers between devices, step(): return lax.ppermute(block, ('height', 'seq'), route)  24.4 us
    ppermute x8, starting transfers between devices, step(): return lax.ppermute(block, ('height', 'seq'), route)  23.9 us
    pallas_call x2, Pallas kernels, finish_pairs(): pl.pallas_call(lambda *refs: finish_kernel(places, *refs), in_specs=[WHOL...  9.63 us
    pallas_call x2, Pallas kernels, split_heads(): pl.pallas_call(lambda *refs: split_kernel(places, turn, pairs, *refs), in...  9.56 us
    pallas_call x2, Pallas kernels, join_heads(): pl.pallas_call(lambda *refs: join_kernel(places, turn, widths, len(earlie...  8.77 us
  transfers between devices with their start and end apart: 36, of which 17 were waited for; matrix products, arithmetic and copies ran while one was open for 1% of the time, Pallas kernels for 30%

profile of v3, /device:TPU:9, one launch (start us, length us, event | category | flops | bytes accessed | tf_op | source)
XLA Modules:
  0.0 374.1 jit_solution(18375679808246994901)
XLA Ops:
  0.6 4.8 %shard_map.85 = (bf16[2,2,256,256]{3,2,1,0:T(8,128)(2,1)}, bf16[2,2,256,256]{3,2,1,0:T(8,128)(2,1)}, bf16[2,2,256,256]{3,2,1,0:T(8,128)(2,1)}, bf16[2,2,256,256]...) custom-call(s32[1]{0:T(128)} %bitcast.refs_0_, ...), custom_call_target="tpu_custom_call" | custom-call | tf_op jit(solution)/shard_map/pallas_call | solution.py:340
  10.5 4.8 %shard_map.86 = (bf16[2,2,256,256]{3,2,1,0:T(8,128)(2,1)}, bf16[2,2,256,256]{3,2,1,0:T(8,128)(2,1)}, bf16[2,2,256,256]{3,2,1,0:T(8,128)(2,1)}, bf16[2,2,256,256]...) custom-call(s32[1]{0:T(128)} %bitcast.refs_0_, ...), custom_call_target="tpu_custom_call" | custom-call | tf_op jit(solution)/shard_map/pallas_call | solution.py:340
  15.3 11.9 %collective-permute-done.refs_1_.refs_4_ = bf16[2,2,256,256]{3,2,1,0:T(8,128)(2,1)S(1)} collective-permute-done((bf16[2,2,256,256]{3,2,1,0:T(8,128)(2,1)}, bf16[2,2,256,256]{3,2,1,0:T(8,128)(2,1)S(1)}, u32[]{:S(2)}, u32[]{:S(2)}) %collective-permute-start) | collective-permute-done | bytes 524320 | tf_op jit(solution)/shard_map/ppermute | solution.py:691
  27.2 4.5 %collective-permute-start.5 = (bf16[2,2,256,256]{3,2,1,0:T(8,128)(2,1)}, bf16[2,2,256,256]{3,2,1,0:T(8,128)(2,1)S(1)}, u32[]{:S(2)}, u32[]{:S(2)}) collective-permute-start(bf16[2,2,256,256]{3,2,1,0:T(8,128)(2,1)} %get-tuple-element.143), channel_id=1, source_target_pairs={{0,20},{1,21},{2,22},{3,23},{4,16},{5,17},{6,18},{7,19},{16,4},{17... | collective-permute-start | bytes 1572872 | tf_op jit(solution)/shard_map/ppermute | solution.py:691
  31.9 21.3 %collective-permute-done.2.refs_3_.refs_6_ = bf16[2,2,256,256]{3,2,1,0:T(8,128)(2,1)S(1)} collective-permute-done((bf16[2,2,256,256]{3,2,1,0:T(8,128)(2,1)}, bf16[2,2,256,256]{3,2,1,0:T(8,128)(2,1)S(1)}, u32[]{:S(2)}, u32[]{:S(2)}) %collective-permute-start.2) | collective-permute-done | bytes 524320 | tf_op jit(solution)/shard_map/ppermute | solution.py:691
  53.2 32.9 %collective-permute-done.5.refs_6_.refs_9_ = bf16[2,2,256,256]{3,2,1,0:T(8,128)(2,1)S(1)} collective-permute-done((bf16[2,2,256,256]{3,2,1,0:T(8,128)(2,1)}, bf16[2,2,256,256]{3,2,1,0:T(8,128)(2,1)S(1)}, u32[]{:S(2)}, u32[]{:S(2)}) %collective-permute-start.5) | collective-permute-done | bytes 524320 | tf_op jit(solution)/shard_map/ppermute | solution.py:691
  86.1 13.0 %collective-permute-done.6.refs_7_.refs_10_ = bf16[2,2,256,256]{3,2,1,0:T(8,128)(2,1)S(1)} collective-permute-done((bf16[2,2,256,256]{3,2,1,0:T(8,128)(2,1)S(1)}, bf16[2,2,256,256]{3,2,1,0:T(8,128)(2,1)S(1)}, u32[]{:S(2)}, u32[]{:S(2)}) %collective-permute-start.6) | collective-permute-done | bytes 524320 | tf_op jit(solution)/shard_map/ppermute | solution.py:691
  99.8 3.1 shard_map.87
  102.9 5.0 %collective-permute-start.7 = (bf16[8,256,256]{2,1,0:T(8,128)(2,1)}, bf16[8,256,256]{2,1,0:T(8,128)(2,1)S(1)}, u32[]{:S(2)}, u32[]{:S(2)}) collective-permute-start(bf16[8,256,256]{2,1,0:T(8,128)(2,1)} %get-tuple-element.145), channel_id=1, source_target_pairs={{0,1},{1,8},{8,9},{2,3},{3,10},{10,11},{4,5},{5,12},{12,13},{6,7},... | collective-permute-start | bytes 3145736 | tf_op jit(solution)/shard_map/ppermute | solution.py:694
  115.1 4.9 %collective-permute-done.7.refs_11_ = bf16[8,256,256]{2,1,0:T(8,128)(2,1)S(1)} collective-permute-done((bf16[8,256,256]{2,1,0:T(8,128)(2,1)}, bf16[8,256,256]{2,1,0:T(8,128)(2,1)S(1)}, u32[]{:S(2)}, u32[]{:S(2)}) %collective-permute-start.7) | collective-permute-done | bytes 1048608 | tf_op jit(solution)/shard_map/ppermute | solution.py:694
  120.0 4.6 %collective-permute-done.8.refs_12_ = bf16[8,256,256]{2,1,0:T(8,128)(2,1)S(1)} collective-permute-done((bf16[8,256,256]{2,1,0:T(8,128)(2,1)}, bf16[8,256,256]{2,1,0:T(8,128)(2,1)S(1)}, u32[]{:S(2)}, u32[]{:S(2)}) %collective-permute-start.8) | collective-permute-done | bytes 1048608 | tf_op jit(solution)/shard_map/ppermute | solution.py:694
  125.5 45.1 %shard_map.88 = (bf16[2,256,128]{2,1,0:T(8,128)(2,1)}, bf16[2,256,128]{2,1,0:T(8,128)(2,1)}, bf16[2,256,128]{2,1,0:T(8,128)(2,1)}, bf16[2,256,128]{2,1,0:T(8,128...) custom-call(s32[1]{0:T(128)} %bitcast.refs_0_, ...), custom_call_target="tpu_custom_call" | custom-call | flops 60000002048 | tf_op jit(solution)/shard_map/pallas_call | solution.py:598
  173.4 3.8 %collective-permute-start.9 = (bf16[8,256,256]{2,1,0:T(8,128)(2,1)}, bf16[8,256,256]{2,1,0:T(8,128)(2,1)S(1)}, u32[]{:S(2)}, u32[]{:S(2)}) collective-permute-start(bf16[8,256,256]{2,1,0:T(8,128)(2,1)} %get-tuple-element.159), channel_id=1, source_target_pairs={{0,1},{1,8},{8,9},{2,3},{3,10},{10,11},{4,5},{5,12},{12,13},{6,7},... | collective-permute-start | bytes 3145736 | tf_op jit(solution)/shard_map/ppermute | solution.py:694
  179.2 13.9 %collective-permute-done.21.refs_6_.refs_9_ = bf16[2,2,256,256]{3,2,1,0:T(8,128)(2,1)S(1)} collective-permute-done((bf16[2,2,256,256]{3,2,1,0:T(8,128)(2,1)S(1)}, bf16[2,2,256,256]{3,2,1,0:T(8,128)(2,1)S(1)}, u32[]{:S(2)}, u32[]{:S(2)}) %collective-permute-start.21) | collective-permute-done | bytes 524320 | tf_op jit(solution)/shard_map/ppermute | solution.py:691
  193.1 6.7 %collective-permute-done.16.refs_1_.refs_4_ = bf16[2,2,256,256]{3,2,1,0:T(8,128)(2,1)S(1)} collective-permute-done((bf16[2,2,256,256]{3,2,1,0:T(8,128)(2,1)S(1)}, bf16[2,2,256,256]{3,2,1,0:T(8,128)(2,1)S(1)}, u32[]{:S(2)}, u32[]{:S(2)}) %collective-permute-start.16) | collective-permute-done | bytes 524320 | tf_op jit(solution)/shard_map/ppermute | solution.py:691
  199.8 4.0 %collective-permute-done.22.refs_7_.refs_10_ = bf16[2,2,256,256]{3,2,1,0:T(8,128)(2,1)S(1)} collective-permute-done((bf16[2,2,256,256]{3,2,1,0:T(8,128)(2,1)S(1)}, bf16[2,2,256,256]{3,2,1,0:T(8,128)(2,1)S(1)}, u32[]{:S(2)}, u32[]{:S(2)}) %collective-permute-start.22) | collective-permute-done | bytes 524320 | tf_op jit(solution)/shard_map/ppermute | solution.py:691
  204.7 3.0 shard_map.90
  207.8 4.8 %collective-permute-start.23 = (bf16[8,256,256]{2,1,0:T(8,128)(2,1)}, bf16[8,256,256]{2,1,0:T(8,128)(2,1)S(1)}, u32[]{:S(2)}, u32[]{:S(2)}) collective-permute-start(bf16[8,256,256]{2,1,0:T(8,128)(2,1)} %get-tuple-element.184), channel_id=1, source_target_pairs={{0,1},{1,8},{8,9},{2,3},{3,10},{10,11},{4,5},{5,12},{12,13},{6,7},... | collective-permute-start | bytes 3145736 | tf_op jit(solution)/shard_map/ppermute | solution.py:694
  216.6 4.8 %shard_map.89 = (bf16[2,256,384]{2,1,0:T(8,128)(2,1)}, bf16[2,256,384]{2,1,0:T(8,128)(2,1)}, bf16[2,256,384]{2,1,0:T(8,128)(2,1)}, bf16[2,256,384]{2,1,0:T(8,128...) custom-call(f32[8,2,256,256]{3,2,1,0:T(8,128)} %get-tuple-element.15, ...), custom_call_target="tpu_custom_call" | custom-call | tf_op jit(solution)/shard_map/pallas_call | solution.py:639
  221.7 4.1 %collective-permute-start.13 = (bf16[2,256,384]{2,1,0:T(8,128)(2,1)}, bf16[2,256,384]{2,1,0:T(8,128)(2,1)S(1)}, u32[]{:S(2)}, u32[]{:S(2)}) collective-permute-start(bf16[2,256,384]{2,1,0:T(8,128)(2,1)} %get-tuple-element.171), channel_id=1, source_target_pairs={{0,20},{1,21},{2,22},{3,23},{4,16},{5,17},{6,18},{7,19},{16,4},{17... | collective-permute-start | bytes 1179656 | tf_op jit(solution)/shard_map/ppermute | solution.py:691
  226.1 3.1 collective-permute-done.24.refs_12_
  230.1 45.0 %shard_map.91 = (bf16[2,256,128]{2,1,0:T(8,128)(2,1)}, bf16[2,256,128]{2,1,0:T(8,128)(2,1)}, bf16[2,256,128]{2,1,0:T(8,128)(2,1)}, bf16[2,256,128]{2,1,0:T(8,128...) custom-call(s32[1]{0:T(128)} %bitcast.refs_0_, ...), custom_call_target="tpu_custom_call" | custom-call | flops 60000002048 | tf_op jit(solution)/shard_map/pallas_call | solution.py:598
  282.0 7.3 %collective-permute-done.25.refs_1_ = bf16[8,256,256]{2,1,0:T(8,128)(2,1)S(1)} collective-permute-done((bf16[8,256,256]{2,1,0:T(8,128)(2,1)}, bf16[8,256,256]{2,1,0:T(8,128)(2,1)S(1)}, u32[]{:S(2)}, u32[]{:S(2)}) %collective-permute-start.25) | collective-permute-done | bytes 1048608 | tf_op jit(solution)/shard_map/ppermute | solution.py:694
  289.2 4.6 %collective-permute-done.26.refs_2_ = bf16[8,256,256]{2,1,0:T(8,128)(2,1)S(1)} collective-permute-done((bf16[8,256,256]{2,1,0:T(8,128)(2,1)}, bf16[8,256,256]{2,1,0:T(8,128)(2,1)S(1)}, u32[]{:S(2)}, u32[]{:S(2)}) %collective-permute-start.26) | collective-permute-done | bytes 1048608 | tf_op jit(solution)/shard_map/ppermute | solution.py:694
  294.8 4.8 %shard_map.92 = (bf16[2,256,384]{2,1,0:T(8,128)(2,1)}, bf16[2,256,384]{2,1,0:T(8,128)(2,1)}, bf16[2,256,384]{2,1,0:T(8,128)(2,1)}, bf16[2,256,384]{2,1,0:T(8,128...) custom-call(f32[8,2,256,256]{3,2,1,0:T(8,128)} %get-tuple-element.20, ...), custom_call_target="tpu_custom_call" | custom-call | tf_op jit(solution)/shard_map/pallas_call | solution.py:639
  305.8 12.5 %collective-permute-done.27.refs_2_ = bf16[2,256,384]{2,1,0:T(8,128)(2,1)S(1)} collective-permute-done((bf16[2,256,384]{2,1,0:T(8,128)(2,1)}, bf16[2,256,384]{2,1,0:T(8,128)(2,1)S(1)}, u32[]{:S(2)}, u32[]{:S(2)}) %collective-permute-start.27) | collective-permute-done | bytes 393248 | tf_op jit(solution)/shard_map/ppermute | solution.py:691
  319.4 8.9 %collective-permute-done.28.refs_3_ = bf16[2,256,384]{2,1,0:T(8,128)(2,1)S(1)} collective-permute-done((bf16[2,256,384]{2,1,0:T(8,128)(2,1)}, bf16[2,256,384]{2,1,0:T(8,128)(2,1)S(1)}, u32[]{:S(2)}, u32[]{:S(2)}) %collective-permute-start.28) | collective-permute-done | bytes 393248 | tf_op jit(solution)/shard_map/ppermute | solution.py:691
  328.9 4.4 %shard_map.93 = (bf16[512,2048]{1,0:T(8,128)(2,1)}, bf16[512,2048]{1,0:T(8,128)(2,1)}, bf16[512,2048]{1,0:T(8,128)(2,1)}) custom-call(s32[1]{0:T(128)} %bitcast.refs_0_, bf16[2,256,384]{2,1,0:T(8,128)(2,1)} %get-tuple-element.227.refs_1_, bf16[2,256,384]{2,1,0:T(8,128)(2,1)} %copy-done.30, bf16[2,256,384]{2,1,0:T(8,128)(2,1)} %copy-done.25, ...), custom_call_target="tpu_custom_call" | custom-call | tf_op jit(solution)/shard_map/pallas_call | solution.py:402
  333.3 20.4 %collective-permute-done.29.refs_4_ = bf16[2,256,384]{2,1,0:T(8,128)(2,1)S(1)} collective-permute-done((bf16[2,256,384]{2,1,0:T(8,128)(2,1)}, bf16[2,256,384]{2,1,0:T(8,128)(2,1)S(1)}, u32[]{:S(2)}, u32[]{:S(2)}) %collective-permute-start.29) | collective-permute-done | bytes 393248 | tf_op jit(solution)/shard_map/ppermute | solution.py:691
  353.7 8.3 %collective-permute-done.32.refs_7_ = bf16[2,256,384]{2,1,0:T(8,128)(2,1)S(1)} collective-permute-done((bf16[2,256,384]{2,1,0:T(8,128)(2,1)}, bf16[2,256,384]{2,1,0:T(8,128)(2,1)S(1)}, u32[]{:S(2)}, u32[]{:S(2)}) %collective-permute-start.32) | collective-permute-done | bytes 393248 | tf_op jit(solution)/shard_map/ppermute | solution.py:691
  362.0 6.7 %collective-permute-done.33.refs_8_ = bf16[2,256,384]{2,1,0:T(8,128)(2,1)S(1)} collective-permute-done((bf16[2,256,384]{2,1,0:T(8,128)(2,1)}, bf16[2,256,384]{2,1,0:T(8,128)(2,1)S(1)}, u32[]{:S(2)}, u32[]{:S(2)}) %collective-permute-start.33) | collective-permute-done | bytes 393248 | tf_op jit(solution)/shard_map/ppermute | solution.py:691
  369.5 4.4 %shard_map.94 = (bf16[512,2048]{1,0:T(8,128)(2,1)}, bf16[512,2048]{1,0:T(8,128)(2,1)}, bf16[512,2048]{1,0:T(8,128)(2,1)}) custom-call(s32[1]{0:T(128)} %bitcast.refs_0_, bf16[2,256,384]{2,1,0:T(8,128)(2,1)} %get-tuple-element.219.refs_1_, bf16[2,256,384]{2,1,0:T(8,128)(2,1)} %copy-done.18, ...), custom_call_target="tpu_custom_call", output_to_operand_aliasing={{0}: (9, {}), {1}: (10, {}), {2}: (11, {})} | custom-call | tf_op jit(solution)/shard_map/pallas_call | solution.py:402
  (169 shorter events, 41.5 us)
Async XLA Ops:
  5.4 21.8 %collective-permute-start = (bf16[2,2,256,256]{3,2,1,0:T(8,128)(2,1)}, bf16[2,2,256,256]{3,2,1,0:T(8,128)(2,1)S(1)}, u32[]{:S(2)}, u32[]{:S(2)}) collective-permute-start(bf16[2,2,256,256]{3,2,1,0:T(8,128)(2,1)} %get-tuple-element.122), channel_id=1, source_target_pairs={{0,2},{1,3},{2,0},{3,1},{4,6},{5,7},{6,4},{7,5},{16,18},{17,19},{1... | collective-permute-start | bytes 1572872 | tf_op jit(solution)/shard_map/ppermute | solution.py:691
  5.5 26.1 %collective-permute-start.1 = (bf16[2,2,256,256]{3,2,1,0:T(8,128)(2,1)}, bf16[2,2,256,256]{3,2,1,0:T(8,128)(2,1)S(1)}, u32[]{:S(2)}, u32[]{:S(2)}) collective-permute-start(bf16[2,2,256,256]{3,2,1,0:T(8,128)(2,1)} %get-tuple-element.123), channel_id=1, source_target_pairs={{0,4},{1,5},{2,6},{3,7},{4,0},{5,1},{6,2},{7,3},{16,20},{17,21},{1... | collective-permute-start | bytes 1572872 | tf_op jit(solution)/shard_map/ppermute | solution.py:691
  8.0 45.2 %collective-permute-start.2 = (bf16[2,2,256,256]{3,2,1,0:T(8,128)(2,1)}, bf16[2,2,256,256]{3,2,1,0:T(8,128)(2,1)S(1)}, u32[]{:S(2)}, u32[]{:S(2)}) collective-permute-start(bf16[2,2,256,256]{3,2,1,0:T(8,128)(2,1)} %get-tuple-element.124), channel_id=1, source_target_pairs={{0,6},{1,7},{2,4},{3,5},{4,2},{5,3},{6,0},{7,1},{16,22},{17,23},{1... | collective-permute-start | bytes 1572872 | tf_op jit(solution)/shard_map/ppermute | solution.py:691
  8.1 45.1 %collective-permute-start.3 = (bf16[2,2,256,256]{3,2,1,0:T(8,128)(2,1)}, bf16[2,2,256,256]{3,2,1,0:T(8,128)(2,1)S(1)}, u32[]{:S(2)}, u32[]{:S(2)}) collective-permute-start(bf16[2,2,256,256]{3,2,1,0:T(8,128)(2,1)} %get-tuple-element.125), channel_id=1, source_target_pairs={{0,16},{1,17},{2,18},{3,19},{4,20},{5,21},{6,22},{7,23},{16,0},{17... | collective-permute-start | bytes 1572872 | tf_op jit(solution)/shard_map/ppermute | solution.py:691
  9.3 43.9 %collective-permute-start.4 = (bf16[2,2,256,256]{3,2,1,0:T(8,128)(2,1)}, bf16[2,2,256,256]{3,2,1,0:T(8,128)(2,1)S(1)}, u32[]{:S(2)}, u32[]{:S(2)}) collective-permute-start(bf16[2,2,256,256]{3,2,1,0:T(8,128)(2,1)} %get-tuple-element.126), channel_id=1, source_target_pairs={{0,18},{1,19},{2,16},{3,17},{4,22},{5,23},{6,20},{7,21},{16,2},{17... | collective-permute-start | bytes 1572872 | tf_op jit(solution)/shard_map/ppermute | solution.py:691
  27.2 58.9 %collective-permute-start.5 = (bf16[2,2,256,256]{3,2,1,0:T(8,128)(2,1)}, bf16[2,2,256,256]{3,2,1,0:T(8,128)(2,1)S(1)}, u32[]{:S(2)}, u32[]{:S(2)}) collective-permute-start(bf16[2,2,256,256]{3,2,1,0:T(8,128)(2,1)} %get-tuple-element.143), channel_id=1, source_target_pairs={{0,20},{1,21},{2,22},{3,23},{4,16},{5,17},{6,18},{7,19},{16,4},{17... | collective-permute-start | bytes 1572872 | tf_op jit(solution)/shard_map/ppermute | solution.py:691
  31.6 67.4 %collective-permute-start.6 = (bf16[2,2,256,256]{3,2,1,0:T(8,128)(2,1)S(1)}, bf16[2,2,256,256]{3,2,1,0:T(8,128)(2,1)S(1)}, u32[]{:S(2)}, u32[]{:S(2)}) collective-permute-start(bf16[2,2,256,256]{3,2,1,0:T(8,128)(2,1)S(1)} %copy-done.41), channel_id=1, source_target_pairs={{0,22},{1,23},{2,20},{3,21},{4,18},{5,19},{6,16},{7,17},{16,6},{17... | collective-permute-start | bytes 1572872 | tf_op jit(solution)/shard_map/ppermute | solution.py:691
  102.9 17.0 %collective-permute-start.7 = (bf16[8,256,256]{2,1,0:T(8,128)(2,1)}, bf16[8,256,256]{2,1,0:T(8,128)(2,1)S(1)}, u32[]{:S(2)}, u32[]{:S(2)}) collective-permute-start(bf16[8,256,256]{2,1,0:T(8,128)(2,1)} %get-tuple-element.145), channel_id=1, source_target_pairs={{0,1},{1,8},{8,9},{2,3},{3,10},{10,11},{4,5},{5,12},{12,13},{6,7},... | collective-permute-start | bytes 3145736 | tf_op jit(solution)/shard_map/ppermute | solution.py:694
  113.6 57.1 %collective-permute-start.17 = (bf16[2,2,256,256]{3,2,1,0:T(8,128)(2,1)}, bf16[2,2,256,256]{3,2,1,0:T(8,128)(2,1)S(1)}, u32[]{:S(2)}, u32[]{:S(2)}) collective-permute-start(bf16[2,2,256,256]{3,2,1,0:T(8,128)(2,1)} %get-tuple-element.178), channel_id=1, source_target_pairs={{0,4},{1,5},{2,6},{3,7},{4,0},{5,1},{6,2},{7,3},{16,20},{17,21},{1... | collective-permute-start | bytes 1572872 | tf_op jit(solution)/shard_map/ppermute | solution.py:691
  113.6 58.7 %collective-permute-start.18 = (bf16[2,2,256,256]{3,2,1,0:T(8,128)(2,1)}, bf16[2,2,256,256]{3,2,1,0:T(8,128)(2,1)S(1)}, u32[]{:S(2)}, u32[]{:S(2)}) collective-permute-start(bf16[2,2,256,256]{3,2,1,0:T(8,128)(2,1)} %get-tuple-element.179), channel_id=1, source_target_pairs={{0,6},{1,7},{2,4},{3,5},{4,2},{5,3},{6,0},{7,1},{16,22},{17,23},{1... | collective-permute-start | bytes 1572872 | tf_op jit(solution)/shard_map/ppermute | solution.py:691
  114.9 58.5 %collective-permute-start.19 = (bf16[2,2,256,256]{3,2,1,0:T(8,128)(2,1)}, bf16[2,2,256,256]{3,2,1,0:T(8,128)(2,1)S(1)}, u32[]{:S(2)}, u32[]{:S(2)}) collective-permute-start(bf16[2,2,256,256]{3,2,1,0:T(8,128)(2,1)} %get-tuple-element.180), channel_id=1, source_target_pairs={{0,16},{1,17},{2,18},{3,19},{4,20},{5,21},{6,22},{7,23},{16,0},{17... | collective-permute-start | bytes 1572872 | tf_op jit(solution)/shard_map/ppermute | solution.py:691
  120.0 57.3 %collective-permute-start.20 = (bf16[2,2,256,256]{3,2,1,0:T(8,128)(2,1)}, bf16[2,2,256,256]{3,2,1,0:T(8,128)(2,1)S(1)}, u32[]{:S(2)}, u32[]{:S(2)}) collective-permute-start(bf16[2,2,256,256]{3,2,1,0:T(8,128)(2,1)} %get-tuple-element.181), channel_id=1, source_target_pairs={{0,18},{1,19},{2,16},{3,17},{4,22},{5,23},{6,20},{7,21},{16,2},{17... | collective-permute-start | bytes 1572872 | tf_op jit(solution)/shard_map/ppermute | solution.py:691
  124.6 68.5 %collective-permute-start.21 = (bf16[2,2,256,256]{3,2,1,0:T(8,128)(2,1)S(1)}, bf16[2,2,256,256]{3,2,1,0:T(8,128)(2,1)S(1)}, u32[]{:S(2)}, u32[]{:S(2)}) collective-permute-start(bf16[2,2,256,256]{3,2,1,0:T(8,128)(2,1)S(1)} %copy-done.40), channel_id=1, source_target_pairs={{0,20},{1,21},{2,22},{3,23},{4,16},{5,17},{6,18},{7,19},{16,4},{17... | collective-permute-start | bytes 1572872 | tf_op jit(solution)/shard_map/ppermute | solution.py:691
  170.7 29.1 %collective-permute-start.16 = (bf16[2,2,256,256]{3,2,1,0:T(8,128)(2,1)S(1)}, bf16[2,2,256,256]{3,2,1,0:T(8,128)(2,1)S(1)}, u32[]{:S(2)}, u32[]{:S(2)}) collective-permute-start(bf16[2,2,256,256]{3,2,1,0:T(8,128)(2,1)S(1)} %copy-done.39), channel_id=1, source_target_pairs={{0,2},{1,3},{2,0},{3,1},{4,6},{5,7},{6,4},{7,5},{16,18},{17,19},{1... | collective-permute-start | bytes 1572872 | tf_op jit(solution)/shard_map/ppermute | solution.py:691
  172.2 31.6 %collective-permute-start.22 = (bf16[2,2,256,256]{3,2,1,0:T(8,128)(2,1)S(1)}, bf16[2,2,256,256]{3,2,1,0:T(8,128)(2,1)S(1)}, u32[]{:S(2)}, u32[]{:S(2)}) collective-permute-start(bf16[2,2,256,256]{3,2,1,0:T(8,128)(2,1)S(1)} %copy-done.38), channel_id=1, source_target_pairs={{0,22},{1,23},{2,20},{3,21},{4,18},{5,19},{6,16},{7,17},{16,6},{17... | collective-permute-start | bytes 1572872 | tf_op jit(solution)/shard_map/ppermute | solution.py:691
  173.4 41.3 %collective-permute-start.9 = (bf16[8,256,256]{2,1,0:T(8,128)(2,1)}, bf16[8,256,256]{2,1,0:T(8,128)(2,1)S(1)}, u32[]{:S(2)}, u32[]{:S(2)}) collective-permute-start(bf16[8,256,256]{2,1,0:T(8,128)(2,1)} %get-tuple-element.159), channel_id=1, source_target_pairs={{0,1},{1,8},{8,9},{2,3},{3,10},{10,11},{4,5},{5,12},{12,13},{6,7},... | collective-permute-start | bytes 3145736 | tf_op jit(solution)/shard_map/ppermute | solution.py:694
  177.3 37.4 %collective-permute-start.10 = (bf16[8,256,256]{2,1,0:T(8,128)(2,1)}, bf16[8,256,256]{2,1,0:T(8,128)(2,1)S(1)}, u32[]{:S(2)}, u32[]{:S(2)}) collective-permute-start(bf16[8,256,256]{2,1,0:T(8,128)(2,1)} %get-tuple-element.160), channel_id=1, source_target_pairs={{1,0},{8,1},{9,8},{3,2},{10,3},{11,10},{5,4},{12,5},{13,12},{7,6},... | collective-permute-start | bytes 3145736 | tf_op jit(solution)/shard_map/ppermute | solution.py:694
  207.8 18.0 %collective-permute-start.23 = (bf16[8,256,256]{2,1,0:T(8,128)(2,1)}, bf16[8,256,256]{2,1,0:T(8,128)(2,1)S(1)}, u32[]{:S(2)}, u32[]{:S(2)}) collective-permute-start(bf16[8,256,256]{2,1,0:T(8,128)(2,1)} %get-tuple-element.184), channel_id=1, source_target_pairs={{0,1},{1,8},{8,9},{2,3},{3,10},{10,11},{4,5},{5,12},{12,13},{6,7},... | collective-permute-start | bytes 3145736 | tf_op jit(solution)/shard_map/ppermute | solution.py:694
  221.5 53.7 %collective-permute-start.11 = (bf16[2,256,384]{2,1,0:T(8,128)(2,1)}, bf16[2,256,384]{2,1,0:T(8,128)(2,1)S(1)}, u32[]{:S(2)}, u32[]{:S(2)}) collective-permute-start(bf16[2,256,384]{2,1,0:T(8,128)(2,1)} %get-tuple-element.169), channel_id=1, source_target_pairs={{0,4},{1,5},{2,6},{3,7},{4,0},{5,1},{6,2},{7,3},{16,20},{17,21},{1... | collective-permute-start | bytes 1179656 | tf_op jit(solution)/shard_map/ppermute | solution.py:691
  221.5 53.7 %collective-permute-start.12 = (bf16[2,256,384]{2,1,0:T(8,128)(2,1)}, bf16[2,256,384]{2,1,0:T(8,128)(2,1)S(1)}, u32[]{:S(2)}, u32[]{:S(2)}) collective-permute-start(bf16[2,256,384]{2,1,0:T(8,128)(2,1)} %get-tuple-element.170), channel_id=1, source_target_pairs={{0,6},{1,7},{2,4},{3,5},{4,2},{5,3},{6,0},{7,1},{16,22},{17,23},{1... | collective-permute-start | bytes 1179656 | tf_op jit(solution)/shard_map/ppermute | solution.py:691
  221.7 53.5 %collective-permute-start.13 = (bf16[2,256,384]{2,1,0:T(8,128)(2,1)}, bf16[2,256,384]{2,1,0:T(8,128)(2,1)S(1)}, u32[]{:S(2)}, u32[]{:S(2)}) collective-permute-start(bf16[2,256,384]{2,1,0:T(8,128)(2,1)} %get-tuple-element.171), channel_id=1, source_target_pairs={{0,20},{1,21},{2,22},{3,23},{4,16},{5,17},{6,18},{7,19},{16,4},{17... | collective-permute-start | bytes 1179656 | tf_op jit(solution)/shard_map/ppermute | solution.py:691
  225.8 49.4 %collective-permute-start.14 = (bf16[2,256,384]{2,1,0:T(8,128)(2,1)}, bf16[2,256,384]{2,1,0:T(8,128)(2,1)S(1)}, u32[]{:S(2)}, u32[]{:S(2)}) collective-permute-start(bf16[2,256,384]{2,1,0:T(8,128)(2,1)} %get-tuple-element.172), channel_id=1, source_target_pairs={{0,16},{1,17},{2,18},{3,19},{4,20},{5,21},{6,22},{7,23},{16,0},{17... | collective-permute-start | bytes 1179656 | tf_op jit(solution)/shard_map/ppermute | solution.py:691
  229.2 46.1 %collective-permute-start.15 = (bf16[2,256,384]{2,1,0:T(8,128)(2,1)}, bf16[2,256,384]{2,1,0:T(8,128)(2,1)S(1)}, u32[]{:S(2)}, u32[]{:S(2)}) collective-permute-start(bf16[2,256,384]{2,1,0:T(8,128)(2,1)} %get-tuple-element.173), channel_id=1, source_target_pairs={{0,18},{1,19},{2,16},{3,17},{4,22},{5,23},{6,20},{7,21},{16,2},{17... | collective-permute-start | bytes 1179656 | tf_op jit(solution)/shard_map/ppermute | solution.py:691
  279.7 22.7 %collective-permute-start.34 = (bf16[2,256,384]{2,1,0:T(8,128)(2,1)S(1)}, bf16[2,256,384]{2,1,0:T(8,128)(2,1)S(1)}, u32[]{:S(2)}, u32[]{:S(2)}) collective-permute-start(bf16[2,256,384]{2,1,0:T(8,128)(2,1)S(1)} %copy-done.43), channel_id=1, source_target_pairs={{0,2},{1,3},{2,0},{3,1},{4,6},{5,7},{6,4},{7,5},{16,18},{17,19},{1... | collective-permute-start | bytes 1179656 | tf_op jit(solution)/shard_map/ppermute | solution.py:691
  281.2 22.3 %collective-permute-start.35 = (bf16[2,256,384]{2,1,0:T(8,128)(2,1)S(1)}, bf16[2,256,384]{2,1,0:T(8,128)(2,1)S(1)}, u32[]{:S(2)}, u32[]{:S(2)}) collective-permute-start(bf16[2,256,384]{2,1,0:T(8,128)(2,1)S(1)} %copy-done.42), channel_id=1, source_target_pairs={{0,22},{1,23},{2,20},{3,21},{4,18},{5,19},{6,16},{7,17},{16,6},{17... | collective-permute-start | bytes 1179656 | tf_op jit(solution)/shard_map/ppermute | solution.py:691
  299.6 18.7 %collective-permute-start.27 = (bf16[2,256,384]{2,1,0:T(8,128)(2,1)}, bf16[2,256,384]{2,1,0:T(8,128)(2,1)S(1)}, u32[]{:S(2)}, u32[]{:S(2)}) collective-permute-start(bf16[2,256,384]{2,1,0:T(8,128)(2,1)} %get-tuple-element.220), channel_id=1, source_target_pairs={{0,2},{1,3},{2,0},{3,1},{4,6},{5,7},{6,4},{7,5},{16,18},{17,19},{1... | collective-permute-start | bytes 1179656 | tf_op jit(solution)/shard_map/ppermute | solution.py:691
  301.0 27.3 %collective-permute-start.28 = (bf16[2,256,384]{2,1,0:T(8,128)(2,1)}, bf16[2,256,384]{2,1,0:T(8,128)(2,1)S(1)}, u32[]{:S(2)}, u32[]{:S(2)}) collective-permute-start(bf16[2,256,384]{2,1,0:T(8,128)(2,1)} %get-tuple-element.221), channel_id=1, source_target_pairs={{0,4},{1,5},{2,6},{3,7},{4,0},{5,1},{6,2},{7,3},{16,20},{17,21},{1... | collective-permute-start | bytes 1179656 | tf_op jit(solution)/shard_map/ppermute | solution.py:691
  302.1 51.6 %collective-permute-start.29 = (bf16[2,256,384]{2,1,0:T(8,128)(2,1)}, bf16[2,256,384]{2,1,0:T(8,128)(2,1)S(1)}, u32[]{:S(2)}, u32[]{:S(2)}) collective-permute-start(bf16[2,256,384]{2,1,0:T(8,128)(2,1)} %get-tuple-element.222), channel_id=1, source_target_pairs={{0,6},{1,7},{2,4},{3,5},{4,2},{5,3},{6,0},{7,1},{16,22},{17,23},{1... | collective-permute-start | bytes 1179656 | tf_op jit(solution)/shard_map/ppermute | solution.py:691
  302.3 51.4 %collective-permute-start.30 = (bf16[2,256,384]{2,1,0:T(8,128)(2,1)}, bf16[2,256,384]{2,1,0:T(8,128)(2,1)S(1)}, u32[]{:S(2)}, u32[]{:S(2)}) collective-permute-start(bf16[2,256,384]{2,1,0:T(8,128)(2,1)} %get-tuple-element.223), channel_id=1, source_target_pairs={{0,16},{1,17},{2,18},{3,19},{4,20},{5,21},{6,22},{7,23},{16,0},{17... | collective-permute-start | bytes 1179656 | tf_op jit(solution)/shard_map/ppermute | solution.py:691
  303.4 50.3 %collective-permute-start.31 = (bf16[2,256,384]{2,1,0:T(8,128)(2,1)}, bf16[2,256,384]{2,1,0:T(8,128)(2,1)S(1)}, u32[]{:S(2)}, u32[]{:S(2)}) collective-permute-start(bf16[2,256,384]{2,1,0:T(8,128)(2,1)} %get-tuple-element.224), channel_id=1, source_target_pairs={{0,18},{1,19},{2,16},{3,17},{4,22},{5,23},{6,20},{7,21},{16,2},{17... | collective-permute-start | bytes 1179656 | tf_op jit(solution)/shard_map/ppermute | solution.py:691
  318.2 43.8 %collective-permute-start.32 = (bf16[2,256,384]{2,1,0:T(8,128)(2,1)}, bf16[2,256,384]{2,1,0:T(8,128)(2,1)S(1)}, u32[]{:S(2)}, u32[]{:S(2)}) collective-permute-start(bf16[2,256,384]{2,1,0:T(8,128)(2,1)} %get-tuple-element.225), channel_id=1, source_target_pairs={{0,20},{1,21},{2,22},{3,23},{4,16},{5,17},{6,18},{7,19},{16,4},{17... | collective-permute-start | bytes 1179656 | tf_op jit(solution)/shard_map/ppermute | solution.py:691
  328.3 40.5 %collective-permute-start.33 = (bf16[2,256,384]{2,1,0:T(8,128)(2,1)}, bf16[2,256,384]{2,1,0:T(8,128)(2,1)S(1)}, u32[]{:S(2)}, u32[]{:S(2)}) collective-permute-start(bf16[2,256,384]{2,1,0:T(8,128)(2,1)} %get-tuple-element.226), channel_id=1, source_target_pairs={{0,22},{1,23},{2,20},{3,21},{4,18},{5,19},{6,16},{7,17},{16,6},{17... | collective-permute-start | bytes 1179656 | tf_op jit(solution)/shard_map/ppermute | solution.py:691
  (48 other events, 1267.2 us)

commit v4 on v3

--- a/solution.py
+++ b/solution.py
@@ -277,6 +277,8 @@
 
 TOK = TILE * TILE
 SPAN = 3
+SLOTS = 4
+PLAN = ((1, 0), (1, 1), (1, 2), (1, 3), (2, 0), (2, 1), (2, 2), (2, 3), (3, 0), (3, 1), (3, 2), (3, 3))
 LANES = 2 * D_HEAD
 LINES = TW * TOK
 LOG2_E = 1.4426950408889634
@@ -352,42 +354,30 @@
     )(place, *arrays)
 
 
-def join_kernel(places, turn, widths, kept, place_ref, *refs):
-    count = len(widths)
-    groups = [refs[n * places : (n + 1) * places] for n in range(count)]
-    refs = refs[count * places + kept :]
-    outs, taken, (ready, in_sem, out_sem) = refs[:3], refs[3 : 3 + count], refs[3 + count :]
-    turns = HEADS // places
+def join_kernel(seats, turn, turns, kept, place_ref, *refs):
+    count = len(seats)
+    blocks, outs = refs[:count], refs[count + kept : count + kept + 3]
+    taken, ready, in_sem, out_sem = refs[count + kept + 3 :]
     loads = []
-    for k in range(places):
-        loads.append(
-            [
-                pltpu.make_async_copy(groups[n][k], taken[n].at[k], in_sem.at[k, n])
-                for n in range(count)
-            ]
-        )
-        for copy in loads[k]:
-            copy.start()
+    for n in range(count):
+        loads.append(pltpu.make_async_copy(blocks[n], taken.at[n], in_sem.at[n]))
+        loads[n].start()
     order = row_order(True)
     stores = []
-    for k in range(places):
-        for copy in loads[k]:
-            copy.wait()
+    for n, k in enumerate(seats):
+        loads[n].wait()
         for row in range(2):
-            which = 0
-            for n in range(count):
-                back = lax.dot_general(
-                    order, taken[n][k, row], NN, preferred_element_type=jnp.float32
-                ).astype(jnp.bfloat16)
-                for lane in range(0, widths[n], D_HEAD):
-                    ready[k, which, row * LINES : (row + 1) * LINES, :] = back[
-                        :, lane : lane + D_HEAD
-                    ]
-                    which += 1
+            back = lax.dot_general(
+                order, taken[n, row], NN, preferred_element_type=jnp.float32
+            ).astype(jnp.bfloat16)
+            for which in range(3):
+                ready[n, which, row * LINES : (row + 1) * LINES, :] = back[
+                    :, which * D_HEAD : (which + 1) * D_HEAD
+                ]
         first = pl.multiple_of(((place_ref[0] ^ k) * turns + turn) * D_HEAD, D_HEAD)
         for which in range(3):
             copy = pltpu.make_async_copy(
-                ready.at[k, which], outs[which].at[:, pl.ds(first, D_HEAD)], out_sem.at[k, which]
+                ready.at[n, which], outs[which].at[:, pl.ds(first, D_HEAD)], out_sem.at[n, which]
             )
             copy.start()
             stores.append(copy)
@@ -395,24 +385,22 @@
         copy.wait()
 
 
-def join_heads(places, turn, place, groups, earlier):
-    rows = 2 * LINES
-    widths = [group[0].shape[-1] for group in groups]
-    count = len(widths)
+def join_heads(seats, turn, turns, place, blocks, earlier):
+    count, rows, lanes = len(seats), 2 * LINES, blocks[0].shape[-1]
     return pl.pallas_call(
-        lambda *refs: join_kernel(places, turn, widths, len(earlier), *refs),
-        in_specs=[SCALARS] + [ANYWHERE] * (count * places + len(earlier)),
+        lambda *refs: join_kernel(seats, turn, turns, len(earlier), *refs),
+        in_specs=[SCALARS] + [ANYWHERE] * (count + len(earlier)),
         out_specs=[ANYWHERE] * 3,
         out_shape=[jax.ShapeDtypeStruct((rows, HEADS * D_HEAD), jnp.bfloat16)] * 3,
-        scratch_shapes=[pltpu.VMEM((places, 2, LINES, width), jnp.bfloat16) for width in widths]
-        + [
-            pltpu.VMEM((places, 3, rows, D_HEAD), jnp.bfloat16),
-            pltpu.SemaphoreType.DMA((places, count)),
-            pltpu.SemaphoreType.DMA((places, 3)),
+        scratch_shapes=[
+            pltpu.VMEM((count, 2, LINES, lanes), jnp.bfloat16),
+            pltpu.VMEM((count, 3, rows, D_HEAD), jnp.bfloat16),
+            pltpu.SemaphoreType.DMA((count,)),
+            pltpu.SemaphoreType.DMA((count, 3)),
         ],
-        input_output_aliases={1 + count * places + n: n for n in range(len(earlier))},
+        input_output_aliases={1 + count + n: n for n in range(len(earlier))},
         compiler_params=PARAMS,
-    )(place, *[block for group in groups for block in group], *earlier)
+    )(place, *blocks, *earlier)
 
 
 def edge_kernel(places, *refs):
@@ -473,106 +461,108 @@
             lines.append(jnp.concatenate(line, axis=1))
         return jnp.concatenate(lines, axis=0)
 
-    def group(col, _):
+    def near_keys(row, near, windows, lanes):
+        return jnp.concatenate(
+            [kv[row + near, :, :, window, lanes].reshape(part, D_HEAD) for window in windows],
+            axis=1,
+        )
+
+    def score_phase(slot, row, col):
         here = pl.multiple_of(col * TOK, TOK)
-        queries, grads, windows, tops = [], [], [], []
-
-        def near_keys(row, near, lanes):
-            return jnp.concatenate(
-                [
-                    kv[row + near, :, :, window, lanes].reshape(part, D_HEAD)
-                    for window in windows[row]
-                ],
-                axis=1,
+        windows = [
+            pl.ds(pl.multiple_of(start_ref[(row * TW + col) * frames + f] * TOK, TOK), piece)
+            for f in range(frames)
+        ]
+        own = own_rows[row, :, :, pl.ds(here, TOK), :].reshape(-1, LANES)
+        query, grad = diagonal(own[:, :D_HEAD]), diagonal(own[:, D_HEAD:])
+        top = None
+        for near in range(3):
+            score_raw = lax.dot_general(
+                near_keys(row, near, windows, slice(0, D_HEAD)), query, NT,
+                preferred_element_type=jnp.float32,
             )
-
-        for row in range(2):
-            windows.append(
-                [
-                    pl.ds(pl.multiple_of(start_ref[(row * TW + col) * frames + f] * TOK, TOK), piece)
-                    for f in range(frames)
-                ]
+            scores[slot, near, :, D_HEAD:] = lax.dot_general(
+                near_keys(row, near, windows, slice(D_HEAD, LANES)), grad, NT,
+                preferred_element_type=jnp.float32,
             )
-            own = own_rows[row, :, :, pl.ds(here, TOK), :].reshape(-1, LANES)
-            queries.append(diagonal(own[:, :D_HEAD]))
-            grads.append(diagonal(own[:, D_HEAD:]))
-            top = None
-            for near in range(3):
-                score_raw = lax.dot_general(
-                    near_keys(row, near, slice(0, D_HEAD)), queries[row], NT,
-                    preferred_element_type=jnp.float32,
+            for frame in range(frames):
+                first = (near * frames + frame) * SPAN
+                bias = jnp.concatenate(
+                    [
+                        jnp.broadcast_to(
+                            bias_ref[row, col, first + c : first + c + 1, :], (TOK, D_HEAD)
+                        )
+                        for c in range(SPAN)
+                    ],
+                    axis=0,
                 )
-                scores[row, near, :, D_HEAD:] = lax.dot_general(
-                    near_keys(row, near, slice(D_HEAD, LANES)), grads[row], NT,
-                    preferred_element_type=jnp.float32,
-                )
-                for frame in range(frames):
-                    first = (near * frames + frame) * SPAN
-                    bias = jnp.concatenate(
-                        [
-                            jnp.broadcast_to(
-                                bias_ref[row, col, first + c : first + c + 1, :], (TOK, D_HEAD)
-                            )
-                            for c in range(SPAN)
-                        ],
-                        axis=0,
-                    )
-                    for sub in range(TILE):
-                        at = (frame * TILE + sub) * piece
-                        score = score_raw[at : at + piece, :] * (scale * LOG2_E) + bias
-                        scores[row, near, at : at + piece, :D_HEAD] = score
-                        most = jnp.max(score.reshape(-1, 8, D_HEAD), axis=0)
-                        top = most if top is None else jnp.maximum(top, most)
-            tops.append(jnp.max(top, axis=0, keepdims=True))
-        sums = []
-        for row in range(2):
-            total = jnp.zeros((8, D_HEAD), jnp.float32)
-            delta = jnp.zeros((8, D_HEAD), jnp.float32)
-            for near in range(3):
-                for at in range(0, part, piece):
-                    prob = jnp.exp2(scores[row, near, at : at + piece, :D_HEAD] - tops[row])
-                    total = total + jnp.sum(prob.reshape(-1, 8, D_HEAD), axis=0)
-                    grad = prob * scores[row, near, at : at + piece, D_HEAD:]
-                    delta = delta + jnp.sum(grad.reshape(-1, 8, D_HEAD), axis=0)
-            total = jnp.sum(total, axis=0, keepdims=True)
-            delta = jnp.sum(delta, axis=0, keepdims=True) / total
-            sums.append((tops[row] + jnp.log2(total), delta))
-        for row in range(2):
-            log_total, delta = sums[row]
-            query_grad = None
-            for near in range(3):
-                for at in range(0, part, piece):
-                    weight = jnp.exp2(scores[row, near, at : at + piece, :D_HEAD] - log_total)
-                    dscore = weight * (scores[row, near, at : at + piece, D_HEAD:] - delta)
-                    low[row, near, at : at + piece, :D_HEAD] = dscore.astype(jnp.bfloat16)
-                    low[row, near, at : at + piece, D_HEAD:] = weight.astype(jnp.bfloat16)
-                key_part = lax.dot_general(
-                    low[row, near, :, :D_HEAD], queries[row], NN, preferred_element_type=jnp.float32
-                )
-                value_part = lax.dot_general(
-                    low[row, near, :, D_HEAD:], grads[row], NN, preferred_element_type=jnp.float32
-                )
-                for f in range(frames):
-                    lanes = slice(f * D_HEAD, (f + 1) * D_HEAD)
-                    added = jnp.concatenate([key_part[:, lanes], value_part[:, lanes]], axis=1)
-                    spot = (row + near, slice(None), slice(None), windows[row][f], slice(None))
-                    acc[spot] = acc[spot] + added.reshape(frames, TILE, piece, LANES)
-                more = lax.dot_general(
-                    low[row, near, :, :D_HEAD],
-                    near_keys(row, near, slice(0, D_HEAD)),
-                    TN,
-                    preferred_element_type=jnp.float32,
-                )
-                query_grad = more if query_grad is None else query_grad + more
+                for sub in range(TILE):
+                    at = (frame * TILE + sub) * piece
+                    score = score_raw[at : at + piece, :] * (scale * LOG2_E) + bias
+                    scores[slot, near, at : at + piece, :D_HEAD] = score
+                    most = jnp.max(score.reshape(-1, 8, D_HEAD), axis=0)
+                    top = most if top is None else jnp.maximum(top, most)
+        return here, windows, query, grad, jnp.max(top, axis=0, keepdims=True)
+
+    def total_phase(slot, top):
+        total = jnp.zeros((8, D_HEAD), jnp.float32)
+        delta = jnp.zeros((8, D_HEAD), jnp.float32)
+        for near in range(3):
+            for at in range(0, part, piece):
+                prob = jnp.exp2(scores[slot, near, at : at + piece, :D_HEAD] - top)
+                total = total + jnp.sum(prob.reshape(-1, 8, D_HEAD), axis=0)
+                grad = prob * scores[slot, near, at : at + piece, D_HEAD:]
+                delta = delta + jnp.sum(grad.reshape(-1, 8, D_HEAD), axis=0)
+        total = jnp.sum(total, axis=0, keepdims=True)
+        delta = jnp.sum(delta, axis=0, keepdims=True) / total
+        return top + jnp.log2(total), delta
+
+    def grad_phase(slot, row, here, windows, query, grad, log_total, delta):
+        query_grad = None
+        for near in range(3):
+            for at in range(0, part, piece):
+                weight = jnp.exp2(scores[slot, near, at : at + piece, :D_HEAD] - log_total)
+                dscore = weight * (scores[slot, near, at : at + piece, D_HEAD:] - delta)
+                low[slot, near, at : at + piece, :D_HEAD] = dscore.astype(jnp.bfloat16)
+                low[slot, near, at : at + piece, D_HEAD:] = weight.astype(jnp.bfloat16)
+            key_part = lax.dot_general(
+                low[slot, near, :, :D_HEAD], query, NN, preferred_element_type=jnp.float32
+            )
+            value_part = lax.dot_general(
+                low[slot, near, :, D_HEAD:], grad, NN, preferred_element_type=jnp.float32
+            )
             for f in range(frames):
-                cells = query_grad.shape[0] // frames
-                mine = query_grad[f * cells : (f + 1) * cells, f * D_HEAD : (f + 1) * D_HEAD]
-                dq[row, f, :, pl.ds(here, TOK), :] = (
-                    (mine * scale).astype(jnp.bfloat16).reshape(TILE, TOK, D_HEAD)
-                )
+                lanes = slice(f * D_HEAD, (f + 1) * D_HEAD)
+                added = jnp.concatenate([key_part[:, lanes], value_part[:, lanes]], axis=1)
+                spot = (row + near, slice(None), slice(None), windows[f], slice(None))
+                acc[spot] = acc[spot] + added.reshape(frames, TILE, piece, LANES)
+            more = lax.dot_general(
+                low[slot, near, :, :D_HEAD],
+                near_keys(row, near, windows, slice(0, D_HEAD)),
+                TN,
+                preferred_element_type=jnp.float32,
+            )
+            query_grad = more if query_grad is None else query_grad + more
+        for f in range(frames):
+            cells = query_grad.shape[0] // frames
+            mine = query_grad[f * cells : (f + 1) * cells, f * D_HEAD : (f + 1) * D_HEAD]
+            dq[row, f, :, pl.ds(here, TOK), :] = (
+                (mine * scale).astype(jnp.bfloat16).reshape(TILE, TOK, D_HEAD)
+            )
+
+    def group(step, _):
+        known, sums = {}, {}
+        for phase, slot in PLAN:
+            row = slot % 2
+            if phase == 1:
+                known[slot] = score_phase(slot, row, step * (SLOTS // 2) + slot // 2)
+            elif phase == 2:
+                sums[slot] = total_phase(slot, known[slot][-1])
+            else:
+                grad_phase(slot, row, *known[slot][:-1], *sums[slot])
         return 0
 
-    lax.fori_loop(0, TW, group, 0)
+    lax.fori_loop(0, 2 * TW // SLOTS, group, 0)
     copies = []
     for k in range(places):
         seat = place_ref[0] ^ k
@@ -607,15 +597,15 @@
             pltpu.VMEM((2, frames, TILE, LINES, LANES), jnp.bfloat16),
             pltpu.VMEM((4, frames, TILE, LINES, LANES), jnp.float32),
             pltpu.VMEM((2, frames, TILE, LINES, D_HEAD), jnp.bfloat16),
-            pltpu.VMEM((2, 3, part, LANES), jnp.float32),
-            pltpu.VMEM((2, 3, part, LANES), jnp.bfloat16),
+            pltpu.VMEM((SLOTS, 3, part, LANES), jnp.float32),
+            pltpu.VMEM((SLOTS, 3, part, LANES), jnp.bfloat16),
             pltpu.SemaphoreType.DMA((places, 2)),
             pltpu.SemaphoreType.DMA((places, 2)),
             pltpu.SemaphoreType.DMA((places, 2)),
         ],
         compiler_params=PARAMS,
         cost_estimate=pl.CostEstimate(
-            flops=60_000_000_000, bytes_accessed=0, transcendentals=0
+            flops=1_000_000, bytes_accessed=0, transcendentals=0
         ),
     )(place, starts, bias, *[block for group in groups for block in group], from_above, from_below)
     return results[:places], *results[places:]
@@ -737,13 +727,15 @@
             passed, grads = ordered([left[k] for k in mixed[:-2]], grads)
             for k, block in zip(mixed, passed):
                 left[k] = block
-            outs = join_heads(places, turn - 1, place, [left], outs)
+            outs = join_heads(range(places), turn - 1, turns, place, left, outs)
         if more:
             coming, grads = after(coming, grads)
             groups = [exchange(coming, mixed)]
         dq, acc, above, below = grads
         leaving = finish_pairs(places, acc, step(below, down), step(above, up), dq)
-    outs = join_heads(places, turns - 1, place, [exchange(leaving, natural)], outs)
+    left = exchange(leaving, natural)
+    for seats in (range(places - 2), range(places - 2, places)):
+        outs = join_heads(seats, turns - 1, turns, place, [left[k] for k in seats], outs)
     key_out, value_out, query_out = outs
     return query_out, key_out, value_out
 

time: 374 us -> 370 us (0.989)
  waiting for transfers between devices: 185 us -> 179 us
    ppermute x28, waiting for transfers between devices: 160 us -> 157 us  [send(): lax.ppermute(block, ('tm', 'seq'), [(i, i ^ 2 * k) for i in range(2 * pla...]
    pallas_call x2 -> x3, Pallas kernels: 8.77 us -> 10.6 us  [join_heads(): pl.pallas_call(lambda *refs: join_kernel(seats, turn, turns, len(earlier)...]
  transfers between devices with their start and end apart: 36 -> 36, of which waited for: 17 -> 17; matrix products, arithmetic and copies ran while one was open for 1% -> 1% of each run, Pallas kernels for 30% -> 31%
where the time goes in v4:
time: 370 us
  waiting for transfers between devices  179 us (48%)
  Pallas kernels  123 us (33%)
  starting transfers between devices  54.7 us (15%)
  local copies, waits for them, and re-layouts  10.8 us (3%)
    ppermute x28, waiting for transfers between devices, send(): lax.ppermute(block, ('tm', 'seq'), [(i, i ^ 2 * k) for i in range(2 * pla...  157 us
    pallas_call x2, Pallas kernels, head_grads(): pl.pallas_call(lambda *refs: grad_kernel(places, len(groups), *refs), in_...  87.1 us
    ppermute x28, starting transfers between devices, send(): lax.ppermute(block, ('tm', 'seq'), [(i, i ^ 2 * k) for i in range(2 * pla...  30.4 us
    ppermute x8, starting transfers between devices, step(): return lax.ppermute(block, ('height', 'seq'), route)  24.4 us
    ppermute x8, waiting for transfers between devices, step(): return lax.ppermute(block, ('height', 'seq'), route)  22.7 us
    pallas_call x3, Pallas kernels, join_heads(): pl.pallas_call(lambda *refs: join_kernel(seats, turn, turns, len(earlier)...  10.6 us
    pallas_call x2, Pallas kernels, finish_pairs(): pl.pallas_call(lambda *refs: finish_kernel(places, *refs), in_specs=[WHOL...  9.62 us
    pallas_call x2, Pallas kernels, split_heads(): pl.pallas_call(lambda *refs: split_kernel(places, turn, pairs, *refs), in...  9.56 us
  transfers between devices with their start and end apart: 36, of which 17 were waited for; matrix products, arithmetic and copies ran while one was open for 1% of the time, Pallas kernels for 31%

profile of v4, /device:TPU:9, one launch (start us, length us, event | category | flops | bytes accessed | tf_op | source)
XLA Modules:
  0.0 369.5 jit_solution(12659715351104715075)
XLA Ops:
  0.6 4.8 %shard_map.85 = (bf16[2,2,256,256]{3,2,1,0:T(8,128)(2,1)}, bf16[2,2,256,256]{3,2,1,0:T(8,128)(2,1)}, bf16[2,2,256,256]{3,2,1,0:T(8,128)(2,1)}, bf16[2,2,256,256]...) custom-call(s32[1]{0:T(128)} %bitcast.refs_0_, ...), custom_call_target="tpu_custom_call" | custom-call | tf_op jit(solution)/shard_map/pallas_call | solution.py:342
  10.5 4.8 %shard_map.86 = (bf16[2,2,256,256]{3,2,1,0:T(8,128)(2,1)}, bf16[2,2,256,256]{3,2,1,0:T(8,128)(2,1)}, bf16[2,2,256,256]{3,2,1,0:T(8,128)(2,1)}, bf16[2,2,256,256]...) custom-call(s32[1]{0:T(128)} %bitcast.refs_0_, ...), custom_call_target="tpu_custom_call" | custom-call | tf_op jit(solution)/shard_map/pallas_call | solution.py:342
  15.3 11.9 %collective-permute-done.refs_1_.refs_4_ = bf16[2,2,256,256]{3,2,1,0:T(8,128)(2,1)S(1)} collective-permute-done((bf16[2,2,256,256]{3,2,1,0:T(8,128)(2,1)}, bf16[2,2,256,256]{3,2,1,0:T(8,128)(2,1)S(1)}, u32[]{:S(2)}, u32[]{:S(2)}) %collective-permute-start) | collective-permute-done | bytes 524320 | tf_op jit(solution)/shard_map/ppermute | solution.py:681
  27.2 4.5 %collective-permute-start.5 = (bf16[2,2,256,256]{3,2,1,0:T(8,128)(2,1)}, bf16[2,2,256,256]{3,2,1,0:T(8,128)(2,1)S(1)}, u32[]{:S(2)}, u32[]{:S(2)}) collective-permute-start(bf16[2,2,256,256]{3,2,1,0:T(8,128)(2,1)} %get-tuple-element.146), channel_id=1, source_target_pairs={{0,20},{1,21},{2,22},{3,23},{4,16},{5,17},{6,18},{7,19},{16,4},{17... | collective-permute-start | bytes 1572872 | tf_op jit(solution)/shard_map/ppermute | solution.py:681
  31.9 21.3 %collective-permute-done.2.refs_3_.refs_6_ = bf16[2,2,256,256]{3,2,1,0:T(8,128)(2,1)S(1)} collective-permute-done((bf16[2,2,256,256]{3,2,1,0:T(8,128)(2,1)}, bf16[2,2,256,256]{3,2,1,0:T(8,128)(2,1)S(1)}, u32[]{:S(2)}, u32[]{:S(2)}) %collective-permute-start.2) | collective-permute-done | bytes 524320 | tf_op jit(solution)/shard_map/ppermute | solution.py:681
  53.2 32.9 %collective-permute-done.5.refs_6_.refs_9_ = bf16[2,2,256,256]{3,2,1,0:T(8,128)(2,1)S(1)} collective-permute-done((bf16[2,2,256,256]{3,2,1,0:T(8,128)(2,1)}, bf16[2,2,256,256]{3,2,1,0:T(8,128)(2,1)S(1)}, u32[]{:S(2)}, u32[]{:S(2)}) %collective-permute-start.5) | collective-permute-done | bytes 524320 | tf_op jit(solution)/shard_map/ppermute | solution.py:681
  86.1 13.0 %collective-permute-done.6.refs_7_.refs_10_ = bf16[2,2,256,256]{3,2,1,0:T(8,128)(2,1)S(1)} collective-permute-done((bf16[2,2,256,256]{3,2,1,0:T(8,128)(2,1)S(1)}, bf16[2,2,256,256]{3,2,1,0:T(8,128)(2,1)S(1)}, u32[]{:S(2)}, u32[]{:S(2)}) %collective-permute-start.6) | collective-permute-done | bytes 524320 | tf_op jit(solution)/shard_map/ppermute | solution.py:681
  99.9 3.1 shard_map.87
  103.0 5.0 %collective-permute-start.7 = (bf16[8,256,256]{2,1,0:T(8,128)(2,1)}, bf16[8,256,256]{2,1,0:T(8,128)(2,1)S(1)}, u32[]{:S(2)}, u32[]{:S(2)}) collective-permute-start(bf16[8,256,256]{2,1,0:T(8,128)(2,1)} %get-tuple-element.148), channel_id=1, source_target_pairs={{0,1},{1,8},{8,9},{2,3},{3,10},{10,11},{4,5},{5,12},{12,13},{6,7},... | collective-permute-start | bytes 3145736 | tf_op jit(solution)/shard_map/ppermute | solution.py:684
  115.5 4.5 %collective-permute-done.7.refs_11_ = bf16[8,256,256]{2,1,0:T(8,128)(2,1)S(1)} collective-permute-done((bf16[8,256,256]{2,1,0:T(8,128)(2,1)}, bf16[8,256,256]{2,1,0:T(8,128)(2,1)S(1)}, u32[]{:S(2)}, u32[]{:S(2)}) %collective-permute-start.7) | collective-permute-done | bytes 1048608 | tf_op jit(solution)/shard_map/ppermute | solution.py:684
  120.0 4.6 %collective-permute-done.8.refs_12_ = bf16[8,256,256]{2,1,0:T(8,128)(2,1)} collective-permute-done((bf16[8,256,256]{2,1,0:T(8,128)(2,1)}, bf16[8,256,256]{2,1,0:T(8,128)(2,1)}, u32[]{:S(2)}, u32[]{:S(2)}) %collective-permute-start.8) | collective-permute-done | bytes 1048608 | tf_op jit(solution)/shard_map/ppermute | solution.py:684
  124.6 43.5 %shard_map.88 = (bf16[2,256,128]{2,1,0:T(8,128)(2,1)}, bf16[2,256,128]{2,1,0:T(8,128)(2,1)}, bf16[2,256,128]{2,1,0:T(8,128)(2,1)}, bf16[2,256,128]{2,1,0:T(8,128...) custom-call(s32[1]{0:T(128)} %bitcast.refs_0_, ...), custom_call_target="tpu_custom_call" | custom-call | flops 1000000 | tf_op jit(solution)/shard_map/pallas_call | solution.py:588
  171.8 3.1 collective-permute-start.9
  176.9 14.1 %collective-permute-done.21.refs_6_.refs_9_ = bf16[2,2,256,256]{3,2,1,0:T(8,128)(2,1)S(1)} collective-permute-done((bf16[2,2,256,256]{3,2,1,0:T(8,128)(2,1)}, bf16[2,2,256,256]{3,2,1,0:T(8,128)(2,1)S(1)}, u32[]{:S(2)}, u32[]{:S(2)}) %collective-permute-start.21) | collective-permute-done | bytes 524320 | tf_op jit(solution)/shard_map/ppermute | solution.py:681
  190.9 7.5 %collective-permute-done.16.refs_1_.refs_4_ = bf16[2,2,256,256]{3,2,1,0:T(8,128)(2,1)S(1)} collective-permute-done((bf16[2,2,256,256]{3,2,1,0:T(8,128)(2,1)S(1)}, bf16[2,2,256,256]{3,2,1,0:T(8,128)(2,1)S(1)}, u32[]{:S(2)}, u32[]{:S(2)}) %collective-permute-start.16) | collective-permute-done | bytes 524320 | tf_op jit(solution)/shard_map/ppermute | solution.py:681
  198.4 3.2 collective-permute-done.22.refs_7_.refs_10_
  202.4 3.0 shard_map.90
  205.5 5.5 %collective-permute-start.23 = (bf16[8,256,256]{2,1,0:T(8,128)(2,1)}, bf16[8,256,256]{2,1,0:T(8,128)(2,1)S(1)}, u32[]{:S(2)}, u32[]{:S(2)}) collective-permute-start(bf16[8,256,256]{2,1,0:T(8,128)(2,1)} %get-tuple-element.187), channel_id=1, source_target_pairs={{0,1},{1,8},{8,9},{2,3},{3,10},{10,11},{4,5},{5,12},{12,13},{6,7},... | collective-permute-start | bytes 3145736 | tf_op jit(solution)/shard_map/ppermute | solution.py:684
  215.1 4.8 %shard_map.89 = (bf16[2,256,384]{2,1,0:T(8,128)(2,1)}, bf16[2,256,384]{2,1,0:T(8,128)(2,1)}, bf16[2,256,384]{2,1,0:T(8,128)(2,1)}, bf16[2,256,384]{2,1,0:T(8,128...) custom-call(f32[8,2,256,256]{3,2,1,0:T(8,128)} %get-tuple-element.16, ...), custom_call_target="tpu_custom_call" | custom-call | tf_op jit(solution)/shard_map/pallas_call | solution.py:629
  220.2 4.1 %collective-permute-start.13 = (bf16[2,256,384]{2,1,0:T(8,128)(2,1)}, bf16[2,256,384]{2,1,0:T(8,128)(2,1)S(1)}, u32[]{:S(2)}, u32[]{:S(2)}) collective-permute-start(bf16[2,256,384]{2,1,0:T(8,128)(2,1)} %get-tuple-element.174), channel_id=1, source_target_pairs={{0,20},{1,21},{2,22},{3,23},{4,16},{5,17},{6,18},{7,19},{16,4},{17... | collective-permute-start | bytes 1179656 | tf_op jit(solution)/shard_map/ppermute | solution.py:681
  228.6 43.5 %shard_map.91 = (bf16[2,256,128]{2,1,0:T(8,128)(2,1)}, bf16[2,256,128]{2,1,0:T(8,128)(2,1)}, bf16[2,256,128]{2,1,0:T(8,128)(2,1)}, bf16[2,256,128]{2,1,0:T(8,128...) custom-call(s32[1]{0:T(128)} %bitcast.refs_0_, ...), custom_call_target="tpu_custom_call" | custom-call | flops 1000000 | tf_op jit(solution)/shard_map/pallas_call | solution.py:588
  280.2 6.0 %collective-permute-done.25.refs_1_ = bf16[8,256,256]{2,1,0:T(8,128)(2,1)S(1)} collective-permute-done((bf16[8,256,256]{2,1,0:T(8,128)(2,1)}, bf16[8,256,256]{2,1,0:T(8,128)(2,1)S(1)}, u32[]{:S(2)}, u32[]{:S(2)}) %collective-permute-start.25) | collective-permute-done | bytes 1048608 | tf_op jit(solution)/shard_map/ppermute | solution.py:684
  286.2 4.6 %collective-permute-done.26.refs_2_ = bf16[8,256,256]{2,1,0:T(8,128)(2,1)S(1)} collective-permute-done((bf16[8,256,256]{2,1,0:T(8,128)(2,1)}, bf16[8,256,256]{2,1,0:T(8,128)(2,1)S(1)}, u32[]{:S(2)}, u32[]{:S(2)}) %collective-permute-start.26) | collective-permute-done | bytes 1048608 | tf_op jit(solution)/shard_map/ppermute | solution.py:684
  291.7 4.8 %shard_map.92 = (bf16[2,256,384]{2,1,0:T(8,128)(2,1)}, bf16[2,256,384]{2,1,0:T(8,128)(2,1)}, bf16[2,256,384]{2,1,0:T(8,128)(2,1)}, bf16[2,256,384]{2,1,0:T(8,128...) custom-call(f32[8,2,256,256]{3,2,1,0:T(8,128)} %get-tuple-element.21, ...), custom_call_target="tpu_custom_call" | custom-call | tf_op jit(solution)/shard_map/pallas_call | solution.py:629
  300.6 3.2 collective-permute-start.33
  303.8 12.5 %collective-permute-done.29.refs_2_ = bf16[2,256,384]{2,1,0:T(8,128)(2,1)S(1)} collective-permute-done((bf16[2,256,384]{2,1,0:T(8,128)(2,1)}, bf16[2,256,384]{2,1,0:T(8,128)(2,1)S(1)}, u32[]{:S(2)}, u32[]{:S(2)}) %collective-permute-start.29) | collective-permute-done | bytes 393248 | tf_op jit(solution)/shard_map/ppermute | solution.py:681
  316.4 9.6 %collective-permute-done.30.refs_3_ = bf16[2,256,384]{2,1,0:T(8,128)(2,1)S(1)} collective-permute-done((bf16[2,256,384]{2,1,0:T(8,128)(2,1)}, bf16[2,256,384]{2,1,0:T(8,128)(2,1)S(1)}, u32[]{:S(2)}, u32[]{:S(2)}) %collective-permute-start.30) | collective-permute-done | bytes 393248 | tf_op jit(solution)/shard_map/ppermute | solution.py:681
  326.0 4.5 %shard_map.93 = (bf16[512,2048]{1,0:T(8,128)(2,1)}, bf16[512,2048]{1,0:T(8,128)(2,1)}, bf16[512,2048]{1,0:T(8,128)(2,1)}) custom-call(s32[1]{0:T(128)} %bitcast.refs_0_, bf16[2,256,384]{2,1,0:T(8,128)(2,1)} %get-tuple-element.230.refs_1_, bf16[2,256,384]{2,1,0:T(8,128)(2,1)} %copy-done.33, bf16[2,256,384]{2,1,0:T(8,128)(2,1)} %copy-done.28, ...), custom_call_target="tpu_custom_call" | custom-call | tf_op jit(solution)/shard_map/pallas_call | solution.py:390
  330.5 20.5 %collective-permute-done.31.refs_4_ = bf16[2,256,384]{2,1,0:T(8,128)(2,1)S(1)} collective-permute-done((bf16[2,256,384]{2,1,0:T(8,128)(2,1)}, bf16[2,256,384]{2,1,0:T(8,128)(2,1)S(1)}, u32[]{:S(2)}, u32[]{:S(2)}) %collective-permute-start.31) | collective-permute-done | bytes 393248 | tf_op jit(solution)/shard_map/ppermute | solution.py:681
  352.1 3.7 %shard_map.94 = (bf16[512,2048]{1,0:T(8,128)(2,1)}, bf16[512,2048]{1,0:T(8,128)(2,1)}, bf16[512,2048]{1,0:T(8,128)(2,1)}) custom-call(s32[1]{0:T(128)} %bitcast.refs_0_, bf16[2,256,384]{2,1,0:T(8,128)(2,1)} %get-tuple-element.224.refs_1_, bf16[2,256,384]{2,1,0:T(8,128)(2,1)} %copy-done.21, ...), custom_call_target="tpu_custom_call", output_to_operand_aliasing={{0}: (7, {}), {1}: (8, {}), {2}: (9, {})} | custom-call | tf_op jit(solution)/shard_map/pallas_call | solution.py:390
  355.9 3.5 collective-permute-done.27.refs_1_
  359.3 6.8 %collective-permute-done.28.refs_2_ = bf16[2,256,384]{2,1,0:T(8,128)(2,1)S(1)} collective-permute-done((bf16[2,256,384]{2,1,0:T(8,128)(2,1)}, bf16[2,256,384]{2,1,0:T(8,128)(2,1)S(1)}, u32[]{:S(2)}, u32[]{:S(2)}) %collective-permute-start.28) | collective-permute-done | bytes 393248 | tf_op jit(solution)/shard_map/ppermute | solution.py:681
  (168 shorter events, 45.9 us)
Async XLA Ops:
  5.4 21.8 %collective-permute-start = (bf16[2,2,256,256]{3,2,1,0:T(8,128)(2,1)}, bf16[2,2,256,256]{3,2,1,0:T(8,128)(2,1)S(1)}, u32[]{:S(2)}, u32[]{:S(2)}) collective-permute-start(bf16[2,2,256,256]{3,2,1,0:T(8,128)(2,1)} %get-tuple-element.125), channel_id=1, source_target_pairs={{0,2},{1,3},{2,0},{3,1},{4,6},{5,7},{6,4},{7,5},{16,18},{17,19},{1... | collective-permute-start | bytes 1572872 | tf_op jit(solution)/shard_map/ppermute | solution.py:681
  5.5 26.1 %collective-permute-start.1 = (bf16[2,2,256,256]{3,2,1,0:T(8,128)(2,1)}, bf16[2,2,256,256]{3,2,1,0:T(8,128)(2,1)S(1)}, u32[]{:S(2)}, u32[]{:S(2)}) collective-permute-start(bf16[2,2,256,256]{3,2,1,0:T(8,128)(2,1)} %get-tuple-element.126), channel_id=1, source_target_pairs={{0,4},{1,5},{2,6},{3,7},{4,0},{5,1},{6,2},{7,3},{16,20},{17,21},{1... | collective-permute-start | bytes 1572872 | tf_op jit(solution)/shard_map/ppermute | solution.py:681
  8.0 45.2 %collective-permute-start.2 = (bf16[2,2,256,256]{3,2,1,0:T(8,128)(2,1)}, bf16[2,2,256,256]{3,2,1,0:T(8,128)(2,1)S(1)}, u32[]{:S(2)}, u32[]{:S(2)}) collective-permute-start(bf16[2,2,256,256]{3,2,1,0:T(8,128)(2,1)} %get-tuple-element.127), channel_id=1, source_target_pairs={{0,6},{1,7},{2,4},{3,5},{4,2},{5,3},{6,0},{7,1},{16,22},{17,23},{1... | collective-permute-start | bytes 1572872 | tf_op jit(solution)/shard_map/ppermute | solution.py:681
  8.1 45.1 %collective-permute-start.3 = (bf16[2,2,256,256]{3,2,1,0:T(8,128)(2,1)}, bf16[2,2,256,256]{3,2,1,0:T(8,128)(2,1)S(1)}, u32[]{:S(2)}, u32[]{:S(2)}) collective-permute-start(bf16[2,2,256,256]{3,2,1,0:T(8,128)(2,1)} %get-tuple-element.128), channel_id=1, source_target_pairs={{0,16},{1,17},{2,18},{3,19},{4,20},{5,21},{6,22},{7,23},{16,0},{17... | collective-permute-start | bytes 1572872 | tf_op jit(solution)/shard_map/ppermute | solution.py:681
  9.3 43.9 %collective-permute-start.4 = (bf16[2,2,256,256]{3,2,1,0:T(8,128)(2,1)}, bf16[2,2,256,256]{3,2,1,0:T(8,128)(2,1)S(1)}, u32[]{:S(2)}, u32[]{:S(2)}) collective-permute-start(bf16[2,2,256,256]{3,2,1,0:T(8,128)(2,1)} %get-tuple-element.129), channel_id=1, source_target_pairs={{0,18},{1,19},{2,16},{3,17},{4,22},{5,23},{6,20},{7,21},{16,2},{17... | collective-permute-start | bytes 1572872 | tf_op jit(solution)/shard_map/ppermute | solution.py:681
  27.2 58.9 %collective-permute-start.5 = (bf16[2,2,256,256]{3,2,1,0:T(8,128)(2,1)}, bf16[2,2,256,256]{3,2,1,0:T(8,128)(2,1)S(1)}, u32[]{:S(2)}, u32[]{:S(2)}) collective-permute-start(bf16[2,2,256,256]{3,2,1,0:T(8,128)(2,1)} %get-tuple-element.146), channel_id=1, source_target_pairs={{0,20},{1,21},{2,22},{3,23},{4,16},{5,17},{6,18},{7,19},{16,4},{17... | collective-permute-start | bytes 1572872 | tf_op jit(solution)/shard_map/ppermute | solution.py:681
  31.6 67.4 %collective-permute-start.6 = (bf16[2,2,256,256]{3,2,1,0:T(8,128)(2,1)S(1)}, bf16[2,2,256,256]{3,2,1,0:T(8,128)(2,1)S(1)}, u32[]{:S(2)}, u32[]{:S(2)}) collective-permute-start(bf16[2,2,256,256]{3,2,1,0:T(8,128)(2,1)S(1)} %copy-done.40), channel_id=1, source_target_pairs={{0,22},{1,23},{2,20},{3,21},{4,18},{5,19},{6,16},{7,17},{16,6},{17... | collective-permute-start | bytes 1572872 | tf_op jit(solution)/shard_map/ppermute | solution.py:681
  103.0 17.0 %collective-permute-start.7 = (bf16[8,256,256]{2,1,0:T(8,128)(2,1)}, bf16[8,256,256]{2,1,0:T(8,128)(2,1)S(1)}, u32[]{:S(2)}, u32[]{:S(2)}) collective-permute-start(bf16[8,256,256]{2,1,0:T(8,128)(2,1)} %get-tuple-element.148), channel_id=1, source_target_pairs={{0,1},{1,8},{8,9},{2,3},{3,10},{10,11},{4,5},{5,12},{12,13},{6,7},... | collective-permute-start | bytes 3145736 | tf_op jit(solution)/shard_map/ppermute | solution.py:684
  111.2 56.9 %collective-permute-start.17 = (bf16[2,2,256,256]{3,2,1,0:T(8,128)(2,1)}, bf16[2,2,256,256]{3,2,1,0:T(8,128)(2,1)S(1)}, u32[]{:S(2)}, u32[]{:S(2)}) collective-permute-start(bf16[2,2,256,256]{3,2,1,0:T(8,128)(2,1)} %get-tuple-element.181), channel_id=1, source_target_pairs={{0,4},{1,5},{2,6},{3,7},{4,0},{5,1},{6,2},{7,3},{16,20},{17,21},{1... | collective-permute-start | bytes 1572872 | tf_op jit(solution)/shard_map/ppermute | solution.py:681
  111.3 59.4 %collective-permute-start.18 = (bf16[2,2,256,256]{3,2,1,0:T(8,128)(2,1)}, bf16[2,2,256,256]{3,2,1,0:T(8,128)(2,1)S(1)}, u32[]{:S(2)}, u32[]{:S(2)}) collective-permute-start(bf16[2,2,256,256]{3,2,1,0:T(8,128)(2,1)} %get-tuple-element.182), channel_id=1, source_target_pairs={{0,6},{1,7},{2,4},{3,5},{4,2},{5,3},{6,0},{7,1},{16,22},{17,23},{1... | collective-permute-start | bytes 1572872 | tf_op jit(solution)/shard_map/ppermute | solution.py:681
  115.2 56.6 %collective-permute-start.19 = (bf16[2,2,256,256]{3,2,1,0:T(8,128)(2,1)}, bf16[2,2,256,256]{3,2,1,0:T(8,128)(2,1)S(1)}, u32[]{:S(2)}, u32[]{:S(2)}) collective-permute-start(bf16[2,2,256,256]{3,2,1,0:T(8,128)(2,1)} %get-tuple-element.183), channel_id=1, source_target_pairs={{0,16},{1,17},{2,18},{3,19},{4,20},{5,21},{6,22},{7,23},{16,0},{17... | collective-permute-start | bytes 1572872 | tf_op jit(solution)/shard_map/ppermute | solution.py:681
  120.0 54.9 %collective-permute-start.20 = (bf16[2,2,256,256]{3,2,1,0:T(8,128)(2,1)S(1)}, bf16[2,2,256,256]{3,2,1,0:T(8,128)(2,1)S(1)}, u32[]{:S(2)}, u32[]{:S(2)}) collective-permute-start(bf16[2,2,256,256]{3,2,1,0:T(8,128)(2,1)S(1)} %copy-done.39), channel_id=1, source_target_pairs={{0,18},{1,19},{2,16},{3,17},{4,22},{5,23},{6,20},{7,21},{16,2},{17... | collective-permute-start | bytes 1572872 | tf_op jit(solution)/shard_map/ppermute | solution.py:681
  124.6 66.4 %collective-permute-start.21 = (bf16[2,2,256,256]{3,2,1,0:T(8,128)(2,1)}, bf16[2,2,256,256]{3,2,1,0:T(8,128)(2,1)S(1)}, u32[]{:S(2)}, u32[]{:S(2)}) collective-permute-start(bf16[2,2,256,256]{3,2,1,0:T(8,128)(2,1)} %get-tuple-element.185), channel_id=1, source_target_pairs={{0,20},{1,21},{2,22},{3,23},{4,16},{5,17},{6,18},{7,19},{16,4},{17... | collective-permute-start | bytes 1572872 | tf_op jit(solution)/shard_map/ppermute | solution.py:681
  168.2 30.2 %collective-permute-start.16 = (bf16[2,2,256,256]{3,2,1,0:T(8,128)(2,1)S(1)}, bf16[2,2,256,256]{3,2,1,0:T(8,128)(2,1)S(1)}, u32[]{:S(2)}, u32[]{:S(2)}) collective-permute-start(bf16[2,2,256,256]{3,2,1,0:T(8,128)(2,1)S(1)} %copy-done.38), channel_id=1, source_target_pairs={{0,2},{1,3},{2,0},{3,1},{4,6},{5,7},{6,4},{7,5},{16,18},{17,19},{1... | collective-permute-start | bytes 1572872 | tf_op jit(solution)/shard_map/ppermute | solution.py:681
  170.7 30.9 %collective-permute-start.22 = (bf16[2,2,256,256]{3,2,1,0:T(8,128)(2,1)S(1)}, bf16[2,2,256,256]{3,2,1,0:T(8,128)(2,1)S(1)}, u32[]{:S(2)}, u32[]{:S(2)}) collective-permute-start(bf16[2,2,256,256]{3,2,1,0:T(8,128)(2,1)S(1)} %copy-done.37), channel_id=1, source_target_pairs={{0,22},{1,23},{2,20},{3,21},{4,18},{5,19},{6,16},{7,17},{16,6},{17... | collective-permute-start | bytes 1572872 | tf_op jit(solution)/shard_map/ppermute | solution.py:681
  171.8 41.3 %collective-permute-start.9 = (bf16[8,256,256]{2,1,0:T(8,128)(2,1)}, bf16[8,256,256]{2,1,0:T(8,128)(2,1)S(1)}, u32[]{:S(2)}, u32[]{:S(2)}) collective-permute-start(bf16[8,256,256]{2,1,0:T(8,128)(2,1)} %get-tuple-element.162), channel_id=1, source_target_pairs={{0,1},{1,8},{8,9},{2,3},{3,10},{10,11},{4,5},{5,12},{12,13},{6,7},... | collective-permute-start | bytes 3145736 | tf_op jit(solution)/shard_map/ppermute | solution.py:684
  174.9 38.2 %collective-permute-start.10 = (bf16[8,256,256]{2,1,0:T(8,128)(2,1)}, bf16[8,256,256]{2,1,0:T(8,128)(2,1)S(1)}, u32[]{:S(2)}, u32[]{:S(2)}) collective-permute-start(bf16[8,256,256]{2,1,0:T(8,128)(2,1)} %get-tuple-element.163), channel_id=1, source_target_pairs={{1,0},{8,1},{9,8},{3,2},{10,3},{11,10},{5,4},{12,5},{13,12},{7,6},... | collective-permute-start | bytes 3145736 | tf_op jit(solution)/shard_map/ppermute | solution.py:684
  205.5 18.8 %collective-permute-start.23 = (bf16[8,256,256]{2,1,0:T(8,128)(2,1)}, bf16[8,256,256]{2,1,0:T(8,128)(2,1)S(1)}, u32[]{:S(2)}, u32[]{:S(2)}) collective-permute-start(bf16[8,256,256]{2,1,0:T(8,128)(2,1)} %get-tuple-element.187), channel_id=1, source_target_pairs={{0,1},{1,8},{8,9},{2,3},{3,10},{10,11},{4,5},{5,12},{12,13},{6,7},... | collective-permute-start | bytes 3145736 | tf_op jit(solution)/shard_map/ppermute | solution.py:684
  220.0 52.2 %collective-permute-start.11 = (bf16[2,256,384]{2,1,0:T(8,128)(2,1)}, bf16[2,256,384]{2,1,0:T(8,128)(2,1)S(1)}, u32[]{:S(2)}, u32[]{:S(2)}) collective-permute-start(bf16[2,256,384]{2,1,0:T(8,128)(2,1)} %get-tuple-element.172), channel_id=1, source_target_pairs={{0,4},{1,5},{2,6},{3,7},{4,0},{5,1},{6,2},{7,3},{16,20},{17,21},{1... | collective-permute-start | bytes 1179656 | tf_op jit(solution)/shard_map/ppermute | solution.py:681
  220.0 52.2 %collective-permute-start.12 = (bf16[2,256,384]{2,1,0:T(8,128)(2,1)}, bf16[2,256,384]{2,1,0:T(8,128)(2,1)S(1)}, u32[]{:S(2)}, u32[]{:S(2)}) collective-permute-start(bf16[2,256,384]{2,1,0:T(8,128)(2,1)} %get-tuple-element.173), channel_id=1, source_target_pairs={{0,6},{1,7},{2,4},{3,5},{4,2},{5,3},{6,0},{7,1},{16,22},{17,23},{1... | collective-permute-start | bytes 1179656 | tf_op jit(solution)/shard_map/ppermute | solution.py:681
  220.2 52.0 %collective-permute-start.13 = (bf16[2,256,384]{2,1,0:T(8,128)(2,1)}, bf16[2,256,384]{2,1,0:T(8,128)(2,1)S(1)}, u32[]{:S(2)}, u32[]{:S(2)}) collective-permute-start(bf16[2,256,384]{2,1,0:T(8,128)(2,1)} %get-tuple-element.174), channel_id=1, source_target_pairs={{0,20},{1,21},{2,22},{3,23},{4,16},{5,17},{6,18},{7,19},{16,4},{17... | collective-permute-start | bytes 1179656 | tf_op jit(solution)/shard_map/ppermute | solution.py:681
  224.3 47.8 %collective-permute-start.14 = (bf16[2,256,384]{2,1,0:T(8,128)(2,1)}, bf16[2,256,384]{2,1,0:T(8,128)(2,1)S(1)}, u32[]{:S(2)}, u32[]{:S(2)}) collective-permute-start(bf16[2,256,384]{2,1,0:T(8,128)(2,1)} %get-tuple-element.175), channel_id=1, source_target_pairs={{0,16},{1,17},{2,18},{3,19},{4,20},{5,21},{6,22},{7,23},{16,0},{17... | collective-permute-start | bytes 1179656 | tf_op jit(solution)/shard_map/ppermute | solution.py:681
  227.6 44.6 %collective-permute-start.15 = (bf16[2,256,384]{2,1,0:T(8,128)(2,1)}, bf16[2,256,384]{2,1,0:T(8,128)(2,1)S(1)}, u32[]{:S(2)}, u32[]{:S(2)}) collective-permute-start(bf16[2,256,384]{2,1,0:T(8,128)(2,1)} %get-tuple-element.176), channel_id=1, source_target_pairs={{0,18},{1,19},{2,16},{3,17},{4,22},{5,23},{6,20},{7,21},{16,2},{17... | collective-permute-start | bytes 1179656 | tf_op jit(solution)/shard_map/ppermute | solution.py:681
  276.9 23.5 %collective-permute-start.34 = (bf16[2,256,384]{2,1,0:T(8,128)(2,1)S(1)}, bf16[2,256,384]{2,1,0:T(8,128)(2,1)S(1)}, u32[]{:S(2)}, u32[]{:S(2)}) collective-permute-start(bf16[2,256,384]{2,1,0:T(8,128)(2,1)S(1)} %copy-done.42), channel_id=1, source_target_pairs={{0,2},{1,3},{2,0},{3,1},{4,6},{5,7},{6,4},{7,5},{16,18},{17,19},{1... | collective-permute-start | bytes 1179656 | tf_op jit(solution)/shard_map/ppermute | solution.py:681
  279.0 21.7 %collective-permute-start.35 = (bf16[2,256,384]{2,1,0:T(8,128)(2,1)S(1)}, bf16[2,256,384]{2,1,0:T(8,128)(2,1)S(1)}, u32[]{:S(2)}, u32[]{:S(2)}) collective-permute-start(bf16[2,256,384]{2,1,0:T(8,128)(2,1)S(1)} %copy-done.41), channel_id=1, source_target_pairs={{0,22},{1,23},{2,20},{3,21},{4,18},{5,19},{6,16},{7,17},{16,6},{17... | collective-permute-start | bytes 1179656 | tf_op jit(solution)/shard_map/ppermute | solution.py:681
  296.5 19.8 %collective-permute-start.29 = (bf16[2,256,384]{2,1,0:T(8,128)(2,1)}, bf16[2,256,384]{2,1,0:T(8,128)(2,1)S(1)}, u32[]{:S(2)}, u32[]{:S(2)}) collective-permute-start(bf16[2,256,384]{2,1,0:T(8,128)(2,1)} %get-tuple-element.225), channel_id=1, source_target_pairs={{0,2},{1,3},{2,0},{3,1},{4,6},{5,7},{6,4},{7,5},{16,18},{17,19},{1... | collective-permute-start | bytes 1179656 | tf_op jit(solution)/shard_map/ppermute | solution.py:681
  299.1 26.9 %collective-permute-start.30 = (bf16[2,256,384]{2,1,0:T(8,128)(2,1)}, bf16[2,256,384]{2,1,0:T(8,128)(2,1)S(1)}, u32[]{:S(2)}, u32[]{:S(2)}) collective-permute-start(bf16[2,256,384]{2,1,0:T(8,128)(2,1)} %get-tuple-element.226), channel_id=1, source_target_pairs={{0,4},{1,5},{2,6},{3,7},{4,0},{5,1},{6,2},{7,3},{16,20},{17,21},{1... | collective-permute-start | bytes 1179656 | tf_op jit(solution)/shard_map/ppermute | solution.py:681
  300.1 50.9 %collective-permute-start.31 = (bf16[2,256,384]{2,1,0:T(8,128)(2,1)}, bf16[2,256,384]{2,1,0:T(8,128)(2,1)S(1)}, u32[]{:S(2)}, u32[]{:S(2)}) collective-permute-start(bf16[2,256,384]{2,1,0:T(8,128)(2,1)} %get-tuple-element.227), channel_id=1, source_target_pairs={{0,6},{1,7},{2,4},{3,5},{4,2},{5,3},{6,0},{7,1},{16,22},{17,23},{1... | collective-permute-start | bytes 1179656 | tf_op jit(solution)/shard_map/ppermute | solution.py:681
  300.4 50.7 %collective-permute-start.32 = (bf16[2,256,384]{2,1,0:T(8,128)(2,1)}, bf16[2,256,384]{2,1,0:T(8,128)(2,1)S(1)}, u32[]{:S(2)}, u32[]{:S(2)}) collective-permute-start(bf16[2,256,384]{2,1,0:T(8,128)(2,1)} %get-tuple-element.228), channel_id=1, source_target_pairs={{0,16},{1,17},{2,18},{3,19},{4,20},{5,21},{6,22},{7,23},{16,0},{17... | collective-permute-start | bytes 1179656 | tf_op jit(solution)/shard_map/ppermute | solution.py:681
  300.6 50.4 %collective-permute-start.33 = (bf16[2,256,384]{2,1,0:T(8,128)(2,1)}, bf16[2,256,384]{2,1,0:T(8,128)(2,1)S(1)}, u32[]{:S(2)}, u32[]{:S(2)}) collective-permute-start(bf16[2,256,384]{2,1,0:T(8,128)(2,1)} %get-tuple-element.229), channel_id=1, source_target_pairs={{0,18},{1,19},{2,16},{3,17},{4,22},{5,23},{6,20},{7,21},{16,2},{17... | collective-permute-start | bytes 1179656 | tf_op jit(solution)/shard_map/ppermute | solution.py:681
  316.3 43.0 %collective-permute-start.27 = (bf16[2,256,384]{2,1,0:T(8,128)(2,1)}, bf16[2,256,384]{2,1,0:T(8,128)(2,1)S(1)}, u32[]{:S(2)}, u32[]{:S(2)}) collective-permute-start(bf16[2,256,384]{2,1,0:T(8,128)(2,1)} %get-tuple-element.222), channel_id=1, source_target_pairs={{0,20},{1,21},{2,22},{3,23},{4,16},{5,17},{6,18},{7,19},{16,4},{17... | collective-permute-start | bytes 1179656 | tf_op jit(solution)/shard_map/ppermute | solution.py:681
  326.0 40.2 %collective-permute-start.28 = (bf16[2,256,384]{2,1,0:T(8,128)(2,1)}, bf16[2,256,384]{2,1,0:T(8,128)(2,1)S(1)}, u32[]{:S(2)}, u32[]{:S(2)}) collective-permute-start(bf16[2,256,384]{2,1,0:T(8,128)(2,1)} %get-tuple-element.223), channel_id=1, source_target_pairs={{0,22},{1,23},{2,20},{3,21},{4,18},{5,19},{6,16},{7,17},{16,6},{17... | collective-permute-start | bytes 1179656 | tf_op jit(solution)/shard_map/ppermute | solution.py:681
  (47 other events, 1176.7 us)

commit v5 on v4

--- a/solution.py
+++ b/solution.py
@@ -301,13 +301,13 @@
     return (source == line * (TW * TILE) + col * TILE + x).astype(jnp.bfloat16)
 
 
-def split_kernel(places, turn, pairs, place_ref, *refs):
-    arrays, outs = refs[: 2 * pairs], refs[2 * pairs : 2 * pairs + places]
-    taken, ready, in_sem, out_sem = refs[2 * pairs + places :]
-    turns = HEADS // places
+def split_kernel(seats, turn, turns, pairs, place_ref, *refs):
+    count = len(seats)
+    arrays, outs = refs[: 2 * pairs], refs[2 * pairs : 2 * pairs + count]
+    taken, ready, in_sem, out_sem = refs[2 * pairs + count :]
     loads = []
-    for k in range(places):
-        first = pl.multiple_of(((place_ref[0] ^ k) * turns + turn) * D_HEAD, D_HEAD)
+    for k in range(count):
+        first = pl.multiple_of(((place_ref[0] ^ seats[k]) * turns + turn) * D_HEAD, D_HEAD)
         loads.append(
             [
                 pltpu.make_async_copy(
@@ -320,7 +320,7 @@
             copy.start()
     order = row_order(False)
     stores = []
-    for k in range(places):
+    for k in range(count):
         for copy in loads[k]:
             copy.wait()
         for pair in range(pairs):
@@ -337,18 +337,18 @@
         copy.wait()
 
 
-def split_heads(places, turn, place, arrays):
-    rows, pairs = arrays[0].shape[0], len(arrays) // 2
+def split_heads(seats, turn, turns, place, arrays):
+    count, rows, pairs = len(seats), arrays[0].shape[0], len(arrays) // 2
     return pl.pallas_call(
-        lambda *refs: split_kernel(places, turn, pairs, *refs),
+        lambda *refs: split_kernel(seats, turn, turns, pairs, *refs),
         in_specs=[SCALARS] + [ANYWHERE] * (2 * pairs),
-        out_specs=[ANYWHERE] * places,
-        out_shape=[jax.ShapeDtypeStruct((pairs, 2, LINES, LANES), jnp.bfloat16)] * places,
+        out_specs=[ANYWHERE] * count,
+        out_shape=[jax.ShapeDtypeStruct((pairs, 2, LINES, LANES), jnp.bfloat16)] * count,
         scratch_shapes=[
-            pltpu.VMEM((places, 2 * pairs, rows, D_HEAD), jnp.bfloat16),
-            pltpu.VMEM((places, pairs, 2, LINES, LANES), jnp.bfloat16),
-            pltpu.SemaphoreType.DMA((places, 2 * pairs)),
-            pltpu.SemaphoreType.DMA((places,)),
+            pltpu.VMEM((count, 2 * pairs, rows, D_HEAD), jnp.bfloat16),
+            pltpu.VMEM((count, pairs, 2, LINES, LANES), jnp.bfloat16),
+            pltpu.SemaphoreType.DMA((count, 2 * pairs)),
+            pltpu.SemaphoreType.DMA((count,)),
         ],
         compiler_params=PARAMS,
     )(place, *arrays)
@@ -611,28 +611,31 @@
     return results[:places], *results[places:]
 
 
-def finish_kernel(places, acc_ref, above_ref, below_ref, *refs):
-    with_query = len(refs) > places
-    outs = refs[-places:]
+def finish_kernel(count, acc_ref, above_ref, below_ref, *refs):
+    queries, outs = refs[:count], refs[count:]
     lane = lax.broadcasted_iota(jnp.int32, (1, LANES), 1)
     factor = jnp.where(lane < D_HEAD, D_HEAD**-0.5, 1.0)
-    for k in range(places):
+    for k in range(count):
         for row, ref in enumerate((above_ref, below_ref)):
             total = acc_ref[k, row] + ref[k].astype(jnp.float32)
             outs[k][row, :, :LANES] = (total * factor).astype(jnp.bfloat16)
-        if with_query:
-            outs[k][:, :, LANES:] = refs[k][...]
-
-
-def finish_pairs(places, acc, above, below, query=()):
-    lanes = LANES + (D_HEAD if query else 0)
+        outs[k][:, :, LANES:] = queries[k][...]
+
+
+def finish_pairs(seats, acc, above, below, query):
+    count, lanes = len(seats), LANES + D_HEAD
+    at = seats[0] // count
+    halo = pl.BlockSpec((count, LINES, LANES), lambda g: (at, 0, 0))
+    block = pl.BlockSpec((2, LINES, D_HEAD), lambda g: (0, 0, 0))
     return pl.pallas_call(
-        lambda *refs: finish_kernel(places, *refs),
-        in_specs=[WHOLE] * (3 + len(query)),
-        out_specs=[WHOLE] * places,
-        out_shape=[jax.ShapeDtypeStruct((2, LINES, lanes), jnp.bfloat16)] * places,
+        lambda *refs: finish_kernel(count, *refs),
+        grid=(1,),
+        in_specs=[pl.BlockSpec((count, 2, LINES, LANES), lambda g: (at, 0, 0, 0)), halo, halo]
+        + [block] * count,
+        out_specs=[pl.BlockSpec((2, LINES, lanes), lambda g: (0, 0, 0))] * count,
+        out_shape=[jax.ShapeDtypeStruct((2, LINES, lanes), jnp.bfloat16)] * count,
         compiler_params=PARAMS,
-    )(acc, above, below, *query)
+    )(acc, above, below, *[query[k] for k in seats])
 
 
 def window_tables(tile_valid, width_shift, first_row):
@@ -690,6 +693,7 @@
         return [moved[k] for k in range(places)]
 
     natural = list(range(1, places))
+    halves = (range(places // 2), range(places // 2, places))
     far, near = [k for k in natural if k & 2], [k for k in natural if not k & 2]
     held = [far[-1], near[0]]
     mixed = far[:-1] + near[1:] + held
@@ -712,12 +716,15 @@
 
     arrays = (key_states, value_states, queries, out_grad)
     outs = ()
-    groups = [exchange(split_heads(places, 0, place, arrays), natural)]
+    blocks = []
+    for seats in halves:
+        blocks += split_heads(seats, 0, turns, place, arrays)
+    groups = [exchange(blocks, natural)]
     leaving = None
     for turn in range(turns):
         more = turn + 1 < turns
         if more:
-            coming = split_heads(places, turn + 1, place, arrays)
+            coming = split_heads(range(places), turn + 1, turns, place, arrays)
             groups[-1][1:6], coming = ordered(groups[-1][1:6], coming)
         first, last = edge_rows(places, groups[0])
         grads = head_grads(places, place, starts, bias, groups, step(last, down), step(first, up))
@@ -732,7 +739,10 @@
             coming, grads = after(coming, grads)
             groups = [exchange(coming, mixed)]
         dq, acc, above, below = grads
-        leaving = finish_pairs(places, acc, step(below, down), step(above, up), dq)
+        from_above, from_below = step(below, down), step(above, up)
+        leaving = []
+        for seats in [range(places)]:
+            leaving += finish_pairs(seats, acc, from_above, from_below, dq)
     left = exchange(leaving, natural)
     for seats in (range(places - 2), range(places - 2, places)):
         outs = join_heads(seats, turns - 1, turns, place, [left[k] for k in seats], outs)

time: 370 us -> 369 us (level)
    pallas_call x4 -> x5, Pallas kernels: 19.2 us -> 21 us  [the longest x3 11.4 us: split_heads(): pl.pallas_call(lambda *refs: split_kernel(seats, turn, turns, pairs, *ref...]
  transfers between devices with their start and end apart: 36 -> 36, of which waited for: 17 -> 17; matrix products, arithmetic and copies ran while one was open for 1% -> 1% of each run, Pallas kernels for 31% -> 32%
where the time goes in v5:
time: 369 us; the launch traced here: 368 us
  waiting for transfers between devices  176 us (48%)
  Pallas kernels  125 us (34%)
  starting transfers between devices  54.8 us (15%)
  local copies, waits for them, and re-layouts  10.8 us (3%)
    ppermute x28, waiting for transfers between devices, send(): lax.ppermute(block, ('tm', 'seq'), [(i, i ^ 2 * k) for i in range(2 * pla...  153 us
    pallas_call x2, Pallas kernels, head_grads(): pl.pallas_call(lambda *refs: grad_kernel(places, len(groups), *refs), in_...  87.1 us
    ppermute x28, starting transfers between devices, send(): lax.ppermute(block, ('tm', 'seq'), [(i, i ^ 2 * k) for i in range(2 * pla...  30.4 us
    ppermute x8, starting transfers between devices, step(): return lax.ppermute(block, ('height', 'seq'), route)  24.3 us
    ppermute x8, waiting for transfers between devices, step(): return lax.ppermute(block, ('height', 'seq'), route)  22.7 us
    pallas_call x3, Pallas kernels, split_heads(): pl.pallas_call(lambda *refs: split_kernel(seats, turn, turns, pairs, *ref...  11.4 us
    pallas_call x3, Pallas kernels, join_heads(): pl.pallas_call(lambda *refs: join_kernel(seats, turn, turns, len(earlier)...  10.6 us
    pallas_call x2, Pallas kernels, finish_pairs(): pl.pallas_call(lambda *refs: finish_kernel(count, *refs), grid=(1,), in_s...  9.6 us
  transfers between devices with their start and end apart: 36, of which 17 were waited for; matrix products, arithmetic and copies ran while one was open for 1% of the time, Pallas kernels for 32%

profile of v5, /device:TPU:9, one launch (start us, length us, event | category | flops | bytes accessed | tf_op | source)
XLA Modules:
  0.0 368.1 jit_solution(7507525334419532489)
XLA Ops:
  0.6 3.3 shard_map.85
  6.7 3.3 shard_map.86
  12.4 4.8 %shard_map.87 = (bf16[2,2,256,256]{3,2,1,0:T(8,128)(2,1)}, bf16[2,2,256,256]{3,2,1,0:T(8,128)(2,1)}, bf16[2,2,256,256]{3,2,1,0:T(8,128)(2,1)}, bf16[2,2,256,256]...) custom-call(s32[1]{0:T(128)} %bitcast.refs_0_, ...), custom_call_target="tpu_custom_call" | custom-call | tf_op jit(solution)/shard_map/pallas_call | solution.py:342
  17.3 8.5 %collective-permute-done.refs_1_.refs_4_ = bf16[2,2,256,256]{3,2,1,0:T(8,128)(2,1)S(1)} collective-permute-done((bf16[2,2,256,256]{3,2,1,0:T(8,128)(2,1)}, bf16[2,2,256,256]{3,2,1,0:T(8,128)(2,1)S(1)}, u32[]{:S(2)}, u32[]{:S(2)}) %collective-permute-start) | collective-permute-done | bytes 524320 | tf_op jit(solution)/shard_map/ppermute | solution.py:684
  25.7 4.5 %collective-permute-start.5 = (bf16[2,2,256,256]{3,2,1,0:T(8,128)(2,1)}, bf16[2,2,256,256]{3,2,1,0:T(8,128)(2,1)S(1)}, u32[]{:S(2)}, u32[]{:S(2)}) collective-permute-start(bf16[2,2,256,256]{3,2,1,0:T(8,128)(2,1)} %get-tuple-element.146), channel_id=1, source_target_pairs={{0,20},{1,21},{2,22},{3,23},{4,16},{5,17},{6,18},{7,19},{16,4},{17... | collective-permute-start | bytes 1572872 | tf_op jit(solution)/shard_map/ppermute | solution.py:684
  30.5 21.3 %collective-permute-done.2.refs_3_.refs_6_ = bf16[2,2,256,256]{3,2,1,0:T(8,128)(2,1)S(1)} collective-permute-done((bf16[2,2,256,256]{3,2,1,0:T(8,128)(2,1)}, bf16[2,2,256,256]{3,2,1,0:T(8,128)(2,1)S(1)}, u32[]{:S(2)}, u32[]{:S(2)}) %collective-permute-start.2) | collective-permute-done | bytes 524320 | tf_op jit(solution)/shard_map/ppermute | solution.py:684
  51.8 32.9 %collective-permute-done.5.refs_6_.refs_9_ = bf16[2,2,256,256]{3,2,1,0:T(8,128)(2,1)S(1)} collective-permute-done((bf16[2,2,256,256]{3,2,1,0:T(8,128)(2,1)}, bf16[2,2,256,256]{3,2,1,0:T(8,128)(2,1)S(1)}, u32[]{:S(2)}, u32[]{:S(2)}) %collective-permute-start.5) | collective-permute-done | bytes 524320 | tf_op jit(solution)/shard_map/ppermute | solution.py:684
  84.7 13.0 %collective-permute-done.6.refs_7_.refs_10_ = bf16[2,2,256,256]{3,2,1,0:T(8,128)(2,1)S(1)} collective-permute-done((bf16[2,2,256,256]{3,2,1,0:T(8,128)(2,1)S(1)}, bf16[2,2,256,256]{3,2,1,0:T(8,128)(2,1)S(1)}, u32[]{:S(2)}, u32[]{:S(2)}) %collective-permute-start.6) | collective-permute-done | bytes 524320 | tf_op jit(solution)/shard_map/ppermute | solution.py:684
  98.4 3.1 shard_map.88
  101.5 5.0 %collective-permute-start.7 = (bf16[8,256,256]{2,1,0:T(8,128)(2,1)}, bf16[8,256,256]{2,1,0:T(8,128)(2,1)S(1)}, u32[]{:S(2)}, u32[]{:S(2)}) collective-permute-start(bf16[8,256,256]{2,1,0:T(8,128)(2,1)} %get-tuple-element.148), channel_id=1, source_target_pairs={{0,1},{1,8},{8,9},{2,3},{3,10},{10,11},{4,5},{5,12},{12,13},{6,7},... | collective-permute-start | bytes 3145736 | tf_op jit(solution)/shard_map/ppermute | solution.py:687
  114.0 4.5 %collective-permute-done.7.refs_11_ = bf16[8,256,256]{2,1,0:T(8,128)(2,1)S(1)} collective-permute-done((bf16[8,256,256]{2,1,0:T(8,128)(2,1)}, bf16[8,256,256]{2,1,0:T(8,128)(2,1)S(1)}, u32[]{:S(2)}, u32[]{:S(2)}) %collective-permute-start.7) | collective-permute-done | bytes 1048608 | tf_op jit(solution)/shard_map/ppermute | solution.py:687
  118.5 4.6 %collective-permute-done.8.refs_12_ = bf16[8,256,256]{2,1,0:T(8,128)(2,1)} collective-permute-done((bf16[8,256,256]{2,1,0:T(8,128)(2,1)}, bf16[8,256,256]{2,1,0:T(8,128)(2,1)}, u32[]{:S(2)}, u32[]{:S(2)}) %collective-permute-start.8) | collective-permute-done | bytes 1048608 | tf_op jit(solution)/shard_map/ppermute | solution.py:687
  123.1 43.6 %shard_map.89 = (bf16[2,256,128]{2,1,0:T(8,128)(2,1)}, bf16[2,256,128]{2,1,0:T(8,128)(2,1)}, bf16[2,256,128]{2,1,0:T(8,128)(2,1)}, bf16[2,256,128]{2,1,0:T(8,128...) custom-call(s32[1]{0:T(128)} %bitcast.refs_0_, ...), custom_call_target="tpu_custom_call" | custom-call | flops 1000000 | tf_op jit(solution)/shard_map/pallas_call | solution.py:588
  175.4 14.1 %collective-permute-done.21.refs_6_.refs_9_ = bf16[2,2,256,256]{3,2,1,0:T(8,128)(2,1)S(1)} collective-permute-done((bf16[2,2,256,256]{3,2,1,0:T(8,128)(2,1)}, bf16[2,2,256,256]{3,2,1,0:T(8,128)(2,1)S(1)}, u32[]{:S(2)}, u32[]{:S(2)}) %collective-permute-start.21) | collective-permute-done | bytes 524320 | tf_op jit(solution)/shard_map/ppermute | solution.py:684
  189.5 7.7 %collective-permute-done.16.refs_1_.refs_4_ = bf16[2,2,256,256]{3,2,1,0:T(8,128)(2,1)S(1)} collective-permute-done((bf16[2,2,256,256]{3,2,1,0:T(8,128)(2,1)S(1)}, bf16[2,2,256,256]{3,2,1,0:T(8,128)(2,1)S(1)}, u32[]{:S(2)}, u32[]{:S(2)}) %collective-permute-start.16) | collective-permute-done | bytes 524320 | tf_op jit(solution)/shard_map/ppermute | solution.py:684
  201.0 3.0 shard_map.91
  204.1 5.5 %collective-permute-start.23 = (bf16[8,256,256]{2,1,0:T(8,128)(2,1)}, bf16[8,256,256]{2,1,0:T(8,128)(2,1)S(1)}, u32[]{:S(2)}, u32[]{:S(2)}) collective-permute-start(bf16[8,256,256]{2,1,0:T(8,128)(2,1)} %get-tuple-element.187), channel_id=1, source_target_pairs={{0,1},{1,8},{8,9},{2,3},{3,10},{10,11},{4,5},{5,12},{12,13},{6,7},... | collective-permute-start | bytes 3145736 | tf_op jit(solution)/shard_map/ppermute | solution.py:687
  213.7 4.8 %shard_map.90 = (bf16[2,256,384]{2,1,0:T(8,128)(2,1)}, bf16[2,256,384]{2,1,0:T(8,128)(2,1)}, bf16[2,256,384]{2,1,0:T(8,128)(2,1)}, bf16[2,256,384]{2,1,0:T(8,128...) custom-call(f32[8,2,256,256]{3,2,1,0:T(8,128)} %get-tuple-element.16, ...), custom_call_target="tpu_custom_call" | custom-call | tf_op jit(solution)/shard_map/pallas_call | solution.py:630
  218.8 4.1 %collective-permute-start.13 = (bf16[2,256,384]{2,1,0:T(8,128)(2,1)}, bf16[2,256,384]{2,1,0:T(8,128)(2,1)S(1)}, u32[]{:S(2)}, u32[]{:S(2)}) collective-permute-start(bf16[2,256,384]{2,1,0:T(8,128)(2,1)} %get-tuple-element.174), channel_id=1, source_target_pairs={{0,20},{1,21},{2,22},{3,23},{4,16},{5,17},{6,18},{7,19},{16,4},{17... | collective-permute-start | bytes 1179656 | tf_op jit(solution)/shard_map/ppermute | solution.py:684
  223.2 3.0 collective-permute-done.24.refs_12_
  227.2 43.5 %shard_map.92 = (bf16[2,256,128]{2,1,0:T(8,128)(2,1)}, bf16[2,256,128]{2,1,0:T(8,128)(2,1)}, bf16[2,256,128]{2,1,0:T(8,128)(2,1)}, bf16[2,256,128]{2,1,0:T(8,128...) custom-call(s32[1]{0:T(128)} %bitcast.refs_0_, ...), custom_call_target="tpu_custom_call" | custom-call | flops 1000000 | tf_op jit(solution)/shard_map/pallas_call | solution.py:588
  278.8 6.0 %collective-permute-done.25.refs_1_ = bf16[8,256,256]{2,1,0:T(8,128)(2,1)S(1)} collective-permute-done((bf16[8,256,256]{2,1,0:T(8,128)(2,1)}, bf16[8,256,256]{2,1,0:T(8,128)(2,1)S(1)}, u32[]{:S(2)}, u32[]{:S(2)}) %collective-permute-start.25) | collective-permute-done | bytes 1048608 | tf_op jit(solution)/shard_map/ppermute | solution.py:687
  284.8 4.6 %collective-permute-done.26.refs_2_ = bf16[8,256,256]{2,1,0:T(8,128)(2,1)S(1)} collective-permute-done((bf16[8,256,256]{2,1,0:T(8,128)(2,1)}, bf16[8,256,256]{2,1,0:T(8,128)(2,1)S(1)}, u32[]{:S(2)}, u32[]{:S(2)}) %collective-permute-start.26) | collective-permute-done | bytes 1048608 | tf_op jit(solution)/shard_map/ppermute | solution.py:687
  290.3 4.8 %shard_map.93 = (bf16[2,256,384]{2,1,0:T(8,128)(2,1)}, bf16[2,256,384]{2,1,0:T(8,128)(2,1)}, bf16[2,256,384]{2,1,0:T(8,128)(2,1)}, bf16[2,256,384]{2,1,0:T(8,128...) custom-call(f32[8,2,256,256]{3,2,1,0:T(8,128)} %get-tuple-element.21, ...), custom_call_target="tpu_custom_call" | custom-call | tf_op jit(solution)/shard_map/pallas_call | solution.py:630
  299.2 3.2 collective-permute-start.33
  302.4 12.5 %collective-permute-done.29.refs_2_ = bf16[2,256,384]{2,1,0:T(8,128)(2,1)S(1)} collective-permute-done((bf16[2,256,384]{2,1,0:T(8,128)(2,1)}, bf16[2,256,384]{2,1,0:T(8,128)(2,1)S(1)}, u32[]{:S(2)}, u32[]{:S(2)}) %collective-permute-start.29) | collective-permute-done | bytes 393248 | tf_op jit(solution)/shard_map/ppermute | solution.py:684
  314.9 9.6 %collective-permute-done.30.refs_3_ = bf16[2,256,384]{2,1,0:T(8,128)(2,1)S(1)} collective-permute-done((bf16[2,256,384]{2,1,0:T(8,128)(2,1)}, bf16[2,256,384]{2,1,0:T(8,128)(2,1)S(1)}, u32[]{:S(2)}, u32[]{:S(2)}) %collective-permute-start.30) | collective-permute-done | bytes 393248 | tf_op jit(solution)/shard_map/ppermute | solution.py:684
  324.6 4.5 %shard_map.94 = (bf16[512,2048]{1,0:T(8,128)(2,1)}, bf16[512,2048]{1,0:T(8,128)(2,1)}, bf16[512,2048]{1,0:T(8,128)(2,1)}) custom-call(s32[1]{0:T(128)} %bitcast.refs_0_, bf16[2,256,384]{2,1,0:T(8,128)(2,1)} %get-tuple-element.230.refs_1_, bf16[2,256,384]{2,1,0:T(8,128)(2,1)} %copy-done.33, bf16[2,256,384]{2,1,0:T(8,128)(2,1)} %copy-done.28, ...), custom_call_target="tpu_custom_call" | custom-call | tf_op jit(solution)/shard_map/pallas_call | solution.py:390
  329.1 20.5 %collective-permute-done.31.refs_4_ = bf16[2,256,384]{2,1,0:T(8,128)(2,1)S(1)} collective-permute-done((bf16[2,256,384]{2,1,0:T(8,128)(2,1)}, bf16[2,256,384]{2,1,0:T(8,128)(2,1)S(1)}, u32[]{:S(2)}, u32[]{:S(2)}) %collective-permute-start.31) | collective-permute-done | bytes 393248 | tf_op jit(solution)/shard_map/ppermute | solution.py:684
  350.7 3.7 %shard_map.95 = (bf16[512,2048]{1,0:T(8,128)(2,1)}, bf16[512,2048]{1,0:T(8,128)(2,1)}, bf16[512,2048]{1,0:T(8,128)(2,1)}) custom-call(s32[1]{0:T(128)} %bitcast.refs_0_, bf16[2,256,384]{2,1,0:T(8,128)(2,1)} %get-tuple-element.224.refs_1_, bf16[2,256,384]{2,1,0:T(8,128)(2,1)} %copy-done.21, ...), custom_call_target="tpu_custom_call", output_to_operand_aliasing={{0}: (7, {}), {1}: (8, {}), {2}: (9, {})} | custom-call | tf_op jit(solution)/shard_map/pallas_call | solution.py:390
  354.5 3.5 collective-permute-done.27.refs_1_
  357.9 6.8 %collective-permute-done.28.refs_2_ = bf16[2,256,384]{2,1,0:T(8,128)(2,1)S(1)} collective-permute-done((bf16[2,256,384]{2,1,0:T(8,128)(2,1)}, bf16[2,256,384]{2,1,0:T(8,128)(2,1)S(1)}, u32[]{:S(2)}, u32[]{:S(2)}) %collective-permute-start.28) | collective-permute-done | bytes 393248 | tf_op jit(solution)/shard_map/ppermute | solution.py:684
  (169 shorter events, 49.0 us)
Async XLA Ops:
  4.0 21.8 %collective-permute-start = (bf16[2,2,256,256]{3,2,1,0:T(8,128)(2,1)}, bf16[2,2,256,256]{3,2,1,0:T(8,128)(2,1)S(1)}, u32[]{:S(2)}, u32[]{:S(2)}) collective-permute-start(bf16[2,2,256,256]{3,2,1,0:T(8,128)(2,1)} %get-tuple-element.125), channel_id=1, source_target_pairs={{0,2},{1,3},{2,0},{3,1},{4,6},{5,7},{6,4},{7,5},{16,18},{17,19},{1... | collective-permute-start | bytes 1572872 | tf_op jit(solution)/shard_map/ppermute | solution.py:684
  4.1 26.1 %collective-permute-start.1 = (bf16[2,2,256,256]{3,2,1,0:T(8,128)(2,1)}, bf16[2,2,256,256]{3,2,1,0:T(8,128)(2,1)S(1)}, u32[]{:S(2)}, u32[]{:S(2)}) collective-permute-start(bf16[2,2,256,256]{3,2,1,0:T(8,128)(2,1)} %get-tuple-element.126), channel_id=1, source_target_pairs={{0,4},{1,5},{2,6},{3,7},{4,0},{5,1},{6,2},{7,3},{16,20},{17,21},{1... | collective-permute-start | bytes 1572872 | tf_op jit(solution)/shard_map/ppermute | solution.py:684
  6.5 45.2 %collective-permute-start.2 = (bf16[2,2,256,256]{3,2,1,0:T(8,128)(2,1)}, bf16[2,2,256,256]{3,2,1,0:T(8,128)(2,1)S(1)}, u32[]{:S(2)}, u32[]{:S(2)}) collective-permute-start(bf16[2,2,256,256]{3,2,1,0:T(8,128)(2,1)} %get-tuple-element.127), channel_id=1, source_target_pairs={{0,6},{1,7},{2,4},{3,5},{4,2},{5,3},{6,0},{7,1},{16,22},{17,23},{1... | collective-permute-start | bytes 1572872 | tf_op jit(solution)/shard_map/ppermute | solution.py:684
  10.0 41.7 %collective-permute-start.3 = (bf16[2,2,256,256]{3,2,1,0:T(8,128)(2,1)}, bf16[2,2,256,256]{3,2,1,0:T(8,128)(2,1)S(1)}, u32[]{:S(2)}, u32[]{:S(2)}) collective-permute-start(bf16[2,2,256,256]{3,2,1,0:T(8,128)(2,1)} %get-tuple-element.128), channel_id=1, source_target_pairs={{0,16},{1,17},{2,18},{3,19},{4,20},{5,21},{6,22},{7,23},{16,0},{17... | collective-permute-start | bytes 1572872 | tf_op jit(solution)/shard_map/ppermute | solution.py:684
  11.3 40.5 %collective-permute-start.4 = (bf16[2,2,256,256]{3,2,1,0:T(8,128)(2,1)}, bf16[2,2,256,256]{3,2,1,0:T(8,128)(2,1)S(1)}, u32[]{:S(2)}, u32[]{:S(2)}) collective-permute-start(bf16[2,2,256,256]{3,2,1,0:T(8,128)(2,1)} %get-tuple-element.129), channel_id=1, source_target_pairs={{0,18},{1,19},{2,16},{3,17},{4,22},{5,23},{6,20},{7,21},{16,2},{17... | collective-permute-start | bytes 1572872 | tf_op jit(solution)/shard_map/ppermute | solution.py:684
  25.7 58.9 %collective-permute-start.5 = (bf16[2,2,256,256]{3,2,1,0:T(8,128)(2,1)}, bf16[2,2,256,256]{3,2,1,0:T(8,128)(2,1)S(1)}, u32[]{:S(2)}, u32[]{:S(2)}) collective-permute-start(bf16[2,2,256,256]{3,2,1,0:T(8,128)(2,1)} %get-tuple-element.146), channel_id=1, source_target_pairs={{0,20},{1,21},{2,22},{3,23},{4,16},{5,17},{6,18},{7,19},{16,4},{17... | collective-permute-start | bytes 1572872 | tf_op jit(solution)/shard_map/ppermute | solution.py:684
  30.2 67.4 %collective-permute-start.6 = (bf16[2,2,256,256]{3,2,1,0:T(8,128)(2,1)S(1)}, bf16[2,2,256,256]{3,2,1,0:T(8,128)(2,1)S(1)}, u32[]{:S(2)}, u32[]{:S(2)}) collective-permute-start(bf16[2,2,256,256]{3,2,1,0:T(8,128)(2,1)S(1)} %copy-done.40), channel_id=1, source_target_pairs={{0,22},{1,23},{2,20},{3,21},{4,18},{5,19},{6,16},{7,17},{16,6},{17... | collective-permute-start | bytes 1572872 | tf_op jit(solution)/shard_map/ppermute | solution.py:684
  101.5 17.0 %collective-permute-start.7 = (bf16[8,256,256]{2,1,0:T(8,128)(2,1)}, bf16[8,256,256]{2,1,0:T(8,128)(2,1)S(1)}, u32[]{:S(2)}, u32[]{:S(2)}) collective-permute-start(bf16[8,256,256]{2,1,0:T(8,128)(2,1)} %get-tuple-element.148), channel_id=1, source_target_pairs={{0,1},{1,8},{8,9},{2,3},{3,10},{10,11},{4,5},{5,12},{12,13},{6,7},... | collective-permute-start | bytes 3145736 | tf_op jit(solution)/shard_map/ppermute | solution.py:687
  109.8 56.9 %collective-permute-start.17 = (bf16[2,2,256,256]{3,2,1,0:T(8,128)(2,1)}, bf16[2,2,256,256]{3,2,1,0:T(8,128)(2,1)S(1)}, u32[]{:S(2)}, u32[]{:S(2)}) collective-permute-start(bf16[2,2,256,256]{3,2,1,0:T(8,128)(2,1)} %get-tuple-element.181), channel_id=1, source_target_pairs={{0,4},{1,5},{2,6},{3,7},{4,0},{5,1},{6,2},{7,3},{16,20},{17,21},{1... | collective-permute-start | bytes 1572872 | tf_op jit(solution)/shard_map/ppermute | solution.py:684
  109.9 59.4 %collective-permute-start.18 = (bf16[2,2,256,256]{3,2,1,0:T(8,128)(2,1)}, bf16[2,2,256,256]{3,2,1,0:T(8,128)(2,1)S(1)}, u32[]{:S(2)}, u32[]{:S(2)}) collective-permute-start(bf16[2,2,256,256]{3,2,1,0:T(8,128)(2,1)} %get-tuple-element.182), channel_id=1, source_target_pairs={{0,6},{1,7},{2,4},{3,5},{4,2},{5,3},{6,0},{7,1},{16,22},{17,23},{1... | collective-permute-start | bytes 1572872 | tf_op jit(solution)/shard_map/ppermute | solution.py:684
  113.8 56.7 %collective-permute-start.19 = (bf16[2,2,256,256]{3,2,1,0:T(8,128)(2,1)}, bf16[2,2,256,256]{3,2,1,0:T(8,128)(2,1)S(1)}, u32[]{:S(2)}, u32[]{:S(2)}) collective-permute-start(bf16[2,2,256,256]{3,2,1,0:T(8,128)(2,1)} %get-tuple-element.183), channel_id=1, source_target_pairs={{0,16},{1,17},{2,18},{3,19},{4,20},{5,21},{6,22},{7,23},{16,0},{17... | collective-permute-start | bytes 1572872 | tf_op jit(solution)/shard_map/ppermute | solution.py:684
  118.5 54.9 %collective-permute-start.20 = (bf16[2,2,256,256]{3,2,1,0:T(8,128)(2,1)S(1)}, bf16[2,2,256,256]{3,2,1,0:T(8,128)(2,1)S(1)}, u32[]{:S(2)}, u32[]{:S(2)}) collective-permute-start(bf16[2,2,256,256]{3,2,1,0:T(8,128)(2,1)S(1)} %copy-done.39), channel_id=1, source_target_pairs={{0,18},{1,19},{2,16},{3,17},{4,22},{5,23},{6,20},{7,21},{16,2},{17... | collective-permute-start | bytes 1572872 | tf_op jit(solution)/shard_map/ppermute | solution.py:684
  123.1 66.4 %collective-permute-start.21 = (bf16[2,2,256,256]{3,2,1,0:T(8,128)(2,1)}, bf16[2,2,256,256]{3,2,1,0:T(8,128)(2,1)S(1)}, u32[]{:S(2)}, u32[]{:S(2)}) collective-permute-start(bf16[2,2,256,256]{3,2,1,0:T(8,128)(2,1)} %get-tuple-element.185), channel_id=1, source_target_pairs={{0,20},{1,21},{2,22},{3,23},{4,16},{5,17},{6,18},{7,19},{16,4},{17... | collective-permute-start | bytes 1572872 | tf_op jit(solution)/shard_map/ppermute | solution.py:684
  166.8 30.4 %collective-permute-start.16 = (bf16[2,2,256,256]{3,2,1,0:T(8,128)(2,1)S(1)}, bf16[2,2,256,256]{3,2,1,0:T(8,128)(2,1)S(1)}, u32[]{:S(2)}, u32[]{:S(2)}) collective-permute-start(bf16[2,2,256,256]{3,2,1,0:T(8,128)(2,1)S(1)} %copy-done.38), channel_id=1, source_target_pairs={{0,2},{1,3},{2,0},{3,1},{4,6},{5,7},{6,4},{7,5},{16,18},{17,19},{1... | collective-permute-start | bytes 1572872 | tf_op jit(solution)/shard_map/ppermute | solution.py:684
  169.3 30.9 %collective-permute-start.22 = (bf16[2,2,256,256]{3,2,1,0:T(8,128)(2,1)S(1)}, bf16[2,2,256,256]{3,2,1,0:T(8,128)(2,1)S(1)}, u32[]{:S(2)}, u32[]{:S(2)}) collective-permute-start(bf16[2,2,256,256]{3,2,1,0:T(8,128)(2,1)S(1)} %copy-done.37), channel_id=1, source_target_pairs={{0,22},{1,23},{2,20},{3,21},{4,18},{5,19},{6,16},{7,17},{16,6},{17... | collective-permute-start | bytes 1572872 | tf_op jit(solution)/shard_map/ppermute | solution.py:684
  170.4 41.3 %collective-permute-start.9 = (bf16[8,256,256]{2,1,0:T(8,128)(2,1)}, bf16[8,256,256]{2,1,0:T(8,128)(2,1)S(1)}, u32[]{:S(2)}, u32[]{:S(2)}) collective-permute-start(bf16[8,256,256]{2,1,0:T(8,128)(2,1)} %get-tuple-element.162), channel_id=1, source_target_pairs={{0,1},{1,8},{8,9},{2,3},{3,10},{10,11},{4,5},{5,12},{12,13},{6,7},... | collective-permute-start | bytes 3145736 | tf_op jit(solution)/shard_map/ppermute | solution.py:687
  173.5 38.2 %collective-permute-start.10 = (bf16[8,256,256]{2,1,0:T(8,128)(2,1)}, bf16[8,256,256]{2,1,0:T(8,128)(2,1)S(1)}, u32[]{:S(2)}, u32[]{:S(2)}) collective-permute-start(bf16[8,256,256]{2,1,0:T(8,128)(2,1)} %get-tuple-element.163), channel_id=1, source_target_pairs={{1,0},{8,1},{9,8},{3,2},{10,3},{11,10},{5,4},{12,5},{13,12},{7,6},... | collective-permute-start | bytes 3145736 | tf_op jit(solution)/shard_map/ppermute | solution.py:687
  204.1 18.8 %collective-permute-start.23 = (bf16[8,256,256]{2,1,0:T(8,128)(2,1)}, bf16[8,256,256]{2,1,0:T(8,128)(2,1)S(1)}, u32[]{:S(2)}, u32[]{:S(2)}) collective-permute-start(bf16[8,256,256]{2,1,0:T(8,128)(2,1)} %get-tuple-element.187), channel_id=1, source_target_pairs={{0,1},{1,8},{8,9},{2,3},{3,10},{10,11},{4,5},{5,12},{12,13},{6,7},... | collective-permute-start | bytes 3145736 | tf_op jit(solution)/shard_map/ppermute | solution.py:687
  218.5 52.2 %collective-permute-start.11 = (bf16[2,256,384]{2,1,0:T(8,128)(2,1)}, bf16[2,256,384]{2,1,0:T(8,128)(2,1)S(1)}, u32[]{:S(2)}, u32[]{:S(2)}) collective-permute-start(bf16[2,256,384]{2,1,0:T(8,128)(2,1)} %get-tuple-element.172), channel_id=1, source_target_pairs={{0,4},{1,5},{2,6},{3,7},{4,0},{5,1},{6,2},{7,3},{16,20},{17,21},{1... | collective-permute-start | bytes 1179656 | tf_op jit(solution)/shard_map/ppermute | solution.py:684
  218.5 52.2 %collective-permute-start.12 = (bf16[2,256,384]{2,1,0:T(8,128)(2,1)}, bf16[2,256,384]{2,1,0:T(8,128)(2,1)S(1)}, u32[]{:S(2)}, u32[]{:S(2)}) collective-permute-start(bf16[2,256,384]{2,1,0:T(8,128)(2,1)} %get-tuple-element.173), channel_id=1, source_target_pairs={{0,6},{1,7},{2,4},{3,5},{4,2},{5,3},{6,0},{7,1},{16,22},{17,23},{1... | collective-permute-start | bytes 1179656 | tf_op jit(solution)/shard_map/ppermute | solution.py:684
  218.8 52.0 %collective-permute-start.13 = (bf16[2,256,384]{2,1,0:T(8,128)(2,1)}, bf16[2,256,384]{2,1,0:T(8,128)(2,1)S(1)}, u32[]{:S(2)}, u32[]{:S(2)}) collective-permute-start(bf16[2,256,384]{2,1,0:T(8,128)(2,1)} %get-tuple-element.174), channel_id=1, source_target_pairs={{0,20},{1,21},{2,22},{3,23},{4,16},{5,17},{6,18},{7,19},{16,4},{17... | collective-permute-start | bytes 1179656 | tf_op jit(solution)/shard_map/ppermute | solution.py:684
  222.9 47.9 %collective-permute-start.14 = (bf16[2,256,384]{2,1,0:T(8,128)(2,1)}, bf16[2,256,384]{2,1,0:T(8,128)(2,1)S(1)}, u32[]{:S(2)}, u32[]{:S(2)}) collective-permute-start(bf16[2,256,384]{2,1,0:T(8,128)(2,1)} %get-tuple-element.175), channel_id=1, source_target_pairs={{0,16},{1,17},{2,18},{3,19},{4,20},{5,21},{6,22},{7,23},{16,0},{17... | collective-permute-start | bytes 1179656 | tf_op jit(solution)/shard_map/ppermute | solution.py:684
  226.2 44.6 %collective-permute-start.15 = (bf16[2,256,384]{2,1,0:T(8,128)(2,1)}, bf16[2,256,384]{2,1,0:T(8,128)(2,1)S(1)}, u32[]{:S(2)}, u32[]{:S(2)}) collective-permute-start(bf16[2,256,384]{2,1,0:T(8,128)(2,1)} %get-tuple-element.176), channel_id=1, source_target_pairs={{0,18},{1,19},{2,16},{3,17},{4,22},{5,23},{6,20},{7,21},{16,2},{17... | collective-permute-start | bytes 1179656 | tf_op jit(solution)/shard_map/ppermute | solution.py:684
  275.5 23.4 %collective-permute-start.34 = (bf16[2,256,384]{2,1,0:T(8,128)(2,1)S(1)}, bf16[2,256,384]{2,1,0:T(8,128)(2,1)S(1)}, u32[]{:S(2)}, u32[]{:S(2)}) collective-permute-start(bf16[2,256,384]{2,1,0:T(8,128)(2,1)S(1)} %copy-done.42), channel_id=1, source_target_pairs={{0,2},{1,3},{2,0},{3,1},{4,6},{5,7},{6,4},{7,5},{16,18},{17,19},{1... | collective-permute-start | bytes 1179656 | tf_op jit(solution)/shard_map/ppermute | solution.py:684
  277.5 21.7 %collective-permute-start.35 = (bf16[2,256,384]{2,1,0:T(8,128)(2,1)S(1)}, bf16[2,256,384]{2,1,0:T(8,128)(2,1)S(1)}, u32[]{:S(2)}, u32[]{:S(2)}) collective-permute-start(bf16[2,256,384]{2,1,0:T(8,128)(2,1)S(1)} %copy-done.41), channel_id=1, source_target_pairs={{0,22},{1,23},{2,20},{3,21},{4,18},{5,19},{6,16},{7,17},{16,6},{17... | collective-permute-start | bytes 1179656 | tf_op jit(solution)/shard_map/ppermute | solution.py:684
  295.1 19.7 %collective-permute-start.29 = (bf16[2,256,384]{2,1,0:T(8,128)(2,1)}, bf16[2,256,384]{2,1,0:T(8,128)(2,1)S(1)}, u32[]{:S(2)}, u32[]{:S(2)}) collective-permute-start(bf16[2,256,384]{2,1,0:T(8,128)(2,1)} %get-tuple-element.225), channel_id=1, source_target_pairs={{0,2},{1,3},{2,0},{3,1},{4,6},{5,7},{6,4},{7,5},{16,18},{17,19},{1... | collective-permute-start | bytes 1179656 | tf_op jit(solution)/shard_map/ppermute | solution.py:684
  297.6 26.9 %collective-permute-start.30 = (bf16[2,256,384]{2,1,0:T(8,128)(2,1)}, bf16[2,256,384]{2,1,0:T(8,128)(2,1)S(1)}, u32[]{:S(2)}, u32[]{:S(2)}) collective-permute-start(bf16[2,256,384]{2,1,0:T(8,128)(2,1)} %get-tuple-element.226), channel_id=1, source_target_pairs={{0,4},{1,5},{2,6},{3,7},{4,0},{5,1},{6,2},{7,3},{16,20},{17,21},{1... | collective-permute-start | bytes 1179656 | tf_op jit(solution)/shard_map/ppermute | solution.py:684
  298.7 50.9 %collective-permute-start.31 = (bf16[2,256,384]{2,1,0:T(8,128)(2,1)}, bf16[2,256,384]{2,1,0:T(8,128)(2,1)S(1)}, u32[]{:S(2)}, u32[]{:S(2)}) collective-permute-start(bf16[2,256,384]{2,1,0:T(8,128)(2,1)} %get-tuple-element.227), channel_id=1, source_target_pairs={{0,6},{1,7},{2,4},{3,5},{4,2},{5,3},{6,0},{7,1},{16,22},{17,23},{1... | collective-permute-start | bytes 1179656 | tf_op jit(solution)/shard_map/ppermute | solution.py:684
  298.9 50.7 %collective-permute-start.32 = (bf16[2,256,384]{2,1,0:T(8,128)(2,1)}, bf16[2,256,384]{2,1,0:T(8,128)(2,1)S(1)}, u32[]{:S(2)}, u32[]{:S(2)}) collective-permute-start(bf16[2,256,384]{2,1,0:T(8,128)(2,1)} %get-tuple-element.228), channel_id=1, source_target_pairs={{0,16},{1,17},{2,18},{3,19},{4,20},{5,21},{6,22},{7,23},{16,0},{17... | collective-permute-start | bytes 1179656 | tf_op jit(solution)/shard_map/ppermute | solution.py:684
  299.2 50.4 %collective-permute-start.33 = (bf16[2,256,384]{2,1,0:T(8,128)(2,1)}, bf16[2,256,384]{2,1,0:T(8,128)(2,1)S(1)}, u32[]{:S(2)}, u32[]{:S(2)}) collective-permute-start(bf16[2,256,384]{2,1,0:T(8,128)(2,1)} %get-tuple-element.229), channel_id=1, source_target_pairs={{0,18},{1,19},{2,16},{3,17},{4,22},{5,23},{6,20},{7,21},{16,2},{17... | collective-permute-start | bytes 1179656 | tf_op jit(solution)/shard_map/ppermute | solution.py:684
  314.8 43.1 %collective-permute-start.27 = (bf16[2,256,384]{2,1,0:T(8,128)(2,1)}, bf16[2,256,384]{2,1,0:T(8,128)(2,1)S(1)}, u32[]{:S(2)}, u32[]{:S(2)}) collective-permute-start(bf16[2,256,384]{2,1,0:T(8,128)(2,1)} %get-tuple-element.222), channel_id=1, source_target_pairs={{0,20},{1,21},{2,22},{3,23},{4,16},{5,17},{6,18},{7,19},{16,4},{17... | collective-permute-start | bytes 1179656 | tf_op jit(solution)/shard_map/ppermute | solution.py:684
  324.5 40.2 %collective-permute-start.28 = (bf16[2,256,384]{2,1,0:T(8,128)(2,1)}, bf16[2,256,384]{2,1,0:T(8,128)(2,1)S(1)}, u32[]{:S(2)}, u32[]{:S(2)}) collective-permute-start(bf16[2,256,384]{2,1,0:T(8,128)(2,1)} %get-tuple-element.223), channel_id=1, source_target_pairs={{0,22},{1,23},{2,20},{3,21},{4,18},{5,19},{6,16},{7,17},{16,6},{17... | collective-permute-start | bytes 1179656 | tf_op jit(solution)/shard_map/ppermute | solution.py:684
  (47 other events, 1169.5 us)

commit v6 on v5

--- a/solution.py
+++ b/solution.py
@@ -404,14 +404,19 @@
 
 
 def edge_kernel(places, *refs):
-    blocks, (first_ref, last_ref), sem = refs[:places], refs[places : places + 2], refs[-1]
-    copies = []
+    blocks, edges = refs[:places], refs[places : places + 2]
+    rows, in_sem, out_sem = refs[places + 2 :]
+    loads = [pltpu.make_async_copy(blocks[k].at[0], rows.at[k], in_sem.at[k]) for k in range(places)]
+    for copy in loads:
+        copy.start()
+    stores = []
     for k in range(places):
-        for row, ref in enumerate((first_ref, last_ref)):
-            copies.append(pltpu.make_async_copy(blocks[k].at[0, row], ref.at[k], sem.at[k, row]))
-    for copy in copies:
-        copy.start()
-    for copy in copies:
+        loads[k].wait()
+        for row in range(2):
+            copy = pltpu.make_async_copy(rows.at[k, row], edges[row].at[k], out_sem.at[k, row])
+            copy.start()
+            stores.append(copy)
+    for copy in stores:
         copy.wait()
 
 
@@ -419,9 +424,13 @@
     return pl.pallas_call(
         lambda *refs: edge_kernel(places, *refs),
         in_specs=[ANYWHERE] * places,
-        out_specs=[WHOLE] * 2,
+        out_specs=[ANYWHERE] * 2,
         out_shape=[jax.ShapeDtypeStruct((places, LINES, LANES), jnp.bfloat16)] * 2,
-        scratch_shapes=[pltpu.SemaphoreType.DMA((places, 2))],
+        scratch_shapes=[
+            pltpu.VMEM((places, 2, LINES, LANES), jnp.bfloat16),
+            pltpu.SemaphoreType.DMA((places,)),
+            pltpu.SemaphoreType.DMA((places, 2)),
+        ],
         compiler_params=PARAMS,
     )(*blocks)
 
@@ -741,7 +750,7 @@
         dq, acc, above, below = grads
         from_above, from_below = step(below, down), step(above, up)
         leaving = []
-        for seats in [range(places)]:
+        for seats in [range(places)] if more else halves:
             leaving += finish_pairs(seats, acc, from_above, from_below, dq)
     left = exchange(leaving, natural)
     for seats in (range(places - 2), range(places - 2, places)):

time: 369 us -> 368 us (level)
    pallas_call x2 -> x3, Pallas kernels: 9.6 us -> 11.3 us  [finish_pairs(): pl.pallas_call(lambda *refs: finish_kernel(count, *refs), grid=(1,), in_s...]
where the time goes in v6:
time: 368 us; the launch traced here: 367 us
  waiting for transfers between devices  173 us (47%)
  Pallas kernels  125 us (34%)
  starting transfers between devices  56.1 us (15%)
  local copies, waits for them, and re-layouts  10.8 us (3%)
    ppermute x28, waiting for transfers between devices, send(): lax.ppermute(block, ('tm', 'seq'), [(i, i ^ 2 * k) for i in range(2 * pla...  150 us
    pallas_call x2, Pallas kernels, head_grads(): pl.pallas_call(lambda *refs: grad_kernel(places, len(groups), *refs), in_...  87.2 us
    ppermute x28, starting transfers between devices, send(): lax.ppermute(block, ('tm', 'seq'), [(i, i ^ 2 * k) for i in range(2 * pla...  31.8 us
    ppermute x8, starting transfers between devices, step(): return lax.ppermute(block, ('height', 'seq'), route)  24.3 us
    ppermute x8, waiting for transfers between devices, step(): return lax.ppermute(block, ('height', 'seq'), route)  22.6 us
    pallas_call x3, Pallas kernels, split_heads(): pl.pallas_call(lambda *refs: split_kernel(seats, turn, turns, pairs, *ref...  11.4 us
    pallas_call x3, Pallas kernels, finish_pairs(): pl.pallas_call(lambda *refs: finish_kernel(count, *refs), grid=(1,), in_s...  11.3 us
    pallas_call x3, Pallas kernels, join_heads(): pl.pallas_call(lambda *refs: join_kernel(seats, turn, turns, len(earlier)...  10.6 us
  transfers between devices with their start and end apart: 36, of which 17 were waited for; matrix products, arithmetic and copies ran while one was open for 1% of the time, Pallas kernels for 32%

profile of v6, /device:TPU:9, one launch (start us, length us, event | category | flops | bytes accessed | tf_op | source)
XLA Modules:
  0.0 367.0 jit_solution(17696014098721719261)
XLA Ops:
  0.6 3.3 shard_map.85
  6.7 3.3 shard_map.86
  12.4 4.8 %shard_map.87 = (bf16[2,2,256,256]{3,2,1,0:T(8,128)(2,1)}, bf16[2,2,256,256]{3,2,1,0:T(8,128)(2,1)}, bf16[2,2,256,256]{3,2,1,0:T(8,128)(2,1)}, bf16[2,2,256,256]...) custom-call(s32[1]{0:T(128)} %bitcast.refs_0_, ...), custom_call_target="tpu_custom_call" | custom-call | tf_op jit(solution)/shard_map/pallas_call | solution.py:342
  17.2 8.5 %collective-permute-done.refs_1_.refs_4_ = bf16[2,2,256,256]{3,2,1,0:T(8,128)(2,1)S(1)} collective-permute-done((bf16[2,2,256,256]{3,2,1,0:T(8,128)(2,1)}, bf16[2,2,256,256]{3,2,1,0:T(8,128)(2,1)S(1)}, u32[]{:S(2)}, u32[]{:S(2)}) %collective-permute-start) | collective-permute-done | bytes 524320 | tf_op jit(solution)/shard_map/ppermute | solution.py:693
  25.7 4.5 %collective-permute-start.5 = (bf16[2,2,256,256]{3,2,1,0:T(8,128)(2,1)}, bf16[2,2,256,256]{3,2,1,0:T(8,128)(2,1)S(1)}, u32[]{:S(2)}, u32[]{:S(2)}) collective-permute-start(bf16[2,2,256,256]{3,2,1,0:T(8,128)(2,1)} %get-tuple-element.146), channel_id=1, source_target_pairs={{0,20},{1,21},{2,22},{3,23},{4,16},{5,17},{6,18},{7,19},{16,4},{17... | collective-permute-start | bytes 1572872 | tf_op jit(solution)/shard_map/ppermute | solution.py:693
  30.5 21.3 %collective-permute-done.2.refs_3_.refs_6_ = bf16[2,2,256,256]{3,2,1,0:T(8,128)(2,1)S(1)} collective-permute-done((bf16[2,2,256,256]{3,2,1,0:T(8,128)(2,1)}, bf16[2,2,256,256]{3,2,1,0:T(8,128)(2,1)S(1)}, u32[]{:S(2)}, u32[]{:S(2)}) %collective-permute-start.2) | collective-permute-done | bytes 524320 | tf_op jit(solution)/shard_map/ppermute | solution.py:693
  51.8 32.9 %collective-permute-done.5.refs_6_.refs_9_ = bf16[2,2,256,256]{3,2,1,0:T(8,128)(2,1)S(1)} collective-permute-done((bf16[2,2,256,256]{3,2,1,0:T(8,128)(2,1)}, bf16[2,2,256,256]{3,2,1,0:T(8,128)(2,1)S(1)}, u32[]{:S(2)}, u32[]{:S(2)}) %collective-permute-start.5) | collective-permute-done | bytes 524320 | tf_op jit(solution)/shard_map/ppermute | solution.py:693
  84.7 13.0 %collective-permute-done.6.refs_7_.refs_10_ = bf16[2,2,256,256]{3,2,1,0:T(8,128)(2,1)S(1)} collective-permute-done((bf16[2,2,256,256]{3,2,1,0:T(8,128)(2,1)S(1)}, bf16[2,2,256,256]{3,2,1,0:T(8,128)(2,1)S(1)}, u32[]{:S(2)}, u32[]{:S(2)}) %collective-permute-start.6) | collective-permute-done | bytes 524320 | tf_op jit(solution)/shard_map/ppermute | solution.py:693
  100.9 5.0 %collective-permute-start.7 = (bf16[8,256,256]{2,1,0:T(8,128)(2,1)}, bf16[8,256,256]{2,1,0:T(8,128)(2,1)S(1)}, u32[]{:S(2)}, u32[]{:S(2)}) collective-permute-start(bf16[8,256,256]{2,1,0:T(8,128)(2,1)} %get-tuple-element.148), channel_id=1, source_target_pairs={{0,1},{1,8},{8,9},{2,3},{3,10},{10,11},{4,5},{5,12},{12,13},{6,7},... | collective-permute-start | bytes 3145736 | tf_op jit(solution)/shard_map/ppermute | solution.py:696
  113.4 4.5 %collective-permute-done.7.refs_11_ = bf16[8,256,256]{2,1,0:T(8,128)(2,1)S(1)} collective-permute-done((bf16[8,256,256]{2,1,0:T(8,128)(2,1)}, bf16[8,256,256]{2,1,0:T(8,128)(2,1)S(1)}, u32[]{:S(2)}, u32[]{:S(2)}) %collective-permute-start.7) | collective-permute-done | bytes 1048608 | tf_op jit(solution)/shard_map/ppermute | solution.py:696
  118.0 4.6 %collective-permute-done.8.refs_12_ = bf16[8,256,256]{2,1,0:T(8,128)(2,1)} collective-permute-done((bf16[8,256,256]{2,1,0:T(8,128)(2,1)}, bf16[8,256,256]{2,1,0:T(8,128)(2,1)}, u32[]{:S(2)}, u32[]{:S(2)}) %collective-permute-start.8) | collective-permute-done | bytes 1048608 | tf_op jit(solution)/shard_map/ppermute | solution.py:696
  122.6 43.6 %shard_map.89 = (bf16[2,256,128]{2,1,0:T(8,128)(2,1)}, bf16[2,256,128]{2,1,0:T(8,128)(2,1)}, bf16[2,256,128]{2,1,0:T(8,128)(2,1)}, bf16[2,256,128]{2,1,0:T(8,128...) custom-call(s32[1]{0:T(128)} %bitcast.refs_0_, ...), custom_call_target="tpu_custom_call" | custom-call | flops 1000000 | tf_op jit(solution)/shard_map/pallas_call | solution.py:597
  169.9 3.0 collective-permute-start.9
  174.8 14.0 %collective-permute-done.21.refs_6_.refs_9_ = bf16[2,2,256,256]{3,2,1,0:T(8,128)(2,1)S(1)} collective-permute-done((bf16[2,2,256,256]{3,2,1,0:T(8,128)(2,1)}, bf16[2,2,256,256]{3,2,1,0:T(8,128)(2,1)S(1)}, u32[]{:S(2)}, u32[]{:S(2)}) %collective-permute-start.21) | collective-permute-done | bytes 524320 | tf_op jit(solution)/shard_map/ppermute | solution.py:693
  188.9 7.6 %collective-permute-done.16.refs_1_.refs_4_ = bf16[2,2,256,256]{3,2,1,0:T(8,128)(2,1)S(1)} collective-permute-done((bf16[2,2,256,256]{3,2,1,0:T(8,128)(2,1)S(1)}, bf16[2,2,256,256]{3,2,1,0:T(8,128)(2,1)S(1)}, u32[]{:S(2)}, u32[]{:S(2)}) %collective-permute-start.16) | collective-permute-done | bytes 524320 | tf_op jit(solution)/shard_map/ppermute | solution.py:693
  196.5 3.0 collective-permute-done.22.refs_7_.refs_10_
  202.9 5.5 %collective-permute-start.23 = (bf16[8,256,256]{2,1,0:T(8,128)(2,1)}, bf16[8,256,256]{2,1,0:T(8,128)(2,1)S(1)}, u32[]{:S(2)}, u32[]{:S(2)}) collective-permute-start(bf16[8,256,256]{2,1,0:T(8,128)(2,1)} %get-tuple-element.187), channel_id=1, source_target_pairs={{0,1},{1,8},{8,9},{2,3},{3,10},{10,11},{4,5},{5,12},{12,13},{6,7},... | collective-permute-start | bytes 3145736 | tf_op jit(solution)/shard_map/ppermute | solution.py:696
  212.5 4.9 %shard_map.90 = (bf16[2,256,384]{2,1,0:T(8,128)(2,1)}, bf16[2,256,384]{2,1,0:T(8,128)(2,1)}, bf16[2,256,384]{2,1,0:T(8,128)(2,1)}, bf16[2,256,384]{2,1,0:T(8,128...) custom-call(f32[8,2,256,256]{3,2,1,0:T(8,128)} %get-tuple-element.16, ...), custom_call_target="tpu_custom_call" | custom-call | tf_op jit(solution)/shard_map/pallas_call | solution.py:639
  217.6 4.1 %collective-permute-start.13 = (bf16[2,256,384]{2,1,0:T(8,128)(2,1)}, bf16[2,256,384]{2,1,0:T(8,128)(2,1)S(1)}, u32[]{:S(2)}, u32[]{:S(2)}) collective-permute-start(bf16[2,256,384]{2,1,0:T(8,128)(2,1)} %get-tuple-element.174), channel_id=1, source_target_pairs={{0,20},{1,21},{2,22},{3,23},{4,16},{5,17},{6,18},{7,19},{16,4},{17... | collective-permute-start | bytes 1179656 | tf_op jit(solution)/shard_map/ppermute | solution.py:693
  226.0 43.6 %shard_map.92 = (bf16[2,256,128]{2,1,0:T(8,128)(2,1)}, bf16[2,256,128]{2,1,0:T(8,128)(2,1)}, bf16[2,256,128]{2,1,0:T(8,128)(2,1)}, bf16[2,256,128]{2,1,0:T(8,128...) custom-call(s32[1]{0:T(128)} %bitcast.refs_0_, ...), custom_call_target="tpu_custom_call" | custom-call | flops 1000000 | tf_op jit(solution)/shard_map/pallas_call | solution.py:597
  277.7 5.9 %collective-permute-done.25.refs_1_ = bf16[8,256,256]{2,1,0:T(8,128)(2,1)S(1)} collective-permute-done((bf16[8,256,256]{2,1,0:T(8,128)(2,1)}, bf16[8,256,256]{2,1,0:T(8,128)(2,1)S(1)}, u32[]{:S(2)}, u32[]{:S(2)}) %collective-permute-start.25) | collective-permute-done | bytes 1048608 | tf_op jit(solution)/shard_map/ppermute | solution.py:696
  283.6 4.6 %collective-permute-done.26.refs_2_ = bf16[8,256,256]{2,1,0:T(8,128)(2,1)S(1)} collective-permute-done((bf16[8,256,256]{2,1,0:T(8,128)(2,1)}, bf16[8,256,256]{2,1,0:T(8,128)(2,1)S(1)}, u32[]{:S(2)}, u32[]{:S(2)}) %collective-permute-start.26) | collective-permute-done | bytes 1048608 | tf_op jit(solution)/shard_map/ppermute | solution.py:696
  289.2 3.2 shard_map.94
  296.2 3.2 shard_map.93
  299.8 3.2 collective-permute-start.33
  303.0 9.6 %collective-permute-done.29.refs_2_ = bf16[2,256,384]{2,1,0:T(8,128)(2,1)S(1)} collective-permute-done((bf16[2,256,384]{2,1,0:T(8,128)(2,1)}, bf16[2,256,384]{2,1,0:T(8,128)(2,1)S(1)}, u32[]{:S(2)}, u32[]{:S(2)}) %collective-permute-start.29) | collective-permute-done | bytes 393248 | tf_op jit(solution)/shard_map/ppermute | solution.py:693
  313.9 8.3 %collective-permute-done.30.refs_3_ = bf16[2,256,384]{2,1,0:T(8,128)(2,1)S(1)} collective-permute-done((bf16[2,256,384]{2,1,0:T(8,128)(2,1)}, bf16[2,256,384]{2,1,0:T(8,128)(2,1)S(1)}, u32[]{:S(2)}, u32[]{:S(2)}) %collective-permute-start.30) | collective-permute-done | bytes 393248 | tf_op jit(solution)/shard_map/ppermute | solution.py:693
  322.2 4.4 %shard_map.95 = (bf16[512,2048]{1,0:T(8,128)(2,1)}, bf16[512,2048]{1,0:T(8,128)(2,1)}, bf16[512,2048]{1,0:T(8,128)(2,1)}) custom-call(s32[1]{0:T(128)} %bitcast.refs_0_, bf16[2,256,384]{2,1,0:T(8,128)(2,1)} %get-tuple-element.230.refs_1_, bf16[2,256,384]{2,1,0:T(8,128)(2,1)} %copy-done.33, bf16[2,256,384]{2,1,0:T(8,128)(2,1)} %copy-done.28, ...), custom_call_target="tpu_custom_call" | custom-call | tf_op jit(solution)/shard_map/pallas_call | solution.py:390
  326.7 21.3 %collective-permute-done.31.refs_4_ = bf16[2,256,384]{2,1,0:T(8,128)(2,1)S(1)} collective-permute-done((bf16[2,256,384]{2,1,0:T(8,128)(2,1)}, bf16[2,256,384]{2,1,0:T(8,128)(2,1)S(1)}, u32[]{:S(2)}, u32[]{:S(2)}) %collective-permute-start.31) | collective-permute-done | bytes 393248 | tf_op jit(solution)/shard_map/ppermute | solution.py:693
  349.1 3.7 %shard_map.96 = (bf16[512,2048]{1,0:T(8,128)(2,1)}, bf16[512,2048]{1,0:T(8,128)(2,1)}, bf16[512,2048]{1,0:T(8,128)(2,1)}) custom-call(s32[1]{0:T(128)} %bitcast.refs_0_, bf16[2,256,384]{2,1,0:T(8,128)(2,1)} %get-tuple-element.224.refs_1_, bf16[2,256,384]{2,1,0:T(8,128)(2,1)} %copy-done.21, ...), custom_call_target="tpu_custom_call", output_to_operand_aliasing={{0}: (7, {}), {1}: (8, {}), {2}: (9, {})} | custom-call | tf_op jit(solution)/shard_map/pallas_call | solution.py:390
  352.8 3.0 collective-permute-done.27.refs_1_
  355.9 7.7 %collective-permute-done.28.refs_2_ = bf16[2,256,384]{2,1,0:T(8,128)(2,1)S(1)} collective-permute-done((bf16[2,256,384]{2,1,0:T(8,128)(2,1)}, bf16[2,256,384]{2,1,0:T(8,128)(2,1)S(1)}, u32[]{:S(2)}, u32[]{:S(2)}) %collective-permute-start.28) | collective-permute-done | bytes 393248 | tf_op jit(solution)/shard_map/ppermute | solution.py:693
  (170 shorter events, 52.3 us)
Async XLA Ops:
  4.0 21.8 %collective-permute-start = (bf16[2,2,256,256]{3,2,1,0:T(8,128)(2,1)}, bf16[2,2,256,256]{3,2,1,0:T(8,128)(2,1)S(1)}, u32[]{:S(2)}, u32[]{:S(2)}) collective-permute-start(bf16[2,2,256,256]{3,2,1,0:T(8,128)(2,1)} %get-tuple-element.125), channel_id=1, source_target_pairs={{0,2},{1,3},{2,0},{3,1},{4,6},{5,7},{6,4},{7,5},{16,18},{17,19},{1... | collective-permute-start | bytes 1572872 | tf_op jit(solution)/shard_map/ppermute | solution.py:693
  4.1 26.1 %collective-permute-start.1 = (bf16[2,2,256,256]{3,2,1,0:T(8,128)(2,1)}, bf16[2,2,256,256]{3,2,1,0:T(8,128)(2,1)S(1)}, u32[]{:S(2)}, u32[]{:S(2)}) collective-permute-start(bf16[2,2,256,256]{3,2,1,0:T(8,128)(2,1)} %get-tuple-element.126), channel_id=1, source_target_pairs={{0,4},{1,5},{2,6},{3,7},{4,0},{5,1},{6,2},{7,3},{16,20},{17,21},{1... | collective-permute-start | bytes 1572872 | tf_op jit(solution)/shard_map/ppermute | solution.py:693
  6.5 45.2 %collective-permute-start.2 = (bf16[2,2,256,256]{3,2,1,0:T(8,128)(2,1)}, bf16[2,2,256,256]{3,2,1,0:T(8,128)(2,1)S(1)}, u32[]{:S(2)}, u32[]{:S(2)}) collective-permute-start(bf16[2,2,256,256]{3,2,1,0:T(8,128)(2,1)} %get-tuple-element.127), channel_id=1, source_target_pairs={{0,6},{1,7},{2,4},{3,5},{4,2},{5,3},{6,0},{7,1},{16,22},{17,23},{1... | collective-permute-start | bytes 1572872 | tf_op jit(solution)/shard_map/ppermute | solution.py:693
  10.0 41.7 %collective-permute-start.3 = (bf16[2,2,256,256]{3,2,1,0:T(8,128)(2,1)}, bf16[2,2,256,256]{3,2,1,0:T(8,128)(2,1)S(1)}, u32[]{:S(2)}, u32[]{:S(2)}) collective-permute-start(bf16[2,2,256,256]{3,2,1,0:T(8,128)(2,1)} %get-tuple-element.128), channel_id=1, source_target_pairs={{0,16},{1,17},{2,18},{3,19},{4,20},{5,21},{6,22},{7,23},{16,0},{17... | collective-permute-start | bytes 1572872 | tf_op jit(solution)/shard_map/ppermute | solution.py:693
  11.3 40.5 %collective-permute-start.4 = (bf16[2,2,256,256]{3,2,1,0:T(8,128)(2,1)}, bf16[2,2,256,256]{3,2,1,0:T(8,128)(2,1)S(1)}, u32[]{:S(2)}, u32[]{:S(2)}) collective-permute-start(bf16[2,2,256,256]{3,2,1,0:T(8,128)(2,1)} %get-tuple-element.129), channel_id=1, source_target_pairs={{0,18},{1,19},{2,16},{3,17},{4,22},{5,23},{6,20},{7,21},{16,2},{17... | collective-permute-start | bytes 1572872 | tf_op jit(solution)/shard_map/ppermute | solution.py:693
  25.7 58.9 %collective-permute-start.5 = (bf16[2,2,256,256]{3,2,1,0:T(8,128)(2,1)}, bf16[2,2,256,256]{3,2,1,0:T(8,128)(2,1)S(1)}, u32[]{:S(2)}, u32[]{:S(2)}) collective-permute-start(bf16[2,2,256,256]{3,2,1,0:T(8,128)(2,1)} %get-tuple-element.146), channel_id=1, source_target_pairs={{0,20},{1,21},{2,22},{3,23},{4,16},{5,17},{6,18},{7,19},{16,4},{17... | collective-permute-start | bytes 1572872 | tf_op jit(solution)/shard_map/ppermute | solution.py:693
  30.2 67.4 %collective-permute-start.6 = (bf16[2,2,256,256]{3,2,1,0:T(8,128)(2,1)S(1)}, bf16[2,2,256,256]{3,2,1,0:T(8,128)(2,1)S(1)}, u32[]{:S(2)}, u32[]{:S(2)}) collective-permute-start(bf16[2,2,256,256]{3,2,1,0:T(8,128)(2,1)S(1)} %copy-done.40), channel_id=1, source_target_pairs={{0,22},{1,23},{2,20},{3,21},{4,18},{5,19},{6,16},{7,17},{16,6},{17... | collective-permute-start | bytes 1572872 | tf_op jit(solution)/shard_map/ppermute | solution.py:693
  100.9 17.0 %collective-permute-start.7 = (bf16[8,256,256]{2,1,0:T(8,128)(2,1)}, bf16[8,256,256]{2,1,0:T(8,128)(2,1)S(1)}, u32[]{:S(2)}, u32[]{:S(2)}) collective-permute-start(bf16[8,256,256]{2,1,0:T(8,128)(2,1)} %get-tuple-element.148), channel_id=1, source_target_pairs={{0,1},{1,8},{8,9},{2,3},{3,10},{10,11},{4,5},{5,12},{12,13},{6,7},... | collective-permute-start | bytes 3145736 | tf_op jit(solution)/shard_map/ppermute | solution.py:696
  109.2 57.0 %collective-permute-start.17 = (bf16[2,2,256,256]{3,2,1,0:T(8,128)(2,1)}, bf16[2,2,256,256]{3,2,1,0:T(8,128)(2,1)S(1)}, u32[]{:S(2)}, u32[]{:S(2)}) collective-permute-start(bf16[2,2,256,256]{3,2,1,0:T(8,128)(2,1)} %get-tuple-element.181), channel_id=1, source_target_pairs={{0,4},{1,5},{2,6},{3,7},{4,0},{5,1},{6,2},{7,3},{16,20},{17,21},{1... | collective-permute-start | bytes 1572872 | tf_op jit(solution)/shard_map/ppermute | solution.py:693
  109.3 59.4 %collective-permute-start.18 = (bf16[2,2,256,256]{3,2,1,0:T(8,128)(2,1)}, bf16[2,2,256,256]{3,2,1,0:T(8,128)(2,1)S(1)}, u32[]{:S(2)}, u32[]{:S(2)}) collective-permute-start(bf16[2,2,256,256]{3,2,1,0:T(8,128)(2,1)} %get-tuple-element.182), channel_id=1, source_target_pairs={{0,6},{1,7},{2,4},{3,5},{4,2},{5,3},{6,0},{7,1},{16,22},{17,23},{1... | collective-permute-start | bytes 1572872 | tf_op jit(solution)/shard_map/ppermute | solution.py:693
  113.2 56.7 %collective-permute-start.19 = (bf16[2,2,256,256]{3,2,1,0:T(8,128)(2,1)}, bf16[2,2,256,256]{3,2,1,0:T(8,128)(2,1)S(1)}, u32[]{:S(2)}, u32[]{:S(2)}) collective-permute-start(bf16[2,2,256,256]{3,2,1,0:T(8,128)(2,1)} %get-tuple-element.183), channel_id=1, source_target_pairs={{0,16},{1,17},{2,18},{3,19},{4,20},{5,21},{6,22},{7,23},{16,0},{17... | collective-permute-start | bytes 1572872 | tf_op jit(solution)/shard_map/ppermute | solution.py:693
  118.0 54.9 %collective-permute-start.20 = (bf16[2,2,256,256]{3,2,1,0:T(8,128)(2,1)S(1)}, bf16[2,2,256,256]{3,2,1,0:T(8,128)(2,1)S(1)}, u32[]{:S(2)}, u32[]{:S(2)}) collective-permute-start(bf16[2,2,256,256]{3,2,1,0:T(8,128)(2,1)S(1)} %copy-done.39), channel_id=1, source_target_pairs={{0,18},{1,19},{2,16},{3,17},{4,22},{5,23},{6,20},{7,21},{16,2},{17... | collective-permute-start | bytes 1572872 | tf_op jit(solution)/shard_map/ppermute | solution.py:693
  122.6 66.3 %collective-permute-start.21 = (bf16[2,2,256,256]{3,2,1,0:T(8,128)(2,1)}, bf16[2,2,256,256]{3,2,1,0:T(8,128)(2,1)S(1)}, u32[]{:S(2)}, u32[]{:S(2)}) collective-permute-start(bf16[2,2,256,256]{3,2,1,0:T(8,128)(2,1)} %get-tuple-element.185), channel_id=1, source_target_pairs={{0,20},{1,21},{2,22},{3,23},{4,16},{5,17},{6,18},{7,19},{16,4},{17... | collective-permute-start | bytes 1572872 | tf_op jit(solution)/shard_map/ppermute | solution.py:693
  166.2 30.3 %collective-permute-start.16 = (bf16[2,2,256,256]{3,2,1,0:T(8,128)(2,1)S(1)}, bf16[2,2,256,256]{3,2,1,0:T(8,128)(2,1)S(1)}, u32[]{:S(2)}, u32[]{:S(2)}) collective-permute-start(bf16[2,2,256,256]{3,2,1,0:T(8,128)(2,1)S(1)} %copy-done.38), channel_id=1, source_target_pairs={{0,2},{1,3},{2,0},{3,1},{4,6},{5,7},{6,4},{7,5},{16,18},{17,19},{1... | collective-permute-start | bytes 1572872 | tf_op jit(solution)/shard_map/ppermute | solution.py:693
  168.7 30.8 %collective-permute-start.22 = (bf16[2,2,256,256]{3,2,1,0:T(8,128)(2,1)S(1)}, bf16[2,2,256,256]{3,2,1,0:T(8,128)(2,1)S(1)}, u32[]{:S(2)}, u32[]{:S(2)}) collective-permute-start(bf16[2,2,256,256]{3,2,1,0:T(8,128)(2,1)S(1)} %copy-done.37), channel_id=1, source_target_pairs={{0,22},{1,23},{2,20},{3,21},{4,18},{5,19},{6,16},{7,17},{16,6},{17... | collective-permute-start | bytes 1572872 | tf_op jit(solution)/shard_map/ppermute | solution.py:693
  169.9 40.6 %collective-permute-start.9 = (bf16[8,256,256]{2,1,0:T(8,128)(2,1)}, bf16[8,256,256]{2,1,0:T(8,128)(2,1)S(1)}, u32[]{:S(2)}, u32[]{:S(2)}) collective-permute-start(bf16[8,256,256]{2,1,0:T(8,128)(2,1)} %get-tuple-element.162), channel_id=1, source_target_pairs={{0,1},{1,8},{8,9},{2,3},{3,10},{10,11},{4,5},{5,12},{12,13},{6,7},... | collective-permute-start | bytes 3145736 | tf_op jit(solution)/shard_map/ppermute | solution.py:696
  172.9 37.6 %collective-permute-start.10 = (bf16[8,256,256]{2,1,0:T(8,128)(2,1)}, bf16[8,256,256]{2,1,0:T(8,128)(2,1)S(1)}, u32[]{:S(2)}, u32[]{:S(2)}) collective-permute-start(bf16[8,256,256]{2,1,0:T(8,128)(2,1)} %get-tuple-element.163), channel_id=1, source_target_pairs={{1,0},{8,1},{9,8},{3,2},{10,3},{11,10},{5,4},{12,5},{13,12},{7,6},... | collective-permute-start | bytes 3145736 | tf_op jit(solution)/shard_map/ppermute | solution.py:696
  202.9 18.9 %collective-permute-start.23 = (bf16[8,256,256]{2,1,0:T(8,128)(2,1)}, bf16[8,256,256]{2,1,0:T(8,128)(2,1)S(1)}, u32[]{:S(2)}, u32[]{:S(2)}) collective-permute-start(bf16[8,256,256]{2,1,0:T(8,128)(2,1)} %get-tuple-element.187), channel_id=1, source_target_pairs={{0,1},{1,8},{8,9},{2,3},{3,10},{10,11},{4,5},{5,12},{12,13},{6,7},... | collective-permute-start | bytes 3145736 | tf_op jit(solution)/shard_map/ppermute | solution.py:696
  217.4 52.2 %collective-permute-start.11 = (bf16[2,256,384]{2,1,0:T(8,128)(2,1)}, bf16[2,256,384]{2,1,0:T(8,128)(2,1)S(1)}, u32[]{:S(2)}, u32[]{:S(2)}) collective-permute-start(bf16[2,256,384]{2,1,0:T(8,128)(2,1)} %get-tuple-element.172), channel_id=1, source_target_pairs={{0,4},{1,5},{2,6},{3,7},{4,0},{5,1},{6,2},{7,3},{16,20},{17,21},{1... | collective-permute-start | bytes 1179656 | tf_op jit(solution)/shard_map/ppermute | solution.py:693
  217.4 52.2 %collective-permute-start.12 = (bf16[2,256,384]{2,1,0:T(8,128)(2,1)}, bf16[2,256,384]{2,1,0:T(8,128)(2,1)S(1)}, u32[]{:S(2)}, u32[]{:S(2)}) collective-permute-start(bf16[2,256,384]{2,1,0:T(8,128)(2,1)} %get-tuple-element.173), channel_id=1, source_target_pairs={{0,6},{1,7},{2,4},{3,5},{4,2},{5,3},{6,0},{7,1},{16,22},{17,23},{1... | collective-permute-start | bytes 1179656 | tf_op jit(solution)/shard_map/ppermute | solution.py:693
  217.6 52.0 %collective-permute-start.13 = (bf16[2,256,384]{2,1,0:T(8,128)(2,1)}, bf16[2,256,384]{2,1,0:T(8,128)(2,1)S(1)}, u32[]{:S(2)}, u32[]{:S(2)}) collective-permute-start(bf16[2,256,384]{2,1,0:T(8,128)(2,1)} %get-tuple-element.174), channel_id=1, source_target_pairs={{0,20},{1,21},{2,22},{3,23},{4,16},{5,17},{6,18},{7,19},{16,4},{17... | collective-permute-start | bytes 1179656 | tf_op jit(solution)/shard_map/ppermute | solution.py:693
  221.7 47.8 %collective-permute-start.14 = (bf16[2,256,384]{2,1,0:T(8,128)(2,1)}, bf16[2,256,384]{2,1,0:T(8,128)(2,1)S(1)}, u32[]{:S(2)}, u32[]{:S(2)}) collective-permute-start(bf16[2,256,384]{2,1,0:T(8,128)(2,1)} %get-tuple-element.175), channel_id=1, source_target_pairs={{0,16},{1,17},{2,18},{3,19},{4,20},{5,21},{6,22},{7,23},{16,0},{17... | collective-permute-start | bytes 1179656 | tf_op jit(solution)/shard_map/ppermute | solution.py:693
  225.0 44.6 %collective-permute-start.15 = (bf16[2,256,384]{2,1,0:T(8,128)(2,1)}, bf16[2,256,384]{2,1,0:T(8,128)(2,1)S(1)}, u32[]{:S(2)}, u32[]{:S(2)}) collective-permute-start(bf16[2,256,384]{2,1,0:T(8,128)(2,1)} %get-tuple-element.176), channel_id=1, source_target_pairs={{0,18},{1,19},{2,16},{3,17},{4,22},{5,23},{6,20},{7,21},{16,2},{17... | collective-permute-start | bytes 1179656 | tf_op jit(solution)/shard_map/ppermute | solution.py:693
  274.3 25.2 %collective-permute-start.34 = (bf16[2,256,384]{2,1,0:T(8,128)(2,1)S(1)}, bf16[2,256,384]{2,1,0:T(8,128)(2,1)S(1)}, u32[]{:S(2)}, u32[]{:S(2)}) collective-permute-start(bf16[2,256,384]{2,1,0:T(8,128)(2,1)S(1)} %copy-done.42), channel_id=1, source_target_pairs={{0,2},{1,3},{2,0},{3,1},{4,6},{5,7},{6,4},{7,5},{16,18},{17,19},{1... | collective-permute-start | bytes 1179656 | tf_op jit(solution)/shard_map/ppermute | solution.py:693
  276.4 23.4 %collective-permute-start.35 = (bf16[2,256,384]{2,1,0:T(8,128)(2,1)S(1)}, bf16[2,256,384]{2,1,0:T(8,128)(2,1)S(1)}, u32[]{:S(2)}, u32[]{:S(2)}) collective-permute-start(bf16[2,256,384]{2,1,0:T(8,128)(2,1)S(1)} %copy-done.41), channel_id=1, source_target_pairs={{0,22},{1,23},{2,20},{3,21},{4,18},{5,19},{6,16},{7,17},{16,6},{17... | collective-permute-start | bytes 1179656 | tf_op jit(solution)/shard_map/ppermute | solution.py:693
  292.4 20.2 %collective-permute-start.29 = (bf16[2,256,384]{2,1,0:T(8,128)(2,1)}, bf16[2,256,384]{2,1,0:T(8,128)(2,1)S(1)}, u32[]{:S(2)}, u32[]{:S(2)}) collective-permute-start(bf16[2,256,384]{2,1,0:T(8,128)(2,1)} %get-tuple-element.225), channel_id=1, source_target_pairs={{0,2},{1,3},{2,0},{3,1},{4,6},{5,7},{6,4},{7,5},{16,18},{17,19},{1... | collective-permute-start | bytes 1179656 | tf_op jit(solution)/shard_map/ppermute | solution.py:693
  294.9 27.2 %collective-permute-start.30 = (bf16[2,256,384]{2,1,0:T(8,128)(2,1)}, bf16[2,256,384]{2,1,0:T(8,128)(2,1)S(1)}, u32[]{:S(2)}, u32[]{:S(2)}) collective-permute-start(bf16[2,256,384]{2,1,0:T(8,128)(2,1)} %get-tuple-element.226), channel_id=1, source_target_pairs={{0,4},{1,5},{2,6},{3,7},{4,0},{5,1},{6,2},{7,3},{16,20},{17,21},{1... | collective-permute-start | bytes 1179656 | tf_op jit(solution)/shard_map/ppermute | solution.py:693
  295.9 52.1 %collective-permute-start.31 = (bf16[2,256,384]{2,1,0:T(8,128)(2,1)}, bf16[2,256,384]{2,1,0:T(8,128)(2,1)S(1)}, u32[]{:S(2)}, u32[]{:S(2)}) collective-permute-start(bf16[2,256,384]{2,1,0:T(8,128)(2,1)} %get-tuple-element.227), channel_id=1, source_target_pairs={{0,6},{1,7},{2,4},{3,5},{4,2},{5,3},{6,0},{7,1},{16,22},{17,23},{1... | collective-permute-start | bytes 1179656 | tf_op jit(solution)/shard_map/ppermute | solution.py:693
  299.5 48.6 %collective-permute-start.32 = (bf16[2,256,384]{2,1,0:T(8,128)(2,1)}, bf16[2,256,384]{2,1,0:T(8,128)(2,1)S(1)}, u32[]{:S(2)}, u32[]{:S(2)}) collective-permute-start(bf16[2,256,384]{2,1,0:T(8,128)(2,1)} %get-tuple-element.228), channel_id=1, source_target_pairs={{0,16},{1,17},{2,18},{3,19},{4,20},{5,21},{6,22},{7,23},{16,0},{17... | collective-permute-start | bytes 1179656 | tf_op jit(solution)/shard_map/ppermute | solution.py:693
  299.8 48.3 %collective-permute-start.33 = (bf16[2,256,384]{2,1,0:T(8,128)(2,1)}, bf16[2,256,384]{2,1,0:T(8,128)(2,1)S(1)}, u32[]{:S(2)}, u32[]{:S(2)}) collective-permute-start(bf16[2,256,384]{2,1,0:T(8,128)(2,1)} %get-tuple-element.229), channel_id=1, source_target_pairs={{0,18},{1,19},{2,16},{3,17},{4,22},{5,23},{6,20},{7,21},{16,2},{17... | collective-permute-start | bytes 1179656 | tf_op jit(solution)/shard_map/ppermute | solution.py:693
  312.6 43.3 %collective-permute-start.27 = (bf16[2,256,384]{2,1,0:T(8,128)(2,1)}, bf16[2,256,384]{2,1,0:T(8,128)(2,1)S(1)}, u32[]{:S(2)}, u32[]{:S(2)}) collective-permute-start(bf16[2,256,384]{2,1,0:T(8,128)(2,1)} %get-tuple-element.218), channel_id=1, source_target_pairs={{0,20},{1,21},{2,22},{3,23},{4,16},{5,17},{6,18},{7,19},{16,4},{17... | collective-permute-start | bytes 1179656 | tf_op jit(solution)/shard_map/ppermute | solution.py:693
  322.2 41.4 %collective-permute-start.28 = (bf16[2,256,384]{2,1,0:T(8,128)(2,1)}, bf16[2,256,384]{2,1,0:T(8,128)(2,1)S(1)}, u32[]{:S(2)}, u32[]{:S(2)}) collective-permute-start(bf16[2,256,384]{2,1,0:T(8,128)(2,1)} %get-tuple-element.219), channel_id=1, source_target_pairs={{0,22},{1,23},{2,20},{3,21},{4,18},{5,19},{6,16},{7,17},{16,6},{17... | collective-permute-start | bytes 1179656 | tf_op jit(solution)/shard_map/ppermute | solution.py:693
  (47 other events, 1045.9 us)
